TPU v7x, 512 devices: a whole 4x8x8 slice. The times are simulated.
512 devices in a mesh: wide: 64 (over x, z, core), narrow: 8 (over y).
Axes of the slice: x: 4, y: 8, z: 8, core: 2. Of those that a mesh axis runs over, the one named last changes fastest.
Arguments:
- right_side: float32 [3, 1024, 128, 128], P(None, 'wide', 'narrow'), may hold values from -8 to 8
- occupancy: int32 [1024, 128, 128], P('wide', 'narrow'), may hold values from 0 to 1, as said below
- region: int32 [1024, 128, 128], P('wide', 'narrow'), may hold values from 0 to 3
- coarse_inverse: float32 [6144, 6144], P(('wide', 'narrow')), as said below
Outputs:
- solution_field: float32 [3, 1024, 128, 128], P(None, 'wide', 'narrow')
- residual: float32 [3, 1024, 128, 128], P(None, 'wide', 'narrow')
Inputs may be any that keep to these rules, and one draw needn't show every extreme that they name: `occupancy`: each subdomain has its own bone fraction between 0.15 and 0.9. `coarse_inverse`: symmetric positive definite.
All inputs are finite; a program needn't handle non-finite values.
Results may differ from a plain program's by a relative error of at most 0.00021.
Values sent between devices are 32-bit elements; how exact they have to be, the bound alone decides.
No kernel may reach another device: no remote copies, remote signals or barrier semaphores. Data moves between devices by JAX's collectives and lax.ppermute only.
A program may use at most 64 MiB of HBM per device.

v0:
```python
import jax
import jax.numpy as jnp
from jax import lax
from jax.sharding import Mesh
from jax.sharding import PartitionSpec as P

ITERS = 2
WIDE_NARROW = ("wide_0", "wide_1", "wide_2", "narrow")
WIDE = ("wide_0", "wide_1", "wide_2")


bone_stiff = 1.0
soft_stiff = 0.1


def from_everyone(array, axis):
    count = lax.axis_size(axis)
    return lax.all_to_all(
        jnp.broadcast_to(array[None], (count, *array.shape)), axis, 0, 0, tiled=True
    )


def over_copies(array, axis):
    return from_everyone(array, axis).sum(axis=0)


def one_axis_at_a_time(array, axes):
    far, near = axes
    nearer = over_copies(array, near)
    return over_copies(nearer, far)


def packed_total(arrays, axis):
    vector, at, gathered = (jnp.concatenate([a.reshape(-1) for a in arrays]), 0, [])
    subtotal = one_axis_at_a_time(vector, axis)
    for a in arrays:
        gathered.append(subtotal[at : at + a.size].reshape(a.shape))
        at += a.size
    return tuple(gathered)


def padded_2(array, sides, width):
    edges = {}
    for axis, dim in sides:
        count, length = (lax.axis_size(axis), array.shape[dim])
        up = [(i, (i + 1) % count) for i in range(count - 1)]
        last = lax.slice_in_dim(array, length - width, length, axis=dim)
        first = lax.slice_in_dim(array, 0, width, axis=dim)
        edges[dim] = (
            lax.ppermute(last, axis, up),
            lax.ppermute(first, axis, [(b, a) for a, b in up]),
        )
    done = []
    for _, dim in sides:
        low, high = edges[dim]
        around = [(width, width) if d in done else (0, 0) for d in range(array.ndim)]
        array = jnp.concatenate([jnp.pad(low, around), array, jnp.pad(high, around)], axis=dim)
        done.append(dim)
    return array


def laid_out(tiles, dim):
    tiles = jnp.moveaxis(tiles, 0, dim)
    lengths = tiles.shape
    return tiles.reshape(*lengths[:dim], lengths[dim] * lengths[dim + 1], *lengths[dim + 2 :])


def gather_axes(array, axes, dim):
    far, near = axes
    first = from_everyone(array, far)
    tiles = jnp.swapaxes(from_everyone(first, near), 0, 1)
    return laid_out(tiles.reshape(-1, *array.shape), dim)


def neighbours(padded):
    return [
        padded[..., 2:, 1:-1, 1:-1],
        padded[..., :-2, 1:-1, 1:-1],
        padded[..., 1:-1, 2:, 1:-1],
        padded[..., 1:-1, :-2, 1:-1],
        padded[..., 1:-1, 1:-1, 2:],
        padded[..., 1:-1, 1:-1, :-2],
    ]


def paired_sums(resid, precond, image):
    return packed_total(
        (jnp.sum(resid * precond), jnp.sum(image * precond)),
        (("wide_0", "wide_1"), ("wide_2", "narrow")),
    )


def local(right_side, occupancy, region, coarse_inverse):
    stiff = soft_stiff + (bone_stiff - soft_stiff) * occupancy.astype(jnp.float32)
    stiff_pad = padded_2(stiff, ((WIDE, 0), ("narrow", 1)), 1)
    stiff_pad = jnp.pad(stiff_pad, ((0, 0), (0, 0), (1, 1)))
    faces = [0.5 * (stiff + other) for other in neighbours(stiff_pad)]
    diagonal = sum(faces) + 0.5 * stiff
    regions = coarse_inverse.shape[0] // 3
    onehot = (region[None] == jnp.arange(regions)[:, None, None, None]).astype(jnp.float32)

    def operate(field):
        padded = padded_2(field, ((WIDE, 1), ("narrow", 2)), 1)
        padded = jnp.pad(padded, ((0, 0), (0, 0), (0, 0), (1, 1)))
        result = 0.25 * stiff * (field + jnp.sum(field, axis=0, keepdims=True))
        for face, other in zip(faces, neighbours(padded)):
            result = result + face * (field - other)
        return result

    def add_rows(piece):
        return jnp.dot(coarse_inverse, piece, precision=lax.Precision.HIGHEST)

    def precondition(resid):
        coarse = jnp.einsum(
            "gxyz,cxyz->gc", onehot, resid, precision=lax.Precision.HIGHEST
        ).reshape(-1)
        answer = add_rows(gather_axes(coarse, (("wide_0", "wide_1"), ("wide_2", "narrow")), 0))
        spread = jnp.einsum(
            "gxyz,gc->cxyz", onehot, answer.reshape(regions, 3), precision=lax.Precision.HIGHEST
        )
        return resid / diagonal + spread

    solution = jnp.zeros_like(right_side)
    resid = right_side
    precond = precondition(resid)
    image = operate(precond)
    rz_now, product = paired_sums(resid, precond, image)
    alpha = rz_now / product
    direction, along = (precond, image)
    for step in range(ITERS):
        solution = solution + alpha * direction
        resid = resid - alpha * along
        if step + 1 < ITERS:
            precond = precondition(resid)
            image = operate(precond)
            rz_next, product = paired_sums(resid, precond, image)
            ratio = rz_next / rz_now
            alpha = rz_next / (product - ratio * rz_next / alpha)
            direction = precond + ratio * direction
            along = image + ratio * along
            rz_now = rz_next
    return (solution, resid)


def solution(mesh):
    finer = Mesh(
        mesh.devices.reshape(4, 8, 2, mesh.shape["narrow"]),
        ("wide_0", "wide_1", "wide_2", "narrow"),
    )
    return jax.shard_map(
        local,
        mesh=finer,
        in_specs=(
            P(None, WIDE, "narrow", None),
            P(WIDE, "narrow", None),
            P(WIDE, "narrow", None),
            P(WIDE_NARROW, None),
        ),
        out_specs=(P(None, WIDE, "narrow", None), P(None, WIDE, "narrow", None)),
        check_vma=False,
    )
```

profile of v0, /device:TPU:1, one launch (start us, length us, event | category | flops | bytes accessed | tf_op | source)
XLA Modules:
  0.0 193.2 jit_solution(16760705136023220839)
XLA Ops:
  0.7 2.6 %convolution_bitcast_fusion.1 = f32[4,3]{1,0:T(4,128)S(1)} fusion(f32[3,16,16,128]{3,2,1,0:T(8,128)} %param.4, s32[16,16,128]{2,1,0:T(8,128)} %param.6), kind=kOutput, calls=%fused_computation.20 | convolution fusion | flops 4849664 | bytes 524336 | tf_op jit(solution)/shard_map/gxyz,cxyz->gc/dot_general | solution.py:114
  3.9 13.7 %all-to-all-start = ((f32[32,1,12]{2,1,0:T(1,128)}), f32[32,1,12]{2,1,0:T(1,128)S(1)}, u32[]{:S(2)}, u32[]{:S(2)}) async-start(f32[32,1,12]{2,1,0:T(1,128)} %broadcast_in_dim.25), calls=%async_computation | async-start | bytes 32768 | tf_op jit(solution)/shard_map/all_to_all | solution.py:18
  18.6 4.3 %collective-permute-start.1 = (f32[1,16,128]{2,1,0:T(8,128)S(1)}, f32[1,16,128]{2,1,0:T(8,128)S(1)}, u32[]{:S(2)}, u32[]{:S(2)}) collective-permute-start(f32[1,16,128]{2,1,0:T(8,128)S(1)} %get-tuple-element.36), channel_id=1, source_target_pairs={{0,8},{8,16},{16,24},{24,32},{32,40},{40,48},{48,56},{56,64},{64,7... | collective-permute-start | bytes 24584 | tf_op jit(solution)/shard_map/ppermute | solution.py:50
  22.9 1.9 collective-permute-start
  24.8 3.2 %collective-permute-start.3 = (f32[16,1,128]{2,1,0:T(1,128)S(1)}, f32[16,1,128]{2,1,0:T(1,128)S(1)}, u32[]{:S(2)}, u32[]{:S(2)}) collective-permute-start(f32[16,1,128]{2,1,0:T(1,128)S(1)} %get-tuple-element.34), channel_id=1, source_target_pairs={{0,1},{1,2},{2,3},{3,4},{4,5},{5,6},{6,7},{8,9},{9,10},{10,11},{11... | collective-permute-start | bytes 24584 | tf_op jit(solution)/shard_map/ppermute | solution.py:50
  30.3 9.2 %all-to-all-start.1 = ((f32[16,1,384]{2,1,0:T(1,128)}), f32[16,1,384]{2,1,0:T(1,128)S(1)}, u32[]{:S(2)}, u32[]{:S(2)}) async-start(f32[16,1,384]{2,1,0:T(1,128)} %reshape.105), calls=%async_computation.1 | async-start | bytes 49152 | tf_op jit(solution)/shard_map/all_to_all | solution.py:18
  40.1 6.5 %all-to-all-done.1 = f32[16,1,384]{2,1,0:T(1,128)S(1)} async-done(((f32[16,1,384]{2,1,0:T(1,128)}), f32[16,1,384]{2,1,0:T(1,128)S(1)}, u32[]{:S(2)}, u32[]{:S(2)}) %all-to-all-start.1) | async-done | bytes 24608 | tf_op jit(solution)/shard_map/all_to_all | solution.py:18
  48.3 5.3 %fusion.66 = f32[1,4,3]{2,0,1:T(1,128)S(1)} fusion(f32[6144,1,1]{0,1,2:T(1,128)S(1)} %reshape.96, f32[4,3,6144]{2,1,0:T(4,128)S(1)} %dot_general.21), kind=kOutput, calls=%fused_computation.132 | convolution fusion | flops 884736 | bytes 319536 | tf_op jit(solution)/shard_map/dot_general | solution.py:111
  54.6 2.6 %collective-permute-start.7 = (f32[3,16,1,128]{3,0,2,1:T(4,128)S(1)}, f32[3,16,1,128]{3,0,2,1:T(4,128)S(1)}, u32[]{:S(2)}, u32[]{:S(2)}) collective-permute-start(f32[3,16,1,128]{3,0,2,1:T(4,128)S(1)} %get-tuple-element.26), channel_id=1, source_target_pairs={{0,1},{1,2},{2,3},{3,4},{4,5},{5,6},{6,7},{8,9},{9,10},{10,11},{11... | collective-permute-start | bytes 73736 | tf_op jit(solution)/shard_map/ppermute | solution.py:50
  58.4 4.9 %collective-permute-start.5 = (f32[3,1,16,128]{3,0,2,1:T(4,128)S(1)}, f32[3,1,16,128]{3,0,2,1:T(4,128)S(1)}, u32[]{:S(2)}, u32[]{:S(2)}) collective-permute-start(f32[3,1,16,128]{3,0,2,1:T(4,128)S(1)} %get-tuple-element.24), channel_id=1, source_target_pairs={{0,8},{8,16},{16,24},{24,32},{32,40},{40,48},{48,56},{56,64},{64,7... | collective-permute-start | bytes 73736 | tf_op jit(solution)/shard_map/ppermute | solution.py:50
  63.3 1.9 collective-permute-start.4
  65.4 3.2 %collective-permute-done.4 = f32[3,1,16,128]{3,0,2,1:T(4,128)S(1)} collective-permute-done((f32[3,1,16,128]{3,0,2,1:T(4,128)S(1)}, f32[3,1,16,128]{3,0,2,1:T(4,128)S(1)}, u32[]{:S(2)}, u32[]{:S(2)}) %collective-permute-start.4) | collective-permute-done | bytes 24608 | tf_op jit(solution)/shard_map/ppermute | solution.py:51
  69.3 2.5 %fusion.8 = (f32[]{:T(128)}, f32[]{:T(128)}, f32[3,16,16,128]{3,0,2,1:T(4,128)S(1)}) fusion(f32[3,16,16,128]{3,0,2,1:T(4,128)S(1)} %convolution_add_fusion.1, f32[3,16,16,128]{3,2,1,0:T(8,128)S(1)} %copy-done.2, f32[3,18,18,130]{3,0,2,1:T(4,128)S(1)} %select_maximum_fusion.4, f32[16,16,128]{2,1,0:T(8,128)S(1)} %get-tuple-element.19, ...), kind=kOutput, calls=%fused_computation.27 | output fusion | flops 3178496 | bytes 3940360 | tf_op jit(solution)/shard_map/add | solution.py:105
  73.3 12.0 %all_to_all.46 = f32[16,1,2]{2,1,0:T(1,128)S(1)} all-to-all(f32[16,1,2]{2,1,0:T(1,128)S(1)} %broadcast_in_dim.28), channel_id=1, replica_groups=mesh['wide_0'=4,'wide_1'=8,'wide_2'=2,'narrow'=8] {'wide_2','narrow'}, dimensions={0} | all-to-all | bytes 256 | tf_op jit(solution)/shard_map/all_to_all | solution.py:18
  85.4 19.1 %all_to_all.47 = f32[32,1,2]{2,1,0:T(1,128)S(1)} all-to-all(f32[32,1,2]{2,1,0:T(1,128)S(1)} %broadcast_in_dim.29), channel_id=1, replica_groups=mesh['wide_0'=4,'wide_1'=8,'wide_2'=2,'narrow'=8] {'wide_0','wide_1'}, dimensions={0} | all-to-all | bytes 512 | tf_op jit(solution)/shard_map/all_to_all | solution.py:18
  108.3 11.6 %all_to_all.48 = f32[32,1,12]{2,1,0:T(1,128)S(1)} all-to-all(f32[32,1,12]{2,1,0:T(1,128)S(1)} %broadcast_in_dim.31), channel_id=1, replica_groups=mesh['wide_0'=4,'wide_1'=8,'wide_2'=2,'narrow'=8] {'wide_0','wide_1'}, dimensions={0} | all-to-all | bytes 3072 | tf_op jit(solution)/shard_map/all_to_all | solution.py:18
  120.1 12.7 %all_to_all.49 = f32[16,1,384]{2,1,0:T(1,128)S(1)} all-to-all(f32[16,1,384]{2,1,0:T(1,128)S(1)} %reshape.107), channel_id=1, replica_groups=mesh['wide_0'=4,'wide_1'=8,'wide_2'=2,'narrow'=8] {'wide_2','narrow'}, dimensions={0} | all-to-all | bytes 49152 | tf_op jit(solution)/shard_map/all_to_all | solution.py:18
  134.1 5.3 %fusion.67 = f32[1,4,3]{2,0,1:T(1,128)S(1)} fusion(f32[6144,1,1]{0,1,2:T(1,128)S(1)} %reshape.100, f32[4,3,6144]{2,1,0:T(4,128)S(1)} %dot_general.21), kind=kOutput, calls=%fused_computation.133 | convolution fusion | flops 884736 | bytes 319536 | tf_op jit(solution)/shard_map/dot_general | solution.py:111
  141.3 2.6 %collective-permute-start.11 = (f32[3,16,1,128]{3,0,2,1:T(4,128)S(1)}, f32[3,16,1,128]{3,0,2,1:T(4,128)S(1)}, u32[]{:S(2)}, u32[]{:S(2)}) collective-permute-start(f32[3,16,1,128]{3,0,2,1:T(4,128)S(1)} %get-tuple-element.22), channel_id=1, source_target_pairs={{0,1},{1,2},{2,3},{3,4},{4,5},{5,6},{6,7},{8,9},{9,10},{10,11},{11... | collective-permute-start | bytes 73736 | tf_op jit(solution)/shard_map/ppermute | solution.py:50
  145.2 2.9 %collective-permute-start.9 = (f32[3,1,16,128]{3,0,2,1:T(4,128)S(1)}, f32[3,1,16,128]{3,0,2,1:T(4,128)S(1)}, u32[]{:S(2)}, u32[]{:S(2)}) collective-permute-start(f32[3,1,16,128]{3,0,2,1:T(4,128)S(1)} %get-tuple-element.20), channel_id=1, source_target_pairs={{0,8},{8,16},{16,24},{24,32},{32,40},{40,48},{48,56},{56,64},{64,7... | collective-permute-start | bytes 73736 | tf_op jit(solution)/shard_map/ppermute | solution.py:50
  150.1 3.2 %collective-permute-done.8 = f32[3,1,16,128]{3,0,2,1:T(4,128)S(1)} collective-permute-done((f32[3,1,16,128]{3,0,2,1:T(4,128)S(1)}, f32[3,1,16,128]{3,0,2,1:T(4,128)S(1)}, u32[]{:S(2)}, u32[]{:S(2)}) %collective-permute-start.8) | collective-permute-done | bytes 24608 | tf_op jit(solution)/shard_map/ppermute | solution.py:51
  154.1 2.5 %multiply_reduce_fusion.1 = (f32[]{:T(128)}, f32[]{:T(128)}, f32[3,16,16,128]{3,0,2,1:T(4,128)S(1)}) fusion(f32[3,16,16,128]{3,0,2,1:T(4,128)S(1)} %convolution_add_fusion, f32[3,16,16,128]{3,0,2,1:T(4,128)S(1)} %get-tuple-element.17, f32[]{:T(128)S(6)} %div.28, f32[3,16,16,128]{3,2,1,0:T(8,128)S(1)} %copy-done.2, ...), kind=kOutput, calls=%fused_computation.83 | output fusion | flops 3375104 | bytes 4464652 | tf_op jit(solution)/shard_map/add | solution.py:105
  157.9 12.1 %all_to_all.50 = f32[16,1,2]{2,1,0:T(1,128)S(1)} all-to-all(f32[16,1,2]{2,1,0:T(1,128)S(1)} %broadcast_in_dim.34), channel_id=1, replica_groups=mesh['wide_0'=4,'wide_1'=8,'wide_2'=2,'narrow'=8] {'wide_2','narrow'}, dimensions={0} | all-to-all | bytes 256 | tf_op jit(solution)/shard_map/all_to_all | solution.py:18
  170.0 16.0 %all_to_all.51 = f32[32,1,2]{2,1,0:T(1,128)S(1)} all-to-all(f32[32,1,2]{2,1,0:T(1,128)S(1)} %broadcast_in_dim.35), channel_id=1, replica_groups=mesh['wide_0'=4,'wide_1'=8,'wide_2'=2,'narrow'=8] {'wide_0','wide_1'}, dimensions={0} | all-to-all | bytes 512 | tf_op jit(solution)/shard_map/all_to_all | solution.py:18
  (81 shorter events, 24.5 us)
Async XLA Ops:
  0.6 39.2 %copy-start = (s32[16,16,128]{2,1,0:T(8,128)S(1)}, s32[16,16,128]{2,1,0:T(8,128)}, u32[]{:S(2)}) copy-start(s32[16,16,128]{2,1,0:T(8,128)} %param.5) | copy-start | bytes 393220
  0.6 28.7 %copy-start.1 = (f32[12,6144]{1,0:T(8,128)S(1)}, f32[12,6144]{1,0:T(8,128)}, u32[]{:S(2)}) copy-start(f32[12,6144]{1,0:T(8,128)} %param.7) | copy-start | bytes 884740
  3.9 25.5 %all-to-all-start = ((f32[32,1,12]{2,1,0:T(1,128)}), f32[32,1,12]{2,1,0:T(1,128)S(1)}, u32[]{:S(2)}, u32[]{:S(2)}) async-start(f32[32,1,12]{2,1,0:T(1,128)} %broadcast_in_dim.25), calls=%async_computation | async-start | bytes 32768 | tf_op jit(solution)/shard_map/all_to_all | solution.py:18
  18.6 21.0 %collective-permute-start.1 = (f32[1,16,128]{2,1,0:T(8,128)S(1)}, f32[1,16,128]{2,1,0:T(8,128)S(1)}, u32[]{:S(2)}, u32[]{:S(2)}) collective-permute-start(f32[1,16,128]{2,1,0:T(8,128)S(1)} %get-tuple-element.36), channel_id=1, source_target_pairs={{0,8},{8,16},{16,24},{24,32},{32,40},{40,48},{48,56},{56,64},{64,7... | collective-permute-start | bytes 24584 | tf_op jit(solution)/shard_map/ppermute | solution.py:50
  22.9 16.7 %collective-permute-start = (f32[1,16,128]{2,1,0:T(8,128)S(1)}, f32[1,16,128]{2,1,0:T(8,128)S(1)}, u32[]{:S(2)}, u32[]{:S(2)}) collective-permute-start(f32[1,16,128]{2,1,0:T(8,128)S(1)} %get-tuple-element.37), channel_id=1, source_target_pairs={{8,0},{16,8},{24,16},{32,24},{40,32},{48,40},{56,48},{64,56},{72,6... | collective-permute-start | bytes 24584 | tf_op jit(solution)/shard_map/ppermute | solution.py:51
  24.8 14.7 %collective-permute-start.3 = (f32[16,1,128]{2,1,0:T(1,128)S(1)}, f32[16,1,128]{2,1,0:T(1,128)S(1)}, u32[]{:S(2)}, u32[]{:S(2)}) collective-permute-start(f32[16,1,128]{2,1,0:T(1,128)S(1)} %get-tuple-element.34), channel_id=1, source_target_pairs={{0,1},{1,2},{2,3},{3,4},{4,5},{5,6},{6,7},{8,9},{9,10},{10,11},{11... | collective-permute-start | bytes 24584 | tf_op jit(solution)/shard_map/ppermute | solution.py:50
  28.0 11.5 %collective-permute-start.2 = (f32[16,1,128]{2,1,0:T(1,128)S(1)}, f32[16,1,128]{2,1,0:T(1,128)S(1)}, u32[]{:S(2)}, u32[]{:S(2)}) collective-permute-start(f32[16,1,128]{2,1,0:T(1,128)S(1)} %get-tuple-element.35), channel_id=1, source_target_pairs={{1,0},{2,1},{3,2},{4,3},{5,4},{6,5},{7,6},{9,8},{10,9},{11,10},{12... | collective-permute-start | bytes 24584 | tf_op jit(solution)/shard_map/ppermute | solution.py:51
  30.3 16.3 %all-to-all-start.1 = ((f32[16,1,384]{2,1,0:T(1,128)}), f32[16,1,384]{2,1,0:T(1,128)S(1)}, u32[]{:S(2)}, u32[]{:S(2)}) async-start(f32[16,1,384]{2,1,0:T(1,128)} %reshape.105), calls=%async_computation.1 | async-start | bytes 49152 | tf_op jit(solution)/shard_map/all_to_all | solution.py:18
  39.9 13.7 %copy-start.2 = (f32[3,16,16,128]{3,2,1,0:T(8,128)S(1)}, f32[3,16,16,128]{3,2,1,0:T(8,128)}, u32[]{:S(2)}) copy-start(f32[3,16,16,128]{3,2,1,0:T(8,128)} %param.4) | copy-start | bytes 1179652
  39.9 13.7 %copy-start.3 = (s32[16,16,128]{2,1,0:T(8,128)S(1)}, s32[16,16,128]{2,1,0:T(8,128)}, u32[]{:S(2)}) copy-start(s32[16,16,128]{2,1,0:T(8,128)} %param.6) | copy-start | bytes 393220
  54.6 10.7 %collective-permute-start.7 = (f32[3,16,1,128]{3,0,2,1:T(4,128)S(1)}, f32[3,16,1,128]{3,0,2,1:T(4,128)S(1)}, u32[]{:S(2)}, u32[]{:S(2)}) collective-permute-start(f32[3,16,1,128]{3,0,2,1:T(4,128)S(1)} %get-tuple-element.26), channel_id=1, source_target_pairs={{0,1},{1,2},{2,3},{3,4},{4,5},{5,6},{6,7},{8,9},{9,10},{10,11},{11... | collective-permute-start | bytes 73736 | tf_op jit(solution)/shard_map/ppermute | solution.py:50
  57.1 8.2 %collective-permute-start.6 = (f32[3,16,1,128]{3,0,2,1:T(4,128)S(1)}, f32[3,16,1,128]{3,0,2,1:T(4,128)S(1)}, u32[]{:S(2)}, u32[]{:S(2)}) collective-permute-start(f32[3,16,1,128]{3,0,2,1:T(4,128)S(1)} %get-tuple-element.27), channel_id=1, source_target_pairs={{1,0},{2,1},{3,2},{4,3},{5,4},{6,5},{7,6},{9,8},{10,9},{11,10},{12... | collective-permute-start | bytes 73736 | tf_op jit(solution)/shard_map/ppermute | solution.py:51
  58.4 6.9 %collective-permute-start.5 = (f32[3,1,16,128]{3,0,2,1:T(4,128)S(1)}, f32[3,1,16,128]{3,0,2,1:T(4,128)S(1)}, u32[]{:S(2)}, u32[]{:S(2)}) collective-permute-start(f32[3,1,16,128]{3,0,2,1:T(4,128)S(1)} %get-tuple-element.24), channel_id=1, source_target_pairs={{0,8},{8,16},{16,24},{24,32},{32,40},{40,48},{48,56},{56,64},{64,7... | collective-permute-start | bytes 73736 | tf_op jit(solution)/shard_map/ppermute | solution.py:50
  63.3 5.2 %collective-permute-start.4 = (f32[3,1,16,128]{3,0,2,1:T(4,128)S(1)}, f32[3,1,16,128]{3,0,2,1:T(4,128)S(1)}, u32[]{:S(2)}, u32[]{:S(2)}) collective-permute-start(f32[3,1,16,128]{3,0,2,1:T(4,128)S(1)} %get-tuple-element.25), channel_id=1, source_target_pairs={{8,0},{16,8},{24,16},{32,24},{40,32},{48,40},{56,48},{64,56},{72,6... | collective-permute-start | bytes 73736 | tf_op jit(solution)/shard_map/ppermute | solution.py:51
  141.3 8.7 %collective-permute-start.11 = (f32[3,16,1,128]{3,0,2,1:T(4,128)S(1)}, f32[3,16,1,128]{3,0,2,1:T(4,128)S(1)}, u32[]{:S(2)}, u32[]{:S(2)}) collective-permute-start(f32[3,16,1,128]{3,0,2,1:T(4,128)S(1)} %get-tuple-element.22), channel_id=1, source_target_pairs={{0,1},{1,2},{2,3},{3,4},{4,5},{5,6},{6,7},{8,9},{9,10},{10,11},{11... | collective-permute-start | bytes 73736 | tf_op jit(solution)/shard_map/ppermute | solution.py:50
  143.9 6.2 %collective-permute-start.10 = (f32[3,16,1,128]{3,0,2,1:T(4,128)S(1)}, f32[3,16,1,128]{3,0,2,1:T(4,128)S(1)}, u32[]{:S(2)}, u32[]{:S(2)}) collective-permute-start(f32[3,16,1,128]{3,0,2,1:T(4,128)S(1)} %get-tuple-element.23), channel_id=1, source_target_pairs={{1,0},{2,1},{3,2},{4,3},{5,4},{6,5},{7,6},{9,8},{10,9},{11,10},{12... | collective-permute-start | bytes 73736 | tf_op jit(solution)/shard_map/ppermute | solution.py:51
  145.2 4.9 %collective-permute-start.9 = (f32[3,1,16,128]{3,0,2,1:T(4,128)S(1)}, f32[3,1,16,128]{3,0,2,1:T(4,128)S(1)}, u32[]{:S(2)}, u32[]{:S(2)}) collective-permute-start(f32[3,1,16,128]{3,0,2,1:T(4,128)S(1)} %get-tuple-element.20), channel_id=1, source_target_pairs={{0,8},{8,16},{16,24},{24,32},{32,40},{40,48},{48,56},{56,64},{64,7... | collective-permute-start | bytes 73736 | tf_op jit(solution)/shard_map/ppermute | solution.py:50
  148.1 5.2 %collective-permute-start.8 = (f32[3,1,16,128]{3,0,2,1:T(4,128)S(1)}, f32[3,1,16,128]{3,0,2,1:T(4,128)S(1)}, u32[]{:S(2)}, u32[]{:S(2)}) collective-permute-start(f32[3,1,16,128]{3,0,2,1:T(4,128)S(1)} %get-tuple-element.21), channel_id=1, source_target_pairs={{8,0},{16,8},{24,16},{32,24},{40,32},{48,40},{56,48},{64,56},{72,6... | collective-permute-start | bytes 73736 | tf_op jit(solution)/shard_map/ppermute | solution.py:51
where the time goes:
time: 194 us; the launch traced here: 193 us
  blocking collectives  83.6 us (43%)
  starting transfers between devices  53 us (27%)
  matrix products  17.6 us (9%)
  other arithmetic  12.9 us (7%)
  waiting for transfers between devices  12.9 us (7%)
  between operations  6.96 us (4%)
  local copies, waits for them, and re-layouts  6.4 us (3%)
    all_to_all x6, blocking collectives, from_everyone(): lax.all_to_all(jnp.broadcast_to(array[None], (count, *array.shape)), axis...  83.6 us
    all_to_all x2, starting transfers between devices, from_everyone(): lax.all_to_all(jnp.broadcast_to(array[None], (count, *array.shape)), axis...  22.9 us
    ppermute x6, starting transfers between devices, padded_2(): lax.ppermute(last, axis, up)  20.4 us
    dot_general x2, matrix products, add_rows(): return jnp.dot(coarse_inverse, piece, precision=lax.Precision.HIGHEST)  10.5 us
    ppermute x6, starting transfers between devices, padded_2(): lax.ppermute(first, axis, [(b, a) for a, b in up])  9.64 us
    all_to_all x2, waiting for transfers between devices, from_everyone(): lax.all_to_all(jnp.broadcast_to(array[None], (count, *array.shape)), axis...  6.47 us
    ppermute x6, waiting for transfers between devices, padded_2(): lax.ppermute(first, axis, [(b, a) for a, b in up])  6.42 us
    add x2, other arithmetic, operate(): result = 0.25 * stiff * (field + jnp.sum(field, axis=0, keepdims=True))  5.09 us
  transfers between devices with their start and end apart: 14, of which 3 were waited for; matrix products, arithmetic and copies ran while one was open for 1% of the time, Pallas kernels for 0%

commit v1 on v0

v1 whole, which is shorter than its diff:
```python
import jax
import jax.numpy as jnp
from jax import lax
from jax.experimental import pallas as pl
from jax.experimental.pallas import tpu as pltpu
from jax.sharding import Mesh
from jax.sharding import PartitionSpec as P

WIDE = ("x", "z", "c")
ROWS = ("x", "z")
COLS = ("c", "y")
NROWS = 32
NCOLS = 16
F32 = jnp.float32
NREG = 4
SLAB = 96
VMEM = pl.BlockSpec(memory_space=pltpu.VMEM)


def shape(*dims):
    return jax.ShapeDtypeStruct(dims, F32)


def call(kernel, outs, ins, scratch=()):
    return pl.pallas_call(
        kernel,
        out_shape=outs,
        in_specs=[VMEM] * len(ins),
        out_specs=jax.tree.map(lambda _: VMEM, outs),
        scratch_shapes=list(scratch),
        compiler_params=pltpu.CompilerParams(vmem_limit_bytes=24 * 1024 * 1024),
    )(*ins)


def stiffness(occ):
    return 0.1 + 0.9 * occ.astype(F32)


def total(v):
    return jnp.sum(jnp.sum(v, axis=0, keepdims=True), axis=1, keepdims=True)


def add_regions(accs, label, field):
    out = list(accs)
    for g in range(NREG):
        mask = label == g + 1
        for c in range(3):
            out[3 * g + c] = out[3 * g + c] + jnp.where(mask, field[c], 0.0)
    return out


def fold(accs, coarse_ref, acc_ref, u_ref, pad_ref, out_ref, sums=()):
    for i in range(3 * NREG):
        acc_ref[i] = accs[i]
    rc = jnp.sum(jnp.sum(acc_ref[...], axis=1), axis=1, keepdims=True)
    u_ref[...] = jnp.sum(coarse_ref[...] * rc, axis=0, keepdims=True)
    pad_ref[...] = jnp.zeros_like(pad_ref)
    for w in range(2 * NROWS):
        pad_ref[w + 1 : w + 2, 0:SLAB] = u_ref[0:1, SLAB * w : SLAB * (w + 1)]
    if sums:
        lane = lax.broadcasted_iota(jnp.int32, (1, 128), 1)
        row = jnp.zeros((1, 128), F32)
        for i, s in enumerate(sums):
            row = jnp.where(lane == SLAB + i, s, row)
        tail = jnp.broadcast_to(row, (4, 128))
    for n in range(NROWS):
        window = pad_ref[2 * n : 2 * n + 4, :]
        if sums:
            window = window + tail
        out_ref[n] = window


FOLD_SCRATCH = (
    pltpu.VMEM((12, 16, 128), F32),
    pltpu.VMEM((1, 6144), F32),
    pltpu.VMEM((72, 128), F32),
)


def first_kernel(r_ref, occ_ref, reg_ref, coarse_ref, out_ref, lo_ref, hi_ref, acc_ref, u_ref, pad_ref):
    def step(x, accs):
        label = reg_ref[x] + 1
        return tuple(add_regions(accs, label, [r_ref[c, x] for c in range(3)]))

    zero = jnp.zeros((16, 128), F32)
    accs = lax.fori_loop(0, 16, step, (zero,) * 12)
    fold(accs, coarse_ref, acc_ref, u_ref, pad_ref, out_ref)
    for ref, at in ((lo_ref, 0), (hi_ref, 12)):
        ref[0] = stiffness(occ_ref[:, at : at + 4, :])
        ref[1] = reg_ref[:, at : at + 4, :].astype(F32) + 1.0
        for c in range(3):
            ref[2 + c] = r_ref[c, :, at : at + 4, :]


def hand_out(part, out_ref):
    for c in range(2):
        rows = part[c : c + 3]
        for y in range(8):
            out_ref[8 * c + y, 0:3, :] = pltpu.roll(rows, (12 - 12 * y) % 128, axis=1)
            out_ref[8 * c + y, 3:4, :] = part[0:1]


def around_kernel(recv_ref, r_ref, occ_ref, reg_ref, lo_ref, hi_ref, out_ref, up_ref, down_ref):
    hand_out(jnp.sum(recv_ref[...], axis=0), out_ref)
    for ref, at in ((up_ref, 13), (down_ref, 0)):
        rows = slice(at, at + 3)
        ref[0, :, 0:16, :] = stiffness(occ_ref[rows])
        ref[1, :, 0:16, :] = reg_ref[rows].astype(F32) + 1.0
        for c in range(3):
            ref[2 + c, :, 0:16, :] = r_ref[c, rows]
        for i in range(5):
            ref[i, :, 16:20, :] = hi_ref[i, rows]
            ref[i, :, 20:24, :] = lo_ref[i, rows]


def pass_kernel(recv_ref, out_ref):
    hand_out(jnp.sum(recv_ref[...], axis=0), out_ref)


def iotas():
    lane = lax.broadcasted_iota(jnp.int32, (24, 128), 1)
    return lane == 0, lane == 127


def coefficients(before, here, after):
    first, last = iotas()
    y_up = pltpu.roll(here, 23, axis=0)
    y_down = pltpu.roll(here, 1, axis=0)
    z_up = jnp.where(last, 0.0, pltpu.roll(here, 127, axis=1))
    z_down = jnp.where(first, 0.0, pltpu.roll(here, 1, axis=1))
    half = 0.5 * here
    faces = [half + 0.5 * other for other in (after, before, y_up, y_down, z_up, z_down)]
    diagonal = faces[0] + faces[1] + faces[2] + faces[3] + faces[4] + faces[5] + half
    faces[4] = jnp.where(last, 0.0, faces[4])
    faces[5] = jnp.where(first, 0.0, faces[5])
    return faces, diagonal


def operate(faces, diagonal, here, befores, fields, afters):
    quarter = 0.25 * here
    main = diagonal - quarter
    shared = quarter * (fields[0] + fields[1] + fields[2])
    out = []
    for c in range(3):
        u = fields[c]
        out.append(
            main * u
            + shared
            - faces[0] * afters[c]
            - faces[1] * befores[c]
            - faces[2] * pltpu.roll(u, 23, axis=0)
            - faces[3] * pltpu.roll(u, 1, axis=0)
            - faces[4] * pltpu.roll(u, 127, axis=1)
            - faces[5] * pltpu.roll(u, 1, axis=1)
        )
    return out


def spread_maps(q, map_ref):
    row = lax.broadcasted_iota(jnp.int32, (24, 128), 0)
    for s in range(3):
        for i in range(12):
            below, own, above = (q[s : s + 1, 12 * d + i : 12 * d + i + 1] for d in range(3))
            map_ref[s, i] = jnp.where(row < 16, own, jnp.where(row < 20, above, below))


def spread(label, map_ref, s, c):
    out = jnp.zeros((24, 128), F32)
    for g in range(NREG):
        out = jnp.where(label == g + 1, map_ref[s, 3 * g + c], out)
    return out


def second_kernel(
    recv_ref, r_ref, occ_ref, reg_ref, lo_ref, hi_ref, below_ref, above_ref, coarse_ref,
    out_ref, k_ref, label_ref, inv_ref, z_ref, w_ref,
    ext_ref, map_ref, acc_ref, u_ref, pad_ref,
):
    q = jnp.sum(recv_ref[...], axis=0)
    spread_maps(q, map_ref)
    k_ref[0:3] = below_ref[0]
    k_ref[19:22] = above_ref[0]
    label_ref[0:3] = below_ref[1]
    label_ref[19:22] = above_ref[1]
    k_ref[3:19, 0:16] = stiffness(occ_ref[...])
    label_ref[3:19, 0:16] = reg_ref[...].astype(F32) + 1.0
    for ref, i in ((k_ref, 0), (label_ref, 1)):
        ref[3:19, 16:20] = hi_ref[i]
        ref[3:19, 20:24] = lo_ref[i]
    for c in range(3):
        ext_ref[c, 0:3] = below_ref[2 + c]
        ext_ref[c, 19:22] = above_ref[2 + c]
        ext_ref[c, 3:19, 0:16] = r_ref[c]
        ext_ref[c, 3:19, 16:20] = hi_ref[2 + c]
        ext_ref[c, 3:19, 20:24] = lo_ref[2 + c]

    def first_step(s):
        def body(x, carry):
            here = k_ref[x]
            _, diagonal = coefficients(k_ref[x - 1], here, k_ref[x + 1])
            inv = jnp.where(here > 0.0, 1.0 / jnp.where(here > 0.0, diagonal, 1.0), 0.0)
            inv_ref[x] = inv
            label = label_ref[x]
            for c in range(3):
                z_ref[c, x] = ext_ref[c, x] * inv + spread(label, map_ref, s, c)
            return carry

        return body

    lax.fori_loop(1, 3, first_step(0), 0)
    lax.fori_loop(3, 19, first_step(1), 0)
    lax.fori_loop(19, 21, first_step(2), 0)

    def image(x):
        here = k_ref[x]
        faces, diagonal = coefficients(k_ref[x - 1], here, k_ref[x + 1])
        fields = [z_ref[c, x] for c in range(3)]
        w = operate(
            faces, diagonal, here, [z_ref[c, x - 1] for c in range(3)], fields, [z_ref[c, x + 1] for c in range(3)]
        )
        for c in range(3):
            w_ref[c, x] = w[c]
        return fields, w

    image(2)
    image(19)

    def second_step(x, carry):
        fields, w = image(x)
        own = [v[0:16] for v in w]
        rz, zw = carry[12], carry[13]
        for c in range(3):
            z = fields[c][0:16]
            rz = rz + ext_ref[c, x, 0:16] * z
            zw = zw + z * own[c]
        return (*add_regions(carry[:12], label_ref[x, 0:16], own), rz, zw)

    zero = jnp.zeros((16, 128), F32)
    carry = lax.fori_loop(3, 19, second_step, (zero,) * 14)
    fold(carry[:12], coarse_ref, acc_ref, u_ref, pad_ref, out_ref, (total(carry[12]), total(carry[13])))


def third_kernel(
    recv_ref, r_ref, k_ref, label_ref, inv_ref, z_ref, w_ref, out_ref, scal_ref, znew_ref, image_ref, map_ref
):
    q = jnp.sum(recv_ref[...], axis=0)
    spread_maps(q, map_ref)
    rz, zw = q[3:4, SLAB : SLAB + 1], q[3:4, SLAB + 1 : SLAB + 2]
    alpha = rz / zw

    def first_step(s):
        def body(x, carry):
            inv, label = inv_ref[x], label_ref[x]
            for c in range(3):
                y = w_ref[c, x] * inv + spread(label, map_ref, s, c)
                znew_ref[c, x - 2] = z_ref[c, x] - alpha * y
            return carry

        return body

    first_step(0)(2, 0)
    lax.fori_loop(3, 19, first_step(1), 0)
    first_step(2)(19, 0)

    def second_step(x, carry):
        here = k_ref[x + 2]
        faces, diagonal = coefficients(k_ref[x + 1], here, k_ref[x + 3])
        fields = [znew_ref[c, x] for c in range(3)]
        image = operate(
            faces, diagonal, here, [znew_ref[c, x - 1] for c in range(3)], fields, [znew_ref[c, x + 1] for c in range(3)]
        )
        new, zaz, cross = carry
        for c in range(3):
            z, az, w = fields[c][0:16], image[c][0:16], w_ref[c, x + 2, 0:16]
            image_ref[c, x - 1] = az
            new = new + (r_ref[c, x - 1] - alpha * w) * z
            zaz = zaz + z * az
            cross = cross + z * w
        return new, zaz, cross

    zero = jnp.zeros((16, 128), F32)
    sums = lax.fori_loop(1, 17, second_step, (zero,) * 3)
    lane = lax.broadcasted_iota(jnp.int32, (1, 128), 1)
    row = jnp.zeros((1, 128), F32)
    for i, s in enumerate(sums):
        row = jnp.where(lane == i, total(s), row)
    scal_ref[...] = q[3:4]
    for n in range(NCOLS):
        out_ref[n] = row


def sum_kernel(recv_ref, out_ref):
    row = jnp.sum(recv_ref[...], axis=0)
    for n in range(NROWS):
        out_ref[n] = row


def last_kernel(recv_ref, scal_ref, r_ref, z_ref, w_ref, znew_ref, image_ref, x_ref, res_ref):
    sums = jnp.sum(recv_ref[...], axis=0)
    new, zaz, cross = (sums[:, i : i + 1] for i in range(3))
    scal = scal_ref[...]
    rz, zw = scal[:, SLAB : SLAB + 1], scal[:, SLAB + 1 : SLAB + 2]
    alpha = rz / zw
    ratio = new / rz
    product = zaz + ratio * (2.0 * cross + ratio * zw)
    second = new / product

    def step(x, carry):
        for c in range(3):
            z, w = z_ref[c, x + 3, 0:16], w_ref[c, x + 3, 0:16]
            x_ref[c, x] = alpha * z + second * (znew_ref[c, x + 1, 0:16] + ratio * z)
            res_ref[c, x] = (r_ref[c, x] - alpha * w) - second * (image_ref[c, x] + ratio * w)
        return carry

    lax.fori_loop(0, 16, step, 0)


def exchange(array, axes):
    return lax.all_to_all(array, axes, 0, 0, tiled=True)


def shifted(array, axis, step):
    count = lax.axis_size(axis)
    pairs = [(i, i + step) for i in range(count) if 0 <= i + step < count]
    return lax.ppermute(array, axis, pairs)


def local(right, occ, reg, coarse):
    send, lo, hi = call(
        first_kernel,
        (shape(NROWS, 4, 128), shape(5, 16, 4, 128), shape(5, 16, 4, 128)),
        (right, occ, reg, coarse),
        FOLD_SCRATCH,
    )
    before = shifted(hi, "y", 1)
    after = shifted(lo, "y", -1)
    got = exchange(send, ROWS)
    send, up, down = call(
        around_kernel,
        (shape(NCOLS, 4, 128), shape(5, 3, 24, 128), shape(5, 3, 24, 128)),
        (got, right, occ, reg, before, after),
    )
    below = shifted(up, WIDE, 1)
    above = shifted(down, WIDE, -1)
    got = exchange(send, COLS)
    plane = (24, 128)
    send, k, label, inv, z, w = call(
        second_kernel,
        (
            shape(NROWS, 4, 128),
            shape(22, *plane),
            shape(22, *plane),
            shape(22, *plane),
            shape(3, 22, *plane),
            shape(3, 22, *plane),
        ),
        (got, right, occ, reg, before, after, below, above, coarse),
        (pltpu.VMEM((3, 22, *plane), F32), pltpu.VMEM((3, 12, *plane), F32), *FOLD_SCRATCH),
    )
    got = exchange(send, ROWS)
    send = call(pass_kernel, shape(NCOLS, 4, 128), (got,))
    got = exchange(send, COLS)
    send, scal, znew, image = call(
        third_kernel,
        (shape(NCOLS, 1, 128), shape(1, 128), shape(3, 18, *plane), shape(3, 16, 16, 128)),
        (got, right, k, label, inv, z, w),
        (pltpu.VMEM((3, 12, *plane), F32),),
    )
    got = exchange(send, COLS)
    send = call(sum_kernel, shape(NROWS, 1, 128), (got,))
    got = exchange(send, ROWS)
    return call(
        last_kernel,
        (shape(3, 16, 16, 128), shape(3, 16, 16, 128)),
        (got, scal, right, z, w, znew, image),
    )


def solution(mesh):
    finer = Mesh(mesh.devices.reshape(4, 8, 2, 8), ("x", "z", "c", "y"))
    field = P(None, WIDE, "y", None)
    labels = P(WIDE, "y", None)
    return jax.shard_map(
        local,
        mesh=finer,
        in_specs=(field, labels, labels, P((*WIDE, "y"), None)),
        out_specs=(field, field),
        check_vma=False,
    )
```

time: 194 us -> 113 us (0.58)
  starting transfers between devices: 53 us -> 12 us
  matrix products: 17.6 us -> 0 us
  other arithmetic: 12.9 us -> 0 us
  waiting for transfers between devices: 12.9 us -> 0.01 us
  Pallas kernels: 0 us -> 9.64 us
  between operations: 6.96 us -> 0.71 us
  local copies, waits for them, and re-layouts: 6.4 us -> 3.8 us
  blocking collectives: 83.6 us -> 85.8 us
    all_to_all x2 -> x0, starting transfers between devices: 22.9 us -> none  [from_everyone(): lax.all_to_all(jnp.broadcast_to(array[None], (count, *array.shape)), axis...]
    ppermute x12 -> x4, starting transfers between devices: 30 us -> 12 us  [shifted(): return lax.ppermute(array, axis, pairs)]
    dot_general x6 -> x0, matrix products: 17.6 us -> none  [the longest x2 10.5 us: add_rows(): return jnp.dot(coarse_inverse, piece, precision=lax.Precision.HIGHEST)]
    pallas_call x0 -> x7, Pallas kernels: none -> 9.64 us  [call(): pl.pallas_call(kernel, out_shape=outs, in_specs=[VMEM] * len(ins), out_sp...]
    all_to_all x2 -> x0, waiting for transfers between devices: 6.47 us -> none  [from_everyone(): lax.all_to_all(jnp.broadcast_to(array[None], (count, *array.shape)), axis...]
    ppermute x12 -> x4, waiting for transfers between devices: 6.43 us -> 0.01 us  [shifted(): return lax.ppermute(array, axis, pairs)]
    add x3 -> x0, other arithmetic: 6.02 us -> none  [the longest x2 5.09 us: operate(): result = 0.25 * stiff * (field + jnp.sum(field, axis=0, keepdims=True))]
    concatenate x5 -> x0, other arithmetic: 4.49 us -> none  [the longest x2 2.69 us: packed_total(): jnp.concatenate([a.reshape(-1) for a in arrays])]
  transfers between devices with their start and end apart: 14 -> 4, of which waited for: 3 -> 0; matrix products, arithmetic and copies ran while one was open for 1% -> 0% of each run, Pallas kernels for 0% -> 0%
where the time goes in v1:
time: 113 us; the launch traced here: 112 us
  blocking collectives  85.8 us (76%)
  starting transfers between devices  12 us (11%)
  Pallas kernels  9.64 us (9%)
  local copies, waits for them, and re-layouts  3.8 us (3%)
    all_to_all x6, blocking collectives, exchange(): return lax.all_to_all(array, axes, 0, 0, tiled=True)  85.8 us
    ppermute x4, starting transfers between devices, shifted(): return lax.ppermute(array, axis, pairs)  12 us
    pallas_call x7, Pallas kernels, call(): pl.pallas_call(kernel, out_shape=outs, in_specs=[VMEM] * len(ins), out_sp...  9.64 us
    unnamed x12, local copies, waits for them, and re-layouts  3.8 us
  transfers between devices with their start and end apart: 4, of which 0 were waited for; matrix products, arithmetic and copies ran while one was open for 0% of the time, Pallas kernels for 0%

profile of v1, /device:TPU:1, one launch (start us, length us, event | category | flops | bytes accessed | tf_op | source)
XLA Modules:
  0.0 112.0 jit_solution(17722813342909559447)
XLA Ops:
  0.6 0.0 copy-start
  0.6 1.0 copy-done
  1.6 1.0 copy-done.2
  2.6 0.9 copy-done.4
  3.5 0.9 copy-done.5
  4.4 0.5 shard_map.59
  5.0 4.0 %collective-permute-start = (f32[5,16,4,128]{3,2,1,0:T(4,128)S(1)}, f32[5,16,4,128]{3,2,1,0:T(4,128)S(1)}, u32[]{:S(2)}, u32[]{:S(2)}) collective-permute-start(f32[5,16,4,128]{3,2,1,0:T(4,128)S(1)} %get-tuple-element.19), channel_id=1, source_target_pairs={{0,1},{1,2},{2,3},{3,4},{4,5},{5,6},{6,7},{8,9},{9,10},{10,11},{11... | collective-permute-start | bytes 491528 | tf_op jit(solution)/shard_map/ppermute | solution.py:325
  9.0 1.3 %collective-permute-start.1 = (f32[5,16,4,128]{3,2,1,0:T(4,128)S(1)}, f32[5,16,4,128]{3,2,1,0:T(4,128)S(1)}, u32[]{:S(2)}, u32[]{:S(2)}) collective-permute-start(f32[5,16,4,128]{3,2,1,0:T(4,128)S(1)} %get-tuple-element.20), channel_id=1, source_target_pairs={{1,0},{2,1},{3,2},{4,3},{5,4},{6,5},{7,6},{9,8},{10,9},{11,10},{12... | collective-permute-start | bytes 491528 | tf_op jit(solution)/shard_map/ppermute | solution.py:325
  10.3 21.5 %all_to_all.30.recv_ref = f32[32,4,128]{2,1,0:T(4,128)S(1)} all-to-all(f32[32,4,128]{2,1,0:T(4,128)S(1)} %get-tuple-element.18), channel_id=1, replica_groups=mesh['x'=4,'z'=8,'c'=2,'y'=8] {'x','z'}, dimensions={0} | all-to-all | bytes 131072 | tf_op jit(solution)/shard_map/all_to_all | solution.py:319
  31.9 0.1 shard_map.60
  32.0 4.8 %collective-permute-start.2 = (f32[5,3,24,128]{3,2,1,0:T(8,128)S(1)}, f32[5,3,24,128]{3,2,1,0:T(8,128)S(1)}, u32[]{:S(2)}, u32[]{:S(2)}) collective-permute-start(f32[5,3,24,128]{3,2,1,0:T(8,128)S(1)} %get-tuple-element.22), channel_id=1, source_target_pairs={{0,8},{8,16},{16,24},{24,32},{32,40},{40,48},{48,56},{56,64},{64,7... | collective-permute-start | bytes 552968 | tf_op jit(solution)/shard_map/ppermute | solution.py:325
  36.8 1.9 %collective-permute-start.3 = (f32[5,3,24,128]{3,2,1,0:T(8,128)S(1)}, f32[5,3,24,128]{3,2,1,0:T(8,128)S(1)}, u32[]{:S(2)}, u32[]{:S(2)}) collective-permute-start(f32[5,3,24,128]{3,2,1,0:T(8,128)S(1)} %get-tuple-element.23), channel_id=1, source_target_pairs={{8,0},{16,8},{24,16},{32,24},{40,32},{48,40},{56,48},{64,56},{72,6... | collective-permute-start | bytes 552968 | tf_op jit(solution)/shard_map/ppermute | solution.py:325
  38.7 16.3 %all_to_all.31.recv_ref = f32[16,4,128]{2,1,0:T(4,128)S(1)} all-to-all(f32[16,4,128]{2,1,0:T(4,128)S(1)} %get-tuple-element.21), channel_id=1, replica_groups=mesh['x'=4,'z'=8,'c'=2,'y'=8] {'c','y'}, dimensions={0} | all-to-all | bytes 65536 | tf_op jit(solution)/shard_map/all_to_all | solution.py:319
  55.0 0.0 collective-permute-done.2.below_ref
  55.0 0.0 collective-permute-done.3.above_ref
  55.1 0.0 copy-start.1
  55.1 4.2 %shard_map.61 = (f32[32,4,128]{2,1,0:T(4,128)S(1)}, f32[22,24,128]{2,1,0:T(8,128)S(1)}, f32[22,24,128]{2,1,0:T(8,128)S(1)}, f32[22,24,128]{2,1,0:T(8,128)S(1)}, ...) custom-call(f32[16,4,128]{2,1,0:T(4,128)S(1)} %all_to_all.31.recv_ref, f32[3,16,16,128]{3,2,1,0:T(8,128)S(1)} %copy-done, ...), custom_call_target="tpu_custom_call" | custom-call | tf_op jit(solution)/shard_map/pallas_call | solution.py:25
  59.3 14.6 %all_to_all.32.recv_ref = f32[32,4,128]{2,1,0:T(4,128)S(1)} all-to-all(f32[32,4,128]{2,1,0:T(4,128)S(1)} %get-tuple-element.24), channel_id=1, replica_groups=mesh['x'=4,'z'=8,'c'=2,'y'=8] {'x','z'}, dimensions={0} | all-to-all | bytes 131072 | tf_op jit(solution)/shard_map/all_to_all | solution.py:319
  73.9 0.1 shard_map.62
  74.1 11.6 %all_to_all.33.recv_ref = f32[16,4,128]{2,1,0:T(4,128)S(1)} all-to-all(f32[16,4,128]{2,1,0:T(4,128)S(1)} %shard_map.62), channel_id=1, replica_groups=mesh['x'=4,'z'=8,'c'=2,'y'=8] {'c','y'}, dimensions={0} | all-to-all | bytes 65536 | tf_op jit(solution)/shard_map/all_to_all | solution.py:319
  85.7 2.2 %shard_map.63 = (f32[16,1,128]{2,1,0:T(1,128)S(1)}, f32[1,128]{1,0:T(1,128)S(1)}, f32[3,18,24,128]{3,2,1,0:T(8,128)S(1)}, f32[3,16,16,128]{3,2,1,0:T(8,128)S(1)}) custom-call(f32[16,4,128]{2,1,0:T(4,128)S(1)} %all_to_all.33.recv_ref, f32[3,16,16,128]{3,2,1,0:T(8,128)S(1)} %copy-done.1, f32[22,24,128]{2,1,0:T(8,128)S(1)} %get-tuple-element.25.k_ref, ...), custom_call_target="tpu_custom_call" | custom-call | tf_op jit(solution)/shard_map/pallas_call | solution.py:25
  87.9 10.1 %all_to_all.34.recv_ref = f32[16,1,128]{2,1,0:T(1,128)S(1)} all-to-all(f32[16,1,128]{2,1,0:T(1,128)S(1)} %get-tuple-element.30), channel_id=1, replica_groups=mesh['x'=4,'z'=8,'c'=2,'y'=8] {'c','y'}, dimensions={0} | all-to-all | bytes 16384 | tf_op jit(solution)/shard_map/all_to_all | solution.py:319
  98.0 11.6 %all_to_all.35.recv_ref = f32[32,1,128]{2,1,0:T(1,128)S(1)} all-to-all(f32[32,1,128]{2,1,0:T(1,128)S(1)} %shard_map.64), channel_id=1, replica_groups=mesh['x'=4,'z'=8,'c'=2,'y'=8] {'x','z'}, dimensions={0} | all-to-all | bytes 32768 | tf_op jit(solution)/shard_map/all_to_all | solution.py:319
  109.6 2.4 %shard_map.65 = (f32[3,16,16,128]{3,2,1,0:T(8,128)}, f32[3,16,16,128]{3,2,1,0:T(8,128)}) custom-call(f32[32,1,128]{2,1,0:T(1,128)S(1)} %all_to_all.35.recv_ref, f32[1,128]{1,0:T(1,128)S(1)} %get-tuple-element.31.scal_ref, f32[3,16,16,128]{3,2,1,0:T(8,128)S(1)} %copy-done.1, f32[3,22,24,128]{3,2,1,0:T(8,128)S(1)} %get-tuple-element.28.z_ref, ...), custom_call_target="tpu_custom_call" | custom-call | tf_op jit(solution)/shard_map/pallas_call | solution.py:25
  (9 shorter events, 0.0 us)
Async XLA Ops:
  0.6 1.0 copy-start
  1.6 1.0 copy-start.2
  2.6 0.9 copy-start.4
  3.5 0.9 copy-start.5
  5.0 26.9 %collective-permute-start = (f32[5,16,4,128]{3,2,1,0:T(4,128)S(1)}, f32[5,16,4,128]{3,2,1,0:T(4,128)S(1)}, u32[]{:S(2)}, u32[]{:S(2)}) collective-permute-start(f32[5,16,4,128]{3,2,1,0:T(4,128)S(1)} %get-tuple-element.19), channel_id=1, source_target_pairs={{0,1},{1,2},{2,3},{3,4},{4,5},{5,6},{6,7},{8,9},{9,10},{10,11},{11... | collective-permute-start | bytes 491528 | tf_op jit(solution)/shard_map/ppermute | solution.py:325
  9.0 22.9 %collective-permute-start.1 = (f32[5,16,4,128]{3,2,1,0:T(4,128)S(1)}, f32[5,16,4,128]{3,2,1,0:T(4,128)S(1)}, u32[]{:S(2)}, u32[]{:S(2)}) collective-permute-start(f32[5,16,4,128]{3,2,1,0:T(4,128)S(1)} %get-tuple-element.20), channel_id=1, source_target_pairs={{1,0},{2,1},{3,2},{4,3},{5,4},{6,5},{7,6},{9,8},{10,9},{11,10},{12... | collective-permute-start | bytes 491528 | tf_op jit(solution)/shard_map/ppermute | solution.py:325
  31.9 23.2 %copy-start.3 = (f32[12,6144]{1,0:T(8,128)S(1)}, f32[12,6144]{1,0:T(8,128)}, u32[]{:S(2)}) copy-start(f32[12,6144]{1,0:T(8,128)} %coarse_ref.3) | copy-start | bytes 884740
  32.0 23.0 %collective-permute-start.2 = (f32[5,3,24,128]{3,2,1,0:T(8,128)S(1)}, f32[5,3,24,128]{3,2,1,0:T(8,128)S(1)}, u32[]{:S(2)}, u32[]{:S(2)}) collective-permute-start(f32[5,3,24,128]{3,2,1,0:T(8,128)S(1)} %get-tuple-element.22), channel_id=1, source_target_pairs={{0,8},{8,16},{16,24},{24,32},{32,40},{40,48},{48,56},{56,64},{64,7... | collective-permute-start | bytes 552968 | tf_op jit(solution)/shard_map/ppermute | solution.py:325
  36.8 18.3 %collective-permute-start.3 = (f32[5,3,24,128]{3,2,1,0:T(8,128)S(1)}, f32[5,3,24,128]{3,2,1,0:T(8,128)S(1)}, u32[]{:S(2)}, u32[]{:S(2)}) collective-permute-start(f32[5,3,24,128]{3,2,1,0:T(8,128)S(1)} %get-tuple-element.23), channel_id=1, source_target_pairs={{8,0},{16,8},{24,16},{32,24},{40,32},{48,40},{56,48},{64,56},{72,6... | collective-permute-start | bytes 552968 | tf_op jit(solution)/shard_map/ppermute | solution.py:325
  55.1 30.6 %copy-start.1 = (f32[3,16,16,128]{3,2,1,0:T(8,128)S(1)}, f32[3,16,16,128]{3,2,1,0:T(8,128)}, u32[]{:S(2)}) copy-start(f32[3,16,16,128]{3,2,1,0:T(8,128)} %r_ref.9) | copy-start | bytes 1179652

commit v2 on v1

v2 whole, which is shorter than its diff:
```python
import jax
import jax.numpy as jnp
import numpy as np
from jax import lax
from jax.experimental import pallas as pl
from jax.experimental.pallas import tpu as pltpu
from jax.sharding import Mesh
from jax.sharding import PartitionSpec as P

WIDE = ("x", "z", "c")
ROWS = ("x", "z")
COLS = ("c", "y")
NROWS = 32
NCOLS = 16
F32 = jnp.float32
NREG = 4
SLAB = 96
VMEM = pl.BlockSpec(memory_space=pltpu.VMEM)


def shape(*dims):
    return jax.ShapeDtypeStruct(dims, F32)


def call(kernel, outs, ins, scratch=(), space=VMEM, cost=0, limit=24):
    return pl.pallas_call(
        kernel,
        out_shape=outs,
        in_specs=[space] * len(ins),
        out_specs=jax.tree.map(lambda _: VMEM, outs),
        scratch_shapes=list(scratch),
        cost_estimate=pl.CostEstimate(flops=cost, bytes_accessed=cost, transcendentals=0) if cost else None,
        compiler_params=pltpu.CompilerParams(vmem_limit_bytes=int(limit * 1024 * 1024)),
    )(*ins)


def total(v):
    return jnp.sum(jnp.sum(v, axis=0, keepdims=True), axis=1, keepdims=True)


def add_regions(accs, label, field):
    out = list(accs)
    for g in range(NREG):
        mask = label == g + 1
        for c in range(3):
            out[3 * g + c] = out[3 * g + c] + jnp.where(mask, field[c], 0.0)
    return out


def in_lanes(acc_ref, at):
    sums = jnp.sum(jnp.sum(acc_ref[...], axis=1), axis=1, keepdims=True)
    row = lax.broadcasted_iota(jnp.int32, (12, 128), 0)
    lane = lax.broadcasted_iota(jnp.int32, (12, 128), 1)
    return jnp.sum(jnp.where(lane == row + at, sums, 0.0), axis=0, keepdims=True)


def fold(accs, coarse_ref, acc_ref, u_ref, pad_ref, out_ref, sums=()):
    for i in range(3 * NREG):
        acc_ref[i] = accs[i]
    rc = jnp.sum(jnp.sum(acc_ref[...], axis=1), axis=1, keepdims=True)
    u_ref[...] = jnp.sum(coarse_ref[...] * rc, axis=0, keepdims=True)
    pad_ref[...] = jnp.zeros_like(pad_ref)
    for w in range(2 * NROWS):
        pad_ref[w + 1 : w + 2, 0:SLAB] = u_ref[0:1, SLAB * w : SLAB * (w + 1)]
    if sums:
        lane = lax.broadcasted_iota(jnp.int32, (1, 128), 1)
        row = jnp.zeros((1, 128), F32)
        for i, s in enumerate(sums):
            row = jnp.where(lane == SLAB + i, s, row)
        tail = jnp.broadcast_to(row, (4, 128))
    for n in range(NROWS):
        window = pad_ref[2 * n : 2 * n + 4, :]
        if sums:
            window = window + tail
        out_ref[n] = window


FOLD_SCRATCH = (
    pltpu.VMEM((12, 16, 128), F32),
    pltpu.VMEM((1, 6144), F32),
    pltpu.VMEM((72, 128), F32),
)


def first_kernel(
    r_hbm, occ_hbm, reg_hbm, coarse_hbm,
    out_ref, lo_ref, hi_ref, r_ref, k_ref, label_ref, coarse_ref,
    occ_ref, reg_ref, acc_ref, u_ref, pad_ref, sems,
):
    pairs = ((r_hbm, r_ref), (reg_hbm, reg_ref), (occ_hbm, occ_ref), (coarse_hbm, coarse_ref))
    copies = [pltpu.make_async_copy(a, b, sems.at[i]) for i, (a, b) in enumerate(pairs)]
    for copy in copies:
        copy.start()
    for copy in copies[:3]:
        copy.wait()
    k_ref[...] = 0.1 + 0.9 * occ_ref[...].astype(F32)
    label_ref[...] = reg_ref[...].astype(F32) + 1.0
    for ref, deep, flat in ((lo_ref, 0, 0), (hi_ref, 12, 14)):
        ref[0] = k_ref[:, deep : deep + 4, :]
        ref[1, :, 0:2] = label_ref[:, flat : flat + 2, :]
        ref[1, :, 2:4] = r_ref[0, :, flat : flat + 2, :]
        ref[2, :, 0:2] = r_ref[1, :, flat : flat + 2, :]
        ref[2, :, 2:4] = r_ref[2, :, flat : flat + 2, :]

    def step(x, accs):
        return tuple(add_regions(accs, label_ref[x], [r_ref[c, x] for c in range(3)]))

    zero = jnp.zeros((16, 128), F32)
    accs = lax.fori_loop(0, 16, step, (zero,) * 12, unroll=2)
    copies[3].wait()
    fold(accs, coarse_ref, acc_ref, u_ref, pad_ref, out_ref)


def hand_out(part, out_ref):
    for c in range(2):
        rows = part[c : c + 3]
        for y in range(8):
            out_ref[8 * c + y, 0:3, :] = pltpu.roll(rows, (12 - 12 * y) % 128, axis=1)
            out_ref[8 * c + y, 3:4, :] = part[0:1]


def tail_rows(lo_ref, hi_ref, i, planes):
    if i == 0:
        return jnp.concatenate([hi_ref[0, planes], lo_ref[0, planes]], axis=1)
    block, at = 1 + (i - 1) // 2, 2 * ((i - 1) % 2)
    above, below = hi_ref[block, planes, at : at + 2], lo_ref[block, planes, at : at + 2]
    none = jnp.zeros((above.shape[0], 4, 128), F32)
    return jnp.concatenate([above, none, below], axis=1)


PACK = 72 + 4 * 40


def pack_kernel(k_ref, label_ref, r_ref, lo_ref, hi_ref, up_ref, down_ref):
    fields = [label_ref] + [r_ref.at[c] for c in range(3)]
    for ref, deep, near, next_ in ((up_ref, 13, 15, 14), (down_ref, 0, 0, 1)):
        tails = tail_rows(lo_ref, hi_ref, 0, pl.ds(deep, 3))
        for i in range(3):
            ref[24 * i : 24 * i + 16] = k_ref[deep + i]
            ref[24 * i + 16 : 24 * i + 24] = tails[i]
        for i, field in enumerate(fields):
            at = 72 + 40 * i
            ref[at : at + 16] = field[near]
            ref[at + 16 : at + 24] = tail_rows(lo_ref, hi_ref, 1 + i, pl.ds(near, 1))[0]
            ref[at + 24 : at + 40] = field[next_]


def extend_kernel(
    r_ref, k_own_ref, label_own_ref, lo_ref, hi_ref, below_ref, above_ref, k_ref, label_ref, inv_ref, f_ref
):
    whole = pl.ds(0, 16)
    k_ref[3:19, 0:16] = k_own_ref[...]
    label_ref[3:19, 0:16] = label_own_ref[...]
    k_ref[3:19, 16:24] = tail_rows(lo_ref, hi_ref, 0, whole)
    label_ref[3:19, 16:24] = tail_rows(lo_ref, hi_ref, 1, whole)
    none = jnp.zeros((8, 128), F32)
    for i in range(3):
        k_ref[i] = below_ref[24 * i : 24 * i + 24]
        k_ref[19 + i] = above_ref[24 * i : 24 * i + 24]
    targets = [label_ref] + [f_ref.at[c] for c in range(3)]
    for i, ref in enumerate(targets):
        at = 72 + 40 * i
        for pack, near, next_ in ((below_ref, 2, 1), (above_ref, 19, 20)):
            ref[near] = pack[at : at + 24]
            ref[next_, 0:16] = pack[at + 24 : at + 40]
            ref[next_, 16:24] = none
    for c in range(3):
        f_ref[c, 3:19, 0:16] = r_ref[c]
        f_ref[c, 3:19, 16:24] = tail_rows(lo_ref, hi_ref, 2 + c, whole)

    def step(x, carry):
        here = k_ref[x]
        _, diagonal = coefficients(k_ref[x - 1], here, k_ref[x + 1])
        inside = here > 0.0
        inv = jnp.where(inside, 1.0 / jnp.where(inside, diagonal, 1.0), 0.0)
        inv_ref[x] = inv
        for c in range(3):
            f_ref[c, x] = f_ref[c, x] * inv
        return carry

    lax.fori_loop(1, 21, step, 0, unroll=2)


def around_kernel(recv_ref, out_ref):
    hand_out(jnp.sum(recv_ref[...], axis=0), out_ref)


def pass_kernel(recv_ref, own_ref, pair_ref, out_ref):
    part = jnp.sum(recv_ref[...], axis=0)
    rows = jnp.concatenate([part, own_ref[...], pair_ref[...]], axis=0)
    for n in range(NCOLS):
        out_ref[n] = rows


def iotas():
    lane = lax.broadcasted_iota(jnp.int32, (24, 128), 1)
    return lane == 0, lane == 127


def coefficients(before, here, after):
    first, last = iotas()
    y_up = pltpu.roll(here, 23, axis=0)
    y_down = pltpu.roll(here, 1, axis=0)
    z_up = jnp.where(last, 0.0, pltpu.roll(here, 127, axis=1))
    z_down = jnp.where(first, 0.0, pltpu.roll(here, 1, axis=1))
    half = 0.5 * here
    faces = [half + 0.5 * other for other in (after, before, y_up, y_down, z_up, z_down)]
    diagonal = faces[0] + faces[1] + faces[2] + faces[3] + faces[4] + faces[5] + half
    faces[4] = jnp.where(last, 0.0, faces[4])
    faces[5] = jnp.where(first, 0.0, faces[5])
    return faces, diagonal


def operate(faces, diagonal, here, befores, fields, afters):
    quarter = 0.25 * here
    main = diagonal - quarter
    shared = quarter * (fields[0] + fields[1] + fields[2])
    out = []
    for c in range(3):
        u = fields[c]
        out.append(
            main * u
            + shared
            - faces[0] * afters[c]
            - faces[1] * befores[c]
            - faces[2] * pltpu.roll(u, 23, axis=0)
            - faces[3] * pltpu.roll(u, 1, axis=0)
            - faces[4] * pltpu.roll(u, 127, axis=1)
            - faces[5] * pltpu.roll(u, 1, axis=1)
        )
    return out


def spread_maps(q, map_ref):
    row = lax.broadcasted_iota(jnp.int32, (24, 128), 0)
    for s in range(3):
        for i in range(12):
            below, own, above = (q[s : s + 1, 12 * d + i : 12 * d + i + 1] for d in range(3))
            map_ref[s, i] = jnp.where(row < 16, own, jnp.where(row < 20, above, below))


def spread(label, map_ref, s, c):
    out = jnp.zeros((24, 128), F32)
    for g in range(NREG):
        out = jnp.where(label == g + 1, map_ref[s, 3 * g + c], out)
    return out


def second_kernel(
    recv_ref, r_ref, k_ref, label_ref, f_ref, coarse_ref,
    out_ref, z_ref, w_ref, own_ref,
    map_ref, acc_ref, u_ref, pad_ref,
):
    q = jnp.sum(recv_ref[...], axis=0)
    spread_maps(q, map_ref)

    def first_step(s):
        def body(x, carry):
            label = label_ref[x]
            for c in range(3):
                z_ref[c, x] = f_ref[c, x] + spread(label, map_ref, s, c)
            return carry

        return body

    lax.fori_loop(1, 3, first_step(0), 0)
    lax.fori_loop(3, 19, first_step(1), 0, unroll=2)
    lax.fori_loop(19, 21, first_step(2), 0)

    def image(x):
        here = k_ref[x]
        faces, diagonal = coefficients(k_ref[x - 1], here, k_ref[x + 1])
        fields = [z_ref[c, x] for c in range(3)]
        w = operate(
            faces, diagonal, here, [z_ref[c, x - 1] for c in range(3)], fields, [z_ref[c, x + 1] for c in range(3)]
        )
        for c in range(3):
            w_ref[c, x] = w[c]
        return fields, w

    image(2)
    image(19)

    def second_step(x, carry):
        fields, w = image(x)
        own = [v[0:16] for v in w]
        rz, zw = carry[12], carry[13]
        for c in range(3):
            z = fields[c][0:16]
            rz = rz + r_ref[c, x - 3] * z
            zw = zw + z * own[c]
        return (*add_regions(carry[:12], label_ref[x, 0:16], own), rz, zw)

    zero = jnp.zeros((16, 128), F32)
    carry = lax.fori_loop(3, 19, second_step, (zero,) * 14)
    fold(carry[:12], coarse_ref, acc_ref, u_ref, pad_ref, out_ref, (total(carry[12]), total(carry[13])))
    own_ref[...] = in_lanes(acc_ref, 12)


def selection():
    out = np.zeros((88, 3 * 128), np.float32)
    for n in range(5):
        for d in range(4):
            for h in range(4):
                g = (h + d) % 4
                for c in range(3):
                    lane = 128 * (n // 2) + 48 * (n % 2) + 12 * d + 3 * h + c
                    out[16 * n + 4 * g + h, lane] -= 1.0
                    if n == 0:
                        out[4 * h + g, lane] -= 1.0
                        if d == 0:
                            out[80 + g, lane] += 1.0
                            out[84 + g, lane] += 1.0
    for g in range(4):
        out[80 + g, 96 + 3 * g] = 1.0
    return out


def tiles(v):
    return v[0:8] + v[8:16]


def pair_kernel(k_ref, label_ref, select_ref, out_ref, acc_ref):
    row = lax.broadcasted_iota(jnp.int32, (24, 128), 0)
    lane = lax.broadcasted_iota(jnp.int32, (24, 128), 1)

    def plane(x, accs, inner):
        here, label = k_ref[x], label_ref[x]
        faces, diagonal = coefficients(k_ref[x - 1], here, k_ref[x + 1])
        y_label = jnp.where(row == 15, 0.0, pltpu.roll(label, 23, axis=0))[0:16]
        z_label = jnp.where(lane == 127, 0.0, pltpu.roll(label, 127, axis=1))[0:16]
        own = label[0:16]
        quarter, coupling = 0.25 * here[0:16], (diagonal - 0.5 * here)[0:16]
        masks = [own == g + 1 for g in range(NREG)]
        out = list(accs)
        for h in range(NREG):
            v = jnp.where(y_label == h + 1, faces[2][0:16], 0.0) + jnp.where(z_label == h + 1, faces[4][0:16], 0.0)
            if inner:
                v = v + jnp.where(label_ref[x + 1, 0:16] == h + 1, faces[0][0:16], 0.0)
            for g in range(NREG):
                out[4 * g + h] = out[4 * g + h] + tiles(jnp.where(masks[g], v, 0.0))
        for g in range(NREG):
            out[16 + g] = out[16 + g] + tiles(jnp.where(masks[g], quarter, 0.0))
            out[20 + g] = out[20 + g] + tiles(jnp.where(masks[g], coupling, 0.0))
        return tuple(out)

    zero = jnp.zeros((8, 128), F32)
    accs = lax.fori_loop(3, 18, lambda x, a: plane(x, a, True), (zero,) * 24)
    accs = plane(18, accs, False)
    for i in range(16):
        acc_ref[i] = accs[i]
    for i in range(8):
        acc_ref[80 + i] = accs[16 + i]
    own = pl.ds(3, 16)
    sides = (
        (k_ref[3, 0:16], label_ref[3, 0:16], k_ref[2, 0:16], label_ref[2, 0:16]),
        (k_ref[18, 0:16], label_ref[18, 0:16], k_ref[19, 0:16], label_ref[19, 0:16]),
        (k_ref[own, 0, :], label_ref[own, 0, :], k_ref[own, 23, :], label_ref[own, 23, :]),
        (k_ref[own, 15, :], label_ref[own, 15, :], k_ref[own, 16, :], label_ref[own, 16, :]),
    )
    for n, (k, label, other, other_label) in enumerate(sides):
        face = 0.5 * k + 0.5 * other
        for g in range(NREG):
            part = jnp.where(label == g + 1, face, 0.0)
            for h in range(NREG):
                acc_ref[16 * n + 16 + 4 * g + h] = tiles(jnp.where(other_label == h + 1, part, 0.0))
    sums = jnp.sum(jnp.sum(acc_ref[...], axis=1), axis=1, keepdims=True)
    for i in range(3):
        out_ref[i : i + 1] = jnp.sum(select_ref[:, 128 * i : 128 * i + 128] * sums, axis=0, keepdims=True)


def moment_kernel(k_ref, label_ref, inv_ref, w_ref, own_ref, out_ref, g_ref, acc_ref):
    def first_step(x, carry):
        inv = inv_ref[x]
        for c in range(3):
            g_ref[c, x - 2] = w_ref[c, x] * inv
        return carry

    lax.fori_loop(2, 20, first_step, 0, unroll=2)

    def step(x, carry):
        here = k_ref[x + 2]
        faces, diagonal = coefficients(k_ref[x + 1], here, k_ref[x + 3])
        fields = [g_ref[c, x] for c in range(3)]
        image = operate(
            faces, diagonal, here, [g_ref[c, x - 1] for c in range(3)], fields, [g_ref[c, x + 1] for c in range(3)]
        )
        own = [v[0:16] for v in image]
        wg, gg = carry[12], carry[13]
        for c in range(3):
            g = fields[c][0:16]
            wg = wg + w_ref[c, x + 2, 0:16] * g
            gg = gg + own[c] * g
        return (*add_regions(carry[:12], label_ref[x + 2, 0:16], own), wg, gg)

    zero = jnp.zeros((16, 128), F32)
    carry = lax.fori_loop(1, 17, step, (zero,) * 14)
    for i in range(12):
        acc_ref[i] = carry[i]
    lane = lax.broadcasted_iota(jnp.int32, (1, 128), 1)
    row = in_lanes(acc_ref, 0) + own_ref[...]
    out_ref[...] = jnp.where(lane == 24, total(carry[12]), jnp.where(lane == 25, total(carry[13]), row))


def group_kernel(recv_ref, out_ref):
    q = jnp.sum(recv_ref[:, 0:4, :], axis=0)
    own = recv_ref[:, 4, :]
    lane = lax.broadcasted_iota(jnp.int32, (16, 128), 1)
    shifted_rows = []
    for s in range(4):
        shifted_rows.append(
            jnp.concatenate([pltpu.roll(q[s : s + 1], (128 - 12 * y) % 128, axis=1) for y in range(8)], axis=0)
        )
    mine, below, above = (
        jnp.concatenate([shifted_rows[s], shifted_rows[s + 1]], axis=0) for s in (1, 0, 2)
    )

    def right(v, by):
        return pltpu.roll(v, by % 128, axis=1)

    def first(v):
        return jnp.where(lane < 12, v, 0.0)

    def four(v):
        v = first(v)
        v = v + right(v, 12)
        return v + right(v, 24)

    alone = first(mine)
    twice = alone + right(alone, 12)
    turned = alone
    for d in range(1, 4):
        turned = turned + right(first(right(twice, -3 * d)), 12 * d)
    turned = turned + right(turned, 48)
    three = mine + right(mine, -1) + right(mine, -2)
    products = (
        recv_ref[:, 5, :] * (turned * (four(mine) + right(four(below), 48)) + right(first(three * three), 96))
        + recv_ref[:, 6, :] * turned * (four(above) + right(four(right(mine, 12)), 48))
        + recv_ref[:, 7, :] * turned * four(right(mine, -12))
        + 2.0 * jnp.where(lane < 12, own * alone, 0.0)
        + jnp.where(lane == 25, own, 0.0)
    )
    pairing = jnp.where((lane >= 12) & (lane < 24), own * twice, jnp.where(lane == 24, own, 0.0))
    at = lax.broadcasted_iota(jnp.int32, (1, 128), 1)
    row = jnp.where(at == 0, total(pairing), jnp.where(at == 1, total(products), 0.0))
    for n in range(NROWS):
        out_ref[n] = row


def third_kernel(recv_ref, k_ref, label_ref, inv_ref, z_ref, w_ref, scal_ref, znew_ref, image_ref, map_ref):
    q = jnp.sum(recv_ref[:, 0:4, :], axis=0)
    near = jnp.where(lax.axis_index("c") == 0, q[0:3], q[1:4])
    spread_maps(pltpu.roll(near, lax.rem(140 - 12 * lax.axis_index("y"), 128), axis=1), map_ref)
    scal_ref[...] = q[0:1]
    rz, zw = q[0:1, SLAB : SLAB + 1], q[0:1, SLAB + 1 : SLAB + 2]
    alpha = rz / zw

    def first_step(s):
        def body(x, carry):
            inv, label = inv_ref[x], label_ref[x]
            for c in range(3):
                y = w_ref[c, x] * inv + spread(label, map_ref, s, c)
                znew_ref[c, x - 2] = z_ref[c, x] - alpha * y
            return carry

        return body

    first_step(0)(2, 0)
    lax.fori_loop(3, 19, first_step(1), 0, unroll=2)
    first_step(2)(19, 0)

    def second_step(x, carry):
        here = k_ref[x + 2]
        faces, diagonal = coefficients(k_ref[x + 1], here, k_ref[x + 3])
        fields = [znew_ref[c, x] for c in range(3)]
        image = operate(
            faces, diagonal, here, [znew_ref[c, x - 1] for c in range(3)], fields, [znew_ref[c, x + 1] for c in range(3)]
        )
        for c in range(3):
            image_ref[c, x - 1] = image[c][0:16]
        return carry

    lax.fori_loop(1, 17, second_step, 0)


def last_kernel(recv_ref, scal_ref, r_ref, z_ref, w_ref, znew_ref, image_ref, x_ref, res_ref):
    sums = jnp.sum(recv_ref[...], axis=0)
    wy, yay = sums[:, 0:1], sums[:, 1:2]
    scal = scal_ref[...]
    rz, zw = scal[:, SLAB : SLAB + 1], scal[:, SLAB + 1 : SLAB + 2]
    alpha = rz / zw
    new = rz + alpha * (alpha * wy - 2.0 * zw)
    zaz = zw + alpha * (alpha * yay - 2.0 * wy)
    cross = zw - alpha * wy
    ratio = new / rz
    second = new / (zaz + ratio * (2.0 * cross + ratio * zw))
    first = alpha + second * ratio

    def step(x, carry):
        for c in range(3):
            x_ref[c, x] = first * z_ref[c, x + 3, 0:16] + second * znew_ref[c, x + 1, 0:16]
            res_ref[c, x] = r_ref[c, x] - first * w_ref[c, x + 3, 0:16] - second * image_ref[c, x]
        return carry

    lax.fori_loop(0, 16, step, 0, unroll=2)


def exchange(array, axes):
    return lax.all_to_all(array, axes, 0, 0, tiled=True)


def shifted(array, axis, step):
    count = lax.axis_size(axis)
    pairs = [(i, i + step) for i in range(count) if 0 <= i + step < count]
    return lax.ppermute(array, axis, pairs)


def local(right, occ, reg, coarse):
    field, plane = (16, 16, 128), (24, 128)
    send, lo, hi, r, k_own, label_own, coarse = call(
        first_kernel,
        (
            shape(NROWS, 4, 128),
            shape(3, 16, 4, 128),
            shape(3, 16, 4, 128),
            shape(3, *field),
            shape(*field),
            shape(*field),
            shape(12, 6144),
        ),
        (right, occ, reg, coarse),
        (
            pltpu.VMEM(field, jnp.int32),
            pltpu.VMEM(field, jnp.int32),
            *FOLD_SCRATCH,
            pltpu.SemaphoreType.DMA((4,)),
        ),
        space=pl.BlockSpec(memory_space=pltpu.HBM),
        limit=53.5,
    )
    before = shifted(hi, "y", 1)
    after = shifted(lo, "y", -1)
    got = exchange(send, ROWS)
    up, down = call(
        pack_kernel, (shape(PACK, 128), shape(PACK, 128)), (k_own, label_own, r, before, after), cost=1000000
    )
    below = shifted(up, WIDE, 1)
    above = shifted(down, WIDE, -1)
    send = call(around_kernel, shape(NCOLS, 4, 128), (got,))
    got = exchange(send, COLS)
    k, label, inv, f = call(
        extend_kernel,
        (shape(22, *plane), shape(22, *plane), shape(22, *plane), shape(3, 22, *plane)),
        (r, k_own, label_own, before, after, below, above),
        cost=3000000,
    )
    pair = call(
        pair_kernel, shape(3, 128), (k, label, jnp.asarray(selection())), (pltpu.VMEM((88, 8, 128), F32),), cost=3000000
    )
    send, z, w, own = call(
        second_kernel,
        (shape(NROWS, 4, 128), shape(3, 22, *plane), shape(3, 22, *plane), shape(1, 128)),
        (got, r, k, label, f, coarse),
        (pltpu.VMEM((3, 12, *plane), F32), *FOLD_SCRATCH),
    )
    got = exchange(send, ROWS)
    own = call(
        moment_kernel,
        shape(1, 128),
        (k, label, inv, w, own),
        (pltpu.VMEM((3, 18, *plane), F32), pltpu.VMEM((12, 16, 128), F32)),
        cost=3000000,
    )
    send = call(pass_kernel, shape(NCOLS, 8, 128), (got, own, pair))
    got = exchange(send, COLS)
    send = call(group_kernel, shape(NROWS, 1, 128), (got,))
    scal, znew, image = call(
        third_kernel,
        (shape(1, 128), shape(3, 18, *plane), shape(3, *field)),
        (got, k, label, inv, z, w),
        (pltpu.VMEM((3, 12, *plane), F32),),
        cost=3000000,
    )
    got = exchange(send, ROWS)
    return call(
        last_kernel,
        (shape(3, *field), shape(3, *field)),
        (got, scal, r, z, w, znew, image),
    )


def solution(mesh):
    finer = Mesh(mesh.devices.reshape(4, 8, 2, 8), ("x", "z", "c", "y"))
    field = P(None, WIDE, "y", None)
    labels = P(WIDE, "y", None)
    return jax.shard_map(
        local,
        mesh=finer,
        in_specs=(field, labels, labels, P((*WIDE, "y"), None)),
        out_specs=(field, field),
        check_vma=False,
    )
```

time: 113 us -> 101 us (0.89)
  blocking collectives: 85.8 us -> 11.8 us
  starting transfers between devices: 12 us -> 48.7 us
  waiting for transfers between devices: 0.01 us -> 16.3 us
  Pallas kernels: 9.64 us -> 16.9 us
  local copies, waits for them, and re-layouts: 3.8 us -> 6.05 us
    all_to_all x6 -> x1, blocking collectives: 85.8 us -> 11.8 us  [exchange(): return lax.all_to_all(array, axes, 0, 0, tiled=True)]
    all_to_all x0 -> x4, starting transfers between devices: none -> 36.7 us  [exchange(): return lax.all_to_all(array, axes, 0, 0, tiled=True)]
    all_to_all x0 -> x4, waiting for transfers between devices: none -> 16.3 us  [exchange(): return lax.all_to_all(array, axes, 0, 0, tiled=True)]
    pallas_call x7 -> x11, Pallas kernels: 9.64 us -> 16.9 us  [call(): pl.pallas_call(kernel, out_shape=outs, in_specs=[space] * len(ins), out_s...]
    unnamed x12 -> x22, local copies, waits for them, and re-layouts: 3.8 us -> 6.05 us
  transfers between devices with their start and end apart: 4 -> 8, of which waited for: 0 -> 4; matrix products, arithmetic and copies ran while one was open for 0% -> 0% of each run, Pallas kernels for 0% -> 8%
where the time goes in v2:
time: 101 us
  starting transfers between devices  48.7 us (48%)
  Pallas kernels  16.9 us (17%)
  waiting for transfers between devices  16.3 us (16%)
  blocking collectives  11.8 us (12%)
  local copies, waits for them, and re-layouts  6.05 us (6%)
    all_to_all x4, starting transfers between devices, exchange(): return lax.all_to_all(array, axes, 0, 0, tiled=True)  36.7 us
    pallas_call x11, Pallas kernels, call(): pl.pallas_call(kernel, out_shape=outs, in_specs=[space] * len(ins), out_s...  16.9 us
    all_to_all x4, waiting for transfers between devices, exchange(): return lax.all_to_all(array, axes, 0, 0, tiled=True)  16.3 us
    ppermute x4, starting transfers between devices, shifted(): return lax.ppermute(array, axis, pairs)  12 us
    all_to_all x1, blocking collectives, exchange(): return lax.all_to_all(array, axes, 0, 0, tiled=True)  11.8 us
    unnamed x22, local copies, waits for them, and re-layouts  6.05 us
  transfers between devices with their start and end apart: 8, of which 4 were waited for; matrix products, arithmetic and copies ran while one was open for 0% of the time, Pallas kernels for 8%

profile of v2, /device:TPU:1, one launch (start us, length us, event | category | flops | bytes accessed | tf_op | source)
XLA Modules:
  0.0 100.6 jit_solution(2213243405191517498)
XLA Ops:
  0.6 2.3 %shard_map.68 = (f32[32,4,128]{2,1,0:T(4,128)}, f32[3,16,4,128]{3,2,1,0:T(4,128)S(1)}, f32[3,16,4,128]{3,2,1,0:T(4,128)S(1)}, f32[3,16,16,128]{3,2,1,0:T(8,128)}...) custom-call(f32[3,16,16,128]{3,2,1,0:T(8,128)} %r_hbm.1, s32[16,16,128]{2,1,0:T(8,128)} %occ_hbm.1, ...), custom_call_target="tpu_custom_call" | custom-call | tf_op jit(solution)/shard_map/pallas_call | solution.py:26
  2.9 4.2 %collective-permute-start = (f32[3,16,4,128]{3,2,1,0:T(4,128)S(1)}, f32[3,16,4,128]{3,2,1,0:T(4,128)S(1)}, u32[]{:S(2)}, u32[]{:S(2)}) collective-permute-start(f32[3,16,4,128]{3,2,1,0:T(4,128)S(1)} %get-tuple-element.26), channel_id=1, source_target_pairs={{0,1},{1,2},{2,3},{3,4},{4,5},{5,6},{6,7},{8,9},{9,10},{10,11},{11... | collective-permute-start | bytes 294920 | tf_op jit(solution)/shard_map/ppermute | solution.py:515
  7.1 1.3 %collective-permute-start.1 = (f32[3,16,4,128]{3,2,1,0:T(4,128)S(1)}, f32[3,16,4,128]{3,2,1,0:T(4,128)S(1)}, u32[]{:S(2)}, u32[]{:S(2)}) collective-permute-start(f32[3,16,4,128]{3,2,1,0:T(4,128)S(1)} %get-tuple-element.27), channel_id=1, source_target_pairs={{1,0},{2,1},{3,2},{4,3},{5,4},{6,5},{7,6},{9,8},{10,9},{11,10},{12... | collective-permute-start | bytes 294920 | tf_op jit(solution)/shard_map/ppermute | solution.py:515
  8.4 12.9 %all-to-all-start = ((f32[32,4,128]{2,1,0:T(4,128)}), f32[32,4,128]{2,1,0:T(4,128)S(1)}, u32[]{:S(2)}, u32[]{:S(2)}) async-start(f32[32,4,128]{2,1,0:T(4,128)} %get-tuple-element.22), calls=%async_computation | async-start | bytes 131072 | tf_op jit(solution)/shard_map/all_to_all | solution.py:509
  21.4 1.0 copy-done
  22.4 4.7 %collective-permute-start.2 = (f32[232,128]{1,0:T(8,128)S(1)}, f32[232,128]{1,0:T(8,128)S(1)}, u32[]{:S(2)}, u32[]{:S(2)}) collective-permute-start(f32[232,128]{1,0:T(8,128)S(1)} %get-tuple-element.28), channel_id=1, source_target_pairs={{0,8},{8,16},{16,24},{24,32},{32,40},{40,48},{48,56},{56,64},{64,7... | collective-permute-start | bytes 356360 | tf_op jit(solution)/shard_map/ppermute | solution.py:515
  27.1 1.9 %collective-permute-start.3 = (f32[232,128]{1,0:T(8,128)S(1)}, f32[232,128]{1,0:T(8,128)S(1)}, u32[]{:S(2)}, u32[]{:S(2)}) collective-permute-start(f32[232,128]{1,0:T(8,128)S(1)} %get-tuple-element.29), channel_id=1, source_target_pairs={{8,0},{16,8},{24,16},{32,24},{40,32},{48,40},{56,48},{64,56},{72,6... | collective-permute-start | bytes 356360 | tf_op jit(solution)/shard_map/ppermute | solution.py:515
  29.0 1.2 %all-to-all-done.recv_ref = f32[32,4,128]{2,1,0:T(4,128)S(1)} async-done(((f32[32,4,128]{2,1,0:T(4,128)}), f32[32,4,128]{2,1,0:T(4,128)S(1)}, u32[]{:S(2)}, u32[]{:S(2)}) %all-to-all-start) | async-done | bytes 65568 | tf_op jit(solution)/shard_map/all_to_all | solution.py:509
  30.9 11.8 %all-to-all-start.1 = ((f32[16,4,128]{2,1,0:T(4,128)}), f32[16,4,128]{2,1,0:T(4,128)S(1)}, u32[]{:S(2)}, u32[]{:S(2)}) async-start(f32[16,4,128]{2,1,0:T(4,128)} %shard_map.69), calls=%async_computation.1 | async-start | bytes 65536 | tf_op jit(solution)/shard_map/all_to_all | solution.py:509
  42.7 1.1 %shard_map.71 = (f32[22,24,128]{2,1,0:T(8,128)S(1)}, f32[22,24,128]{2,1,0:T(8,128)S(1)}, f32[22,24,128]{2,1,0:T(8,128)S(1)}, f32[3,22,24,128]{3,2,1,0:T(8,128)S(1)}) custom-call(f32[3,16,16,128]{3,2,1,0:T(8,128)S(1)} %copy-done.1, f32[16,16,128]{2,1,0:T(8,128)S(1)} %get-tuple-element.24.k_ref.k_own_ref, f32[16,16,128]{2,1,0:T(8,128)S(1)} %copy-done.4, ...), custom_call_target="tpu_custom_call" | custom-call | flops 3000000 | bytes 3000000 | tf_op jit(solution)/shard_map/pallas_call | solution.py:26
  44.7 5.0 %all-to-all-done.1.recv_ref = f32[16,4,128]{2,1,0:T(4,128)S(1)} async-done(((f32[16,4,128]{2,1,0:T(4,128)}), f32[16,4,128]{2,1,0:T(4,128)S(1)}, u32[]{:S(2)}, u32[]{:S(2)}) %all-to-all-start.1) | async-done | bytes 32800 | tf_op jit(solution)/shard_map/all_to_all | solution.py:509
  49.7 1.1 %copy-done.3 = f32[3,22,24,128]{3,2,1,0:T(8,128)S(1)} copy-done((f32[3,22,24,128]{3,2,1,0:T(8,128)S(1)}, f32[3,22,24,128]{3,2,1,0:T(8,128)}, u32[]{:S(2)}) %copy-start.3) | copy-done | bytes 811032
  50.9 3.2 %shard_map.72 = (f32[32,4,128]{2,1,0:T(4,128)}, f32[3,22,24,128]{3,2,1,0:T(8,128)S(1)}, f32[3,22,24,128]{3,2,1,0:T(8,128)S(1)}, f32[1,128]{1,0:T(1,128)S(1)}) custom-call(f32[16,4,128]{2,1,0:T(4,128)S(1)} %all-to-all-done.1.recv_ref, f32[3,16,16,128]{3,2,1,0:T(8,128)S(1)} %copy-done.1, f32[22,24,128]{2,1,0:T(8,128)S(1)} %get-tuple-element.30.k_ref, ...), custom_call_target="tpu_custom_call" | custom-call | tf_op jit(solution)/shard_map/pallas_call | solution.py:26
  54.1 7.5 %all-to-all-start.2 = ((f32[32,4,128]{2,1,0:T(4,128)}), f32[32,4,128]{2,1,0:T(4,128)S(1)}, u32[]{:S(2)}, u32[]{:S(2)}) async-start(f32[32,4,128]{2,1,0:T(4,128)} %get-tuple-element.34), calls=%async_computation.2 | async-start | bytes 131072 | tf_op jit(solution)/shard_map/all_to_all | solution.py:509
  61.6 2.0 %shard_map.74.pair_ref = f32[3,128]{1,0:T(4,128)S(1)} custom-call(f32[22,24,128]{2,1,0:T(8,128)S(1)} %get-tuple-element.30.k_ref, f32[22,24,128]{2,1,0:T(8,128)S(1)} %get-tuple-element.31.label_ref, f32[88,384]{1,0:T(8,128)S(1)} %copy-done.8), custom_call_target="tpu_custom_call" | custom-call | flops 3000000 | bytes 3000000 | tf_op jit(solution)/shard_map/pallas_call | solution.py:26
  63.6 1.8 %shard_map.73.own_ref = f32[1,128]{1,0:T(1,128)S(1)} custom-call(f32[22,24,128]{2,1,0:T(8,128)S(1)} %get-tuple-element.30.k_ref, f32[22,24,128]{2,1,0:T(8,128)S(1)} %get-tuple-element.31.label_ref, f32[22,24,128]{2,1,0:T(8,128)S(1)} %get-tuple-element.35.inv_ref, f32[3,22,24,128]{3,2,1,0:T(8,128)S(1)} %get-tuple-element.36.w_ref, ...), custom_call_target="tpu_custom_call" | custom-call | flops 3000000 | bytes 3000000 | tf_op jit(solution)/shard_map/pallas_call | solution.py:26
  65.4 5.0 %all-to-all-done.2.recv_ref = f32[32,4,128]{2,1,0:T(4,128)S(1)} async-done(((f32[32,4,128]{2,1,0:T(4,128)}), f32[32,4,128]{2,1,0:T(4,128)S(1)}, u32[]{:S(2)}, u32[]{:S(2)}) %all-to-all-start.2) | async-done | bytes 65568 | tf_op jit(solution)/shard_map/all_to_all | solution.py:509
  70.5 11.8 %all_to_all.25.recv_ref = f32[16,8,128]{2,1,0:T(8,128)S(1)} all-to-all(f32[16,8,128]{2,1,0:T(8,128)S(1)} %shard_map.75), channel_id=1, replica_groups=mesh['x'=4,'z'=8,'c'=2,'y'=8] {'c','y'}, dimensions={0} | all-to-all | bytes 131072 | tf_op jit(solution)/shard_map/all_to_all | solution.py:509
  82.3 1.1 %shard_map.76 = f32[32,1,128]{2,1,0:T(1,128)} custom-call(f32[16,8,128]{2,1,0:T(8,128)S(1)} %all_to_all.25.recv_ref), custom_call_target="tpu_custom_call" | custom-call | tf_op jit(solution)/shard_map/pallas_call | solution.py:26
  83.4 4.5 %all-to-all-start.4 = ((f32[32,1,128]{2,1,0:T(1,128)}), f32[32,1,128]{2,1,0:T(1,128)}, u32[]{:S(2)}, u32[]{:S(2)}) async-start(f32[32,1,128]{2,1,0:T(1,128)} %shard_map.76), calls=%async_computation.4 | async-start | bytes 32768 | tf_op jit(solution)/shard_map/all_to_all | solution.py:509
  87.9 2.0 %shard_map.77 = (f32[1,128]{1,0:T(1,128)S(1)}, f32[3,18,24,128]{3,2,1,0:T(8,128)S(1)}, f32[3,16,16,128]{3,2,1,0:T(8,128)S(1)}) custom-call(f32[16,8,128]{2,1,0:T(8,128)S(1)} %all_to_all.25.recv_ref, f32[22,24,128]{2,1,0:T(8,128)S(1)} %get-tuple-element.30.k_ref, f32[22,24,128]{2,1,0:T(8,128)S(1)} %get-tuple-element.31.label_ref, ...), custom_call_target="tpu_custom_call" | custom-call | flops 3000000 | bytes 3000000 | tf_op jit(solution)/shard_map/pallas_call | solution.py:26
  91.3 5.0 %all-to-all-done.4.recv_ref = f32[32,1,128]{2,1,0:T(1,128)} async-done(((f32[32,1,128]{2,1,0:T(1,128)}), f32[32,1,128]{2,1,0:T(1,128)}, u32[]{:S(2)}, u32[]{:S(2)}) %all-to-all-start.4) | async-done | bytes 16416 | tf_op jit(solution)/shard_map/all_to_all | solution.py:509
  97.0 1.0 copy-done.6
  98.0 2.7 %shard_map.78 = (f32[3,16,16,128]{3,2,1,0:T(8,128)}, f32[3,16,16,128]{3,2,1,0:T(8,128)}) custom-call(f32[32,1,128]{2,1,0:T(1,128)} %all-to-all-done.4.recv_ref, f32[1,128]{1,0:T(1,128)S(1)} %copy-done.10, f32[3,16,16,128]{3,2,1,0:T(8,128)S(1)} %copy-done.1, f32[3,22,24,128]{3,2,1,0:T(8,128)S(1)} %get-tuple-element.38.z_ref, ...), custom_call_target="tpu_custom_call" | custom-call | tf_op jit(solution)/shard_map/pallas_call | solution.py:26
  (26 shorter events, 3.7 us)
Async XLA Ops:
  2.9 18.4 %copy-start.4 = (f32[16,16,128]{2,1,0:T(8,128)S(1)}, f32[16,16,128]{2,1,0:T(8,128)}, u32[]{:S(2)}) copy-start(f32[16,16,128]{2,1,0:T(8,128)} %get-tuple-element.25.label_ref.label_own_ref) | copy-start | bytes 393220
  2.9 18.4 %collective-permute-start = (f32[3,16,4,128]{3,2,1,0:T(4,128)S(1)}, f32[3,16,4,128]{3,2,1,0:T(4,128)S(1)}, u32[]{:S(2)}, u32[]{:S(2)}) collective-permute-start(f32[3,16,4,128]{3,2,1,0:T(4,128)S(1)} %get-tuple-element.26), channel_id=1, source_target_pairs={{0,1},{1,2},{2,3},{3,4},{4,5},{5,6},{6,7},{8,9},{9,10},{10,11},{11... | collective-permute-start | bytes 294920 | tf_op jit(solution)/shard_map/ppermute | solution.py:515
  7.1 14.2 %collective-permute-start.1 = (f32[3,16,4,128]{3,2,1,0:T(4,128)S(1)}, f32[3,16,4,128]{3,2,1,0:T(4,128)S(1)}, u32[]{:S(2)}, u32[]{:S(2)}) collective-permute-start(f32[3,16,4,128]{3,2,1,0:T(4,128)S(1)} %get-tuple-element.27), channel_id=1, source_target_pairs={{1,0},{2,1},{3,2},{4,3},{5,4},{6,5},{7,6},{9,8},{10,9},{11,10},{12... | collective-permute-start | bytes 294920 | tf_op jit(solution)/shard_map/ppermute | solution.py:515
  8.4 21.8 %all-to-all-start = ((f32[32,4,128]{2,1,0:T(4,128)}), f32[32,4,128]{2,1,0:T(4,128)S(1)}, u32[]{:S(2)}, u32[]{:S(2)}) async-start(f32[32,4,128]{2,1,0:T(4,128)} %get-tuple-element.22), calls=%async_computation | async-start | bytes 131072 | tf_op jit(solution)/shard_map/all_to_all | solution.py:509
  21.4 1.0 copy-start
  22.4 20.4 %copy-start.1 = (f32[3,16,16,128]{3,2,1,0:T(8,128)S(1)}, f32[3,16,16,128]{3,2,1,0:T(8,128)}, u32[]{:S(2)}) copy-start(f32[3,16,16,128]{3,2,1,0:T(8,128)} %get-tuple-element.23.r_ref) | copy-start | bytes 1179652
  22.4 20.3 %collective-permute-start.2 = (f32[232,128]{1,0:T(8,128)S(1)}, f32[232,128]{1,0:T(8,128)S(1)}, u32[]{:S(2)}, u32[]{:S(2)}) collective-permute-start(f32[232,128]{1,0:T(8,128)S(1)} %get-tuple-element.28), channel_id=1, source_target_pairs={{0,8},{8,16},{16,24},{24,32},{32,40},{40,48},{48,56},{56,64},{64,7... | collective-permute-start | bytes 356360 | tf_op jit(solution)/shard_map/ppermute | solution.py:515
  27.1 15.7 %collective-permute-start.3 = (f32[232,128]{1,0:T(8,128)S(1)}, f32[232,128]{1,0:T(8,128)S(1)}, u32[]{:S(2)}, u32[]{:S(2)}) collective-permute-start(f32[232,128]{1,0:T(8,128)S(1)} %get-tuple-element.29), channel_id=1, source_target_pairs={{8,0},{16,8},{24,16},{32,24},{40,32},{48,40},{56,48},{64,56},{72,6... | collective-permute-start | bytes 356360 | tf_op jit(solution)/shard_map/ppermute | solution.py:515
  30.9 18.8 %all-to-all-start.1 = ((f32[16,4,128]{2,1,0:T(4,128)}), f32[16,4,128]{2,1,0:T(4,128)S(1)}, u32[]{:S(2)}, u32[]{:S(2)}) async-start(f32[16,4,128]{2,1,0:T(4,128)} %shard_map.69), calls=%async_computation.1 | async-start | bytes 65536 | tf_op jit(solution)/shard_map/all_to_all | solution.py:509
  42.7 7.0 %copy-start.7 = (f32[12,6144]{1,0:T(8,128)S(1)}, f32[12,6144]{1,0:T(8,128)}, u32[]{:S(2)}) copy-start(f32[12,6144]{1,0:T(8,128)} %get-tuple-element.33.coarse_ref) | copy-start | bytes 884740
  43.8 0.9 copy-start.2
  49.7 1.1 %copy-start.3 = (f32[3,22,24,128]{3,2,1,0:T(8,128)S(1)}, f32[3,22,24,128]{3,2,1,0:T(8,128)}, u32[]{:S(2)}) copy-start(f32[3,22,24,128]{3,2,1,0:T(8,128)} %copy-done.2) | copy-start | bytes 2433028
  50.9 10.7 %copy-start.8 = (f32[88,384]{1,0:T(8,128)S(1)}, f32[88,384]{1,0:T(8,128)}, u32[]{:S(2)}) copy-start(f32[88,384]{1,0:T(8,128)} %constant.2.clone.select_ref) | copy-start | bytes 405508
  54.1 16.3 %all-to-all-start.2 = ((f32[32,4,128]{2,1,0:T(4,128)}), f32[32,4,128]{2,1,0:T(4,128)S(1)}, u32[]{:S(2)}, u32[]{:S(2)}) async-start(f32[32,4,128]{2,1,0:T(4,128)} %get-tuple-element.34), calls=%async_computation.2 | async-start | bytes 131072 | tf_op jit(solution)/shard_map/all_to_all | solution.py:509
  83.4 12.9 %all-to-all-start.4 = ((f32[32,1,128]{2,1,0:T(1,128)}), f32[32,1,128]{2,1,0:T(1,128)}, u32[]{:S(2)}, u32[]{:S(2)}) async-start(f32[32,1,128]{2,1,0:T(1,128)} %shard_map.76), calls=%async_computation.4 | async-start | bytes 32768 | tf_op jit(solution)/shard_map/all_to_all | solution.py:509
  90.0 0.7 copy-start.5
  90.7 0.6 copy-start.9
  96.3 0.7 copy-start.10
  97.0 1.0 copy-start.6

commit v3 on v2

--- a/solution.py
+++ b/solution.py
@@ -22,13 +22,14 @@
     return jax.ShapeDtypeStruct(dims, F32)
 
 
-def call(kernel, outs, ins, scratch=(), space=VMEM, cost=0, limit=24):
+def call(kernel, outs, ins, scratch=(), space=VMEM, cost=0, limit=24, alias=None):
     return pl.pallas_call(
         kernel,
         out_shape=outs,
         in_specs=[space] * len(ins),
         out_specs=jax.tree.map(lambda _: VMEM, outs),
         scratch_shapes=list(scratch),
+        input_output_aliases=alias or {},
         cost_estimate=pl.CostEstimate(flops=cost, bytes_accessed=cost, transcendentals=0) if cost else None,
         compiler_params=pltpu.CompilerParams(vmem_limit_bytes=int(limit * 1024 * 1024)),
     )(*ins)
@@ -275,7 +276,7 @@
             faces, diagonal, here, [z_ref[c, x - 1] for c in range(3)], fields, [z_ref[c, x + 1] for c in range(3)]
         )
         for c in range(3):
-            w_ref[c, x] = w[c]
+            w_ref[c, x - 2] = w[c]
         return fields, w
 
     image(2)
@@ -373,7 +374,7 @@
     def first_step(x, carry):
         inv = inv_ref[x]
         for c in range(3):
-            g_ref[c, x - 2] = w_ref[c, x] * inv
+            g_ref[c, x - 2] = w_ref[c, x - 2] * inv
         return carry
 
     lax.fori_loop(2, 20, first_step, 0, unroll=2)
@@ -389,7 +390,7 @@
         wg, gg = carry[12], carry[13]
         for c in range(3):
             g = fields[c][0:16]
-            wg = wg + w_ref[c, x + 2, 0:16] * g
+            wg = wg + w_ref[c, x, 0:16] * g
             gg = gg + own[c] * g
         return (*add_regions(carry[:12], label_ref[x + 2, 0:16], own), wg, gg)
 
@@ -447,7 +448,7 @@
         out_ref[n] = row
 
 
-def third_kernel(recv_ref, k_ref, label_ref, inv_ref, z_ref, w_ref, scal_ref, znew_ref, image_ref, map_ref):
+def third_kernel(recv_ref, k_ref, label_ref, inv_ref, z_ref, w_ref, scal_ref, own_ref, image_ref, znew_ref, map_ref):
     q = jnp.sum(recv_ref[:, 0:4, :], axis=0)
     near = jnp.where(lax.axis_index("c") == 0, q[0:3], q[1:4])
     spread_maps(pltpu.roll(near, lax.rem(140 - 12 * lax.axis_index("y"), 128), axis=1), map_ref)
@@ -459,7 +460,7 @@
         def body(x, carry):
             inv, label = inv_ref[x], label_ref[x]
             for c in range(3):
-                y = w_ref[c, x] * inv + spread(label, map_ref, s, c)
+                y = w_ref[c, x - 2] * inv + spread(label, map_ref, s, c)
                 znew_ref[c, x - 2] = z_ref[c, x] - alpha * y
             return carry
 
@@ -477,6 +478,7 @@
             faces, diagonal, here, [znew_ref[c, x - 1] for c in range(3)], fields, [znew_ref[c, x + 1] for c in range(3)]
         )
         for c in range(3):
+            own_ref[c, x - 1] = fields[c][0:16]
             image_ref[c, x - 1] = image[c][0:16]
         return carry
 
@@ -498,8 +500,8 @@
 
     def step(x, carry):
         for c in range(3):
-            x_ref[c, x] = first * z_ref[c, x + 3, 0:16] + second * znew_ref[c, x + 1, 0:16]
-            res_ref[c, x] = r_ref[c, x] - first * w_ref[c, x + 3, 0:16] - second * image_ref[c, x]
+            x_ref[c, x] = first * z_ref[c, x + 3, 0:16] + second * znew_ref[c, x]
+            res_ref[c, x] = r_ref[c, x] - first * w_ref[c, x + 1, 0:16] - second * image_ref[c, x]
         return carry
 
     lax.fori_loop(0, 16, step, 0, unroll=2)
@@ -528,7 +530,7 @@
             shape(*field),
             shape(12, 6144),
         ),
-        (right, occ, reg, coarse),
+        tuple(pltpu.with_memory_space_constraint(a, pltpu.HBM) for a in (right, occ, reg, coarse)),
         (
             pltpu.VMEM(field, jnp.int32),
             pltpu.VMEM(field, jnp.int32),
@@ -536,7 +538,7 @@
             pltpu.SemaphoreType.DMA((4,)),
         ),
         space=pl.BlockSpec(memory_space=pltpu.HBM),
-        limit=53.5,
+        limit=24,
     )
     before = shifted(hi, "y", 1)
     after = shifted(lo, "y", -1)
@@ -559,9 +561,10 @@
     )
     send, z, w, own = call(
         second_kernel,
-        (shape(NROWS, 4, 128), shape(3, 22, *plane), shape(3, 22, *plane), shape(1, 128)),
+        (shape(NROWS, 4, 128), shape(3, 22, *plane), shape(3, 18, *plane), shape(1, 128)),
         (got, r, k, label, f, coarse),
         (pltpu.VMEM((3, 12, *plane), F32), *FOLD_SCRATCH),
+        alias={4: 1},
     )
     got = exchange(send, ROWS)
     own = call(
@@ -576,16 +579,16 @@
     send = call(group_kernel, shape(NROWS, 1, 128), (got,))
     scal, znew, image = call(
         third_kernel,
-        (shape(1, 128), shape(3, 18, *plane), shape(3, *field)),
+        (shape(1, 128), shape(3, *field), shape(3, *field)),
         (got, k, label, inv, z, w),
-        (pltpu.VMEM((3, 12, *plane), F32),),
+        (pltpu.VMEM((3, 18, *plane), F32), pltpu.VMEM((3, 12, *plane), F32)),
         cost=3000000,
     )
     got = exchange(send, ROWS)
     return call(
         last_kernel,
         (shape(3, *field), shape(3, *field)),
-        (got, scal, r, z, w, znew, image),
+        (got, scal, right, z, w, znew, image),
     )
 
 

time: 101 us -> 95.8 us (0.949)
  local copies, waits for them, and re-layouts: 6.05 us -> 0.01 us
  waiting for transfers between devices: 16.3 us -> 19.9 us
  starting transfers between devices: 48.7 us -> 46.6 us
    unnamed x22 -> x4, local copies, waits for them, and re-layouts: 6.05 us -> 0.01 us
    all_to_all x4, waiting for transfers between devices: 16.3 us -> 19.9 us  [exchange(): return lax.all_to_all(array, axes, 0, 0, tiled=True)]
    all_to_all x4, starting transfers between devices: 36.7 us -> 34.8 us  [exchange(): return lax.all_to_all(array, axes, 0, 0, tiled=True)]
where the time goes in v3:
time: 95.8 us; the launch traced here: 95.4 us
  starting transfers between devices  46.6 us (49%)
  waiting for transfers between devices  19.9 us (21%)
  Pallas kernels  16.3 us (17%)
  blocking collectives  11.8 us (12%)
    all_to_all x4, starting transfers between devices, exchange(): return lax.all_to_all(array, axes, 0, 0, tiled=True)  34.8 us
    all_to_all x4, waiting for transfers between devices, exchange(): return lax.all_to_all(array, axes, 0, 0, tiled=True)  19.9 us
    pallas_call x11, Pallas kernels, call(): pl.pallas_call(kernel, out_shape=outs, in_specs=[space] * len(ins), out_s...  16.3 us
    all_to_all x1, blocking collectives, exchange(): return lax.all_to_all(array, axes, 0, 0, tiled=True)  11.8 us
    ppermute x4, starting transfers between devices, shifted(): return lax.ppermute(array, axis, pairs)  11.8 us
  transfers between devices with their start and end apart: 8, of which 4 were waited for; matrix products, arithmetic and copies ran while one was open for 0% of the time, Pallas kernels for 8%

profile of v3, /device:TPU:1, one launch (start us, length us, event | category | flops | bytes accessed | tf_op | source)
XLA Modules:
  0.0 95.4 jit_solution(11104057283340805311)
XLA Ops:
  0.6 2.3 %shard_map.68 = (f32[32,4,128]{2,1,0:T(4,128)}, f32[3,16,4,128]{3,2,1,0:T(4,128)S(1)}, f32[3,16,4,128]{3,2,1,0:T(4,128)S(1)}, f32[3,16,16,128]{3,2,1,0:T(8,128)S...) custom-call(f32[3,16,16,128]{3,2,1,0:T(8,128)} %r_ref.1, ...), custom_call_target="tpu_custom_call" | custom-call | tf_op jit(solution)/shard_map/pallas_call | solution.py:26
  2.9 4.0 %collective-permute-start = (f32[3,16,4,128]{3,2,1,0:T(4,128)S(1)}, f32[3,16,4,128]{3,2,1,0:T(4,128)S(1)}, u32[]{:S(2)}, u32[]{:S(2)}) collective-permute-start(f32[3,16,4,128]{3,2,1,0:T(4,128)S(1)} %get-tuple-element.26), channel_id=1, source_target_pairs={{0,1},{1,2},{2,3},{3,4},{4,5},{5,6},{6,7},{8,9},{9,10},{10,11},{11... | collective-permute-start | bytes 294920 | tf_op jit(solution)/shard_map/ppermute | solution.py:517
  7.0 1.3 %collective-permute-start.1 = (f32[3,16,4,128]{3,2,1,0:T(4,128)S(1)}, f32[3,16,4,128]{3,2,1,0:T(4,128)S(1)}, u32[]{:S(2)}, u32[]{:S(2)}) collective-permute-start(f32[3,16,4,128]{3,2,1,0:T(4,128)S(1)} %get-tuple-element.27), channel_id=1, source_target_pairs={{1,0},{2,1},{3,2},{4,3},{5,4},{6,5},{7,6},{9,8},{10,9},{11,10},{12... | collective-permute-start | bytes 294920 | tf_op jit(solution)/shard_map/ppermute | solution.py:517
  8.3 12.9 %all-to-all-start = ((f32[32,4,128]{2,1,0:T(4,128)}), f32[32,4,128]{2,1,0:T(4,128)S(1)}, u32[]{:S(2)}, u32[]{:S(2)}) async-start(f32[32,4,128]{2,1,0:T(4,128)} %get-tuple-element.22), calls=%async_computation | async-start | bytes 131072 | tf_op jit(solution)/shard_map/all_to_all | solution.py:511
  21.2 0.0 collective-permute-done.lo_ref
  21.2 4.5 %collective-permute-start.2 = (f32[232,128]{1,0:T(8,128)S(1)}, f32[232,128]{1,0:T(8,128)S(1)}, u32[]{:S(2)}, u32[]{:S(2)}) collective-permute-start(f32[232,128]{1,0:T(8,128)S(1)} %get-tuple-element.28), channel_id=1, source_target_pairs={{0,8},{8,16},{16,24},{24,32},{32,40},{40,48},{48,56},{56,64},{64,7... | collective-permute-start | bytes 356360 | tf_op jit(solution)/shard_map/ppermute | solution.py:517
  25.8 1.9 %collective-permute-start.3 = (f32[232,128]{1,0:T(8,128)S(1)}, f32[232,128]{1,0:T(8,128)S(1)}, u32[]{:S(2)}, u32[]{:S(2)}) collective-permute-start(f32[232,128]{1,0:T(8,128)S(1)} %get-tuple-element.29), channel_id=1, source_target_pairs={{8,0},{16,8},{24,16},{32,24},{40,32},{48,40},{56,48},{64,56},{72,6... | collective-permute-start | bytes 356360 | tf_op jit(solution)/shard_map/ppermute | solution.py:517
  27.7 2.3 %all-to-all-done.recv_ref = f32[32,4,128]{2,1,0:T(4,128)S(1)} async-done(((f32[32,4,128]{2,1,0:T(4,128)}), f32[32,4,128]{2,1,0:T(4,128)S(1)}, u32[]{:S(2)}, u32[]{:S(2)}) %all-to-all-start) | async-done | bytes 65568 | tf_op jit(solution)/shard_map/all_to_all | solution.py:511
  30.0 0.7 shard_map.69
  30.8 11.8 %all-to-all-start.1 = ((f32[16,4,128]{2,1,0:T(4,128)}), f32[16,4,128]{2,1,0:T(4,128)S(1)}, u32[]{:S(2)}, u32[]{:S(2)}) async-start(f32[16,4,128]{2,1,0:T(4,128)} %shard_map.69), calls=%async_computation.1 | async-start | bytes 65536 | tf_op jit(solution)/shard_map/all_to_all | solution.py:511
  42.6 1.1 %shard_map.71 = (f32[22,24,128]{2,1,0:T(8,128)S(1)}, f32[22,24,128]{2,1,0:T(8,128)S(1)}, f32[22,24,128]{2,1,0:T(8,128)S(1)}, f32[3,22,24,128]{3,2,1,0:T(8,128)S(1)}) custom-call(f32[3,16,16,128]{3,2,1,0:T(8,128)S(1)} %get-tuple-element.23.r_ref, f32[16,16,128]{2,1,0:T(8,128)S(1)} %get-tuple-element.24.k_ref.k_own_ref, ...), custom_call_target="tpu_custom_call" | custom-call | flops 3000000 | bytes 3000000 | tf_op jit(solution)/shard_map/pallas_call | solution.py:26
  43.6 6.0 %all-to-all-done.1.recv_ref = f32[16,4,128]{2,1,0:T(4,128)S(1)} async-done(((f32[16,4,128]{2,1,0:T(4,128)}), f32[16,4,128]{2,1,0:T(4,128)S(1)}, u32[]{:S(2)}, u32[]{:S(2)}) %all-to-all-start.1) | async-done | bytes 32800 | tf_op jit(solution)/shard_map/all_to_all | solution.py:511
  49.6 3.3 %shard_map.72 = (f32[32,4,128]{2,1,0:T(4,128)}, f32[3,22,24,128]{3,2,1,0:T(8,128)S(1)}, f32[3,18,24,128]{3,2,1,0:T(8,128)S(1)}, f32[1,128]{1,0:T(1,128)S(1)}) custom-call(f32[16,4,128]{2,1,0:T(4,128)S(1)} %all-to-all-done.1.recv_ref, f32[3,16,16,128]{3,2,1,0:T(8,128)S(1)} %get-tuple-element.23.r_ref, ...), custom_call_target="tpu_custom_call", output_to_operand_aliasing={{1}: (4, {})} | custom-call | tf_op jit(solution)/shard_map/pallas_call | solution.py:26
  52.9 6.3 %all-to-all-start.2 = ((f32[32,4,128]{2,1,0:T(4,128)}), f32[32,4,128]{2,1,0:T(4,128)S(1)}, u32[]{:S(2)}, u32[]{:S(2)}) async-start(f32[32,4,128]{2,1,0:T(4,128)} %get-tuple-element.34), calls=%async_computation.2 | async-start | bytes 131072 | tf_op jit(solution)/shard_map/all_to_all | solution.py:511
  59.2 2.0 %shard_map.74.pair_ref = f32[3,128]{1,0:T(4,128)S(1)} custom-call(f32[22,24,128]{2,1,0:T(8,128)S(1)} %get-tuple-element.30.k_ref, f32[22,24,128]{2,1,0:T(8,128)S(1)} %get-tuple-element.31.label_ref, f32[88,384]{1,0:T(8,128)S(1)} %copy-done.1), custom_call_target="tpu_custom_call" | custom-call | flops 3000000 | bytes 3000000 | tf_op jit(solution)/shard_map/pallas_call | solution.py:26
  61.2 1.8 %shard_map.73.own_ref = f32[1,128]{1,0:T(1,128)S(1)} custom-call(f32[22,24,128]{2,1,0:T(8,128)S(1)} %get-tuple-element.30.k_ref, f32[22,24,128]{2,1,0:T(8,128)S(1)} %get-tuple-element.31.label_ref, f32[22,24,128]{2,1,0:T(8,128)S(1)} %get-tuple-element.35.inv_ref, f32[3,18,24,128]{3,2,1,0:T(8,128)S(1)} %get-tuple-element.36.w_ref, ...), custom_call_target="tpu_custom_call" | custom-call | flops 3000000 | bytes 3000000 | tf_op jit(solution)/shard_map/pallas_call | solution.py:26
  63.0 5.0 %all-to-all-done.2.recv_ref = f32[32,4,128]{2,1,0:T(4,128)S(1)} async-done(((f32[32,4,128]{2,1,0:T(4,128)}), f32[32,4,128]{2,1,0:T(4,128)S(1)}, u32[]{:S(2)}, u32[]{:S(2)}) %all-to-all-start.2) | async-done | bytes 65568 | tf_op jit(solution)/shard_map/all_to_all | solution.py:511
  68.1 11.8 %all_to_all.25.recv_ref = f32[16,8,128]{2,1,0:T(8,128)S(1)} all-to-all(f32[16,8,128]{2,1,0:T(8,128)S(1)} %shard_map.75), channel_id=1, replica_groups=mesh['x'=4,'z'=8,'c'=2,'y'=8] {'c','y'}, dimensions={0} | all-to-all | bytes 131072 | tf_op jit(solution)/shard_map/all_to_all | solution.py:511
  79.9 1.1 %shard_map.76 = f32[32,1,128]{2,1,0:T(1,128)} custom-call(f32[16,8,128]{2,1,0:T(8,128)S(1)} %all_to_all.25.recv_ref), custom_call_target="tpu_custom_call" | custom-call | tf_op jit(solution)/shard_map/pallas_call | solution.py:26
  81.0 3.8 %all-to-all-start.4 = ((f32[32,1,128]{2,1,0:T(1,128)}), f32[32,1,128]{2,1,0:T(1,128)S(1)}, u32[]{:S(2)}, u32[]{:S(2)}) async-start(f32[32,1,128]{2,1,0:T(1,128)} %shard_map.76), calls=%async_computation.4 | async-start | bytes 32768 | tf_op jit(solution)/shard_map/all_to_all | solution.py:511
  84.8 0.0 copy-start
  84.9 2.0 %shard_map.77 = (f32[1,128]{1,0:T(1,128)S(1)}, f32[3,16,16,128]{3,2,1,0:T(8,128)S(1)}, f32[3,16,16,128]{3,2,1,0:T(8,128)S(1)}) custom-call(f32[16,8,128]{2,1,0:T(8,128)S(1)} %all_to_all.25.recv_ref, f32[22,24,128]{2,1,0:T(8,128)S(1)} %get-tuple-element.30.k_ref, f32[22,24,128]{2,1,0:T(8,128)S(1)} %get-tuple-element.31.label_ref, ...), custom_call_target="tpu_custom_call" | custom-call | flops 3000000 | bytes 3000000 | tf_op jit(solution)/shard_map/pallas_call | solution.py:26
  86.9 6.5 %all-to-all-done.4.recv_ref = f32[32,1,128]{2,1,0:T(1,128)S(1)} async-done(((f32[32,1,128]{2,1,0:T(1,128)}), f32[32,1,128]{2,1,0:T(1,128)S(1)}, u32[]{:S(2)}, u32[]{:S(2)}) %all-to-all-start.4) | async-done | bytes 16416 | tf_op jit(solution)/shard_map/all_to_all | solution.py:511
  93.4 1.9 %shard_map.78 = (f32[3,16,16,128]{3,2,1,0:T(8,128)}, f32[3,16,16,128]{3,2,1,0:T(8,128)}) custom-call(f32[32,1,128]{2,1,0:T(1,128)S(1)} %all-to-all-done.4.recv_ref, f32[1,128]{1,0:T(1,128)S(1)} %get-tuple-element.39.scal_ref, f32[3,16,16,128]{3,2,1,0:T(8,128)S(1)} %copy-done, f32[3,22,24,128]{3,2,1,0:T(8,128)S(1)} %get-tuple-element.38.z_ref, ...), custom_call_target="tpu_custom_call" | custom-call | tf_op jit(solution)/shard_map/pallas_call | solution.py:26
  (8 shorter events, 0.1 us)
Async XLA Ops:
  2.9 18.2 %collective-permute-start = (f32[3,16,4,128]{3,2,1,0:T(4,128)S(1)}, f32[3,16,4,128]{3,2,1,0:T(4,128)S(1)}, u32[]{:S(2)}, u32[]{:S(2)}) collective-permute-start(f32[3,16,4,128]{3,2,1,0:T(4,128)S(1)} %get-tuple-element.26), channel_id=1, source_target_pairs={{0,1},{1,2},{2,3},{3,4},{4,5},{5,6},{6,7},{8,9},{9,10},{10,11},{11... | collective-permute-start | bytes 294920 | tf_op jit(solution)/shard_map/ppermute | solution.py:517
  7.0 14.2 %collective-permute-start.1 = (f32[3,16,4,128]{3,2,1,0:T(4,128)S(1)}, f32[3,16,4,128]{3,2,1,0:T(4,128)S(1)}, u32[]{:S(2)}, u32[]{:S(2)}) collective-permute-start(f32[3,16,4,128]{3,2,1,0:T(4,128)S(1)} %get-tuple-element.27), channel_id=1, source_target_pairs={{1,0},{2,1},{3,2},{4,3},{5,4},{6,5},{7,6},{9,8},{10,9},{11,10},{12... | collective-permute-start | bytes 294920 | tf_op jit(solution)/shard_map/ppermute | solution.py:517
  8.3 21.8 %all-to-all-start = ((f32[32,4,128]{2,1,0:T(4,128)}), f32[32,4,128]{2,1,0:T(4,128)S(1)}, u32[]{:S(2)}, u32[]{:S(2)}) async-start(f32[32,4,128]{2,1,0:T(4,128)} %get-tuple-element.22), calls=%async_computation | async-start | bytes 131072 | tf_op jit(solution)/shard_map/all_to_all | solution.py:511
  21.2 21.3 %collective-permute-start.2 = (f32[232,128]{1,0:T(8,128)S(1)}, f32[232,128]{1,0:T(8,128)S(1)}, u32[]{:S(2)}, u32[]{:S(2)}) collective-permute-start(f32[232,128]{1,0:T(8,128)S(1)} %get-tuple-element.28), channel_id=1, source_target_pairs={{0,8},{8,16},{16,24},{24,32},{32,40},{40,48},{48,56},{56,64},{64,7... | collective-permute-start | bytes 356360 | tf_op jit(solution)/shard_map/ppermute | solution.py:517
  25.8 16.8 %collective-permute-start.3 = (f32[232,128]{1,0:T(8,128)S(1)}, f32[232,128]{1,0:T(8,128)S(1)}, u32[]{:S(2)}, u32[]{:S(2)}) collective-permute-start(f32[232,128]{1,0:T(8,128)S(1)} %get-tuple-element.29), channel_id=1, source_target_pairs={{8,0},{16,8},{24,16},{32,24},{40,32},{48,40},{56,48},{64,56},{72,6... | collective-permute-start | bytes 356360 | tf_op jit(solution)/shard_map/ppermute | solution.py:517
  30.8 18.8 %all-to-all-start.1 = ((f32[16,4,128]{2,1,0:T(4,128)}), f32[16,4,128]{2,1,0:T(4,128)S(1)}, u32[]{:S(2)}, u32[]{:S(2)}) async-start(f32[16,4,128]{2,1,0:T(4,128)} %shard_map.69), calls=%async_computation.1 | async-start | bytes 65536 | tf_op jit(solution)/shard_map/all_to_all | solution.py:511
  49.6 9.6 %copy-start.1 = (f32[88,384]{1,0:T(8,128)S(1)}, f32[88,384]{1,0:T(8,128)}, u32[]{:S(2)}) copy-start(f32[88,384]{1,0:T(8,128)} %constant.2.clone.select_ref) | copy-start | bytes 405508
  52.9 15.2 %all-to-all-start.2 = ((f32[32,4,128]{2,1,0:T(4,128)}), f32[32,4,128]{2,1,0:T(4,128)S(1)}, u32[]{:S(2)}, u32[]{:S(2)}) async-start(f32[32,4,128]{2,1,0:T(4,128)} %get-tuple-element.34), calls=%async_computation.2 | async-start | bytes 131072 | tf_op jit(solution)/shard_map/all_to_all | solution.py:511
  81.0 12.4 %all-to-all-start.4 = ((f32[32,1,128]{2,1,0:T(1,128)}), f32[32,1,128]{2,1,0:T(1,128)S(1)}, u32[]{:S(2)}, u32[]{:S(2)}) async-start(f32[32,1,128]{2,1,0:T(1,128)} %shard_map.76), calls=%async_computation.4 | async-start | bytes 32768 | tf_op jit(solution)/shard_map/all_to_all | solution.py:511
  84.8 8.6 %copy-start = (f32[3,16,16,128]{3,2,1,0:T(8,128)S(1)}, f32[3,16,16,128]{3,2,1,0:T(8,128)}, u32[]{:S(2)}) copy-start(f32[3,16,16,128]{3,2,1,0:T(8,128)} %r_ref.1) | copy-start | bytes 1179652

commit v4 on v3

--- a/solution.py
+++ b/solution.py
@@ -83,9 +83,13 @@
 )
 
 
+def even_column():
+    return lax.rem(lax.axis_index("y"), 2) == 0
+
+
 def first_kernel(
     r_hbm, occ_hbm, reg_hbm, coarse_hbm,
-    out_ref, lo_ref, hi_ref, r_ref, k_ref, label_ref, coarse_ref,
+    out_ref, a_ref, b_ref, r_ref, k_ref, label_ref, coarse_ref,
     occ_ref, reg_ref, acc_ref, u_ref, pad_ref, sems,
 ):
     pairs = ((r_hbm, r_ref), (reg_hbm, reg_ref), (occ_hbm, occ_ref), (coarse_hbm, coarse_ref))
@@ -96,12 +100,12 @@
         copy.wait()
     k_ref[...] = 0.1 + 0.9 * occ_ref[...].astype(F32)
     label_ref[...] = reg_ref[...].astype(F32) + 1.0
-    for ref, deep, flat in ((lo_ref, 0, 0), (hi_ref, 12, 14)):
-        ref[0] = k_ref[:, deep : deep + 4, :]
-        ref[1, :, 0:2] = label_ref[:, flat : flat + 2, :]
-        ref[1, :, 2:4] = r_ref[0, :, flat : flat + 2, :]
-        ref[2, :, 0:2] = r_ref[1, :, flat : flat + 2, :]
-        ref[2, :, 2:4] = r_ref[2, :, flat : flat + 2, :]
+    even = even_column()
+    for ref, last in ((a_ref, even), (b_ref, jnp.logical_not(even))):
+        ref[0] = jnp.where(last, k_ref[:, 12:16, :], k_ref[:, 0:4, :])
+        for i, field in enumerate([label_ref] + [r_ref.at[c] for c in range(3)]):
+            at = 2 * (i % 2)
+            ref[1 + i // 2, :, at : at + 2] = jnp.where(last, field[:, 14:16, :], field[:, 0:2, :])
 
     def step(x, accs):
         return tuple(add_regions(accs, label_ref[x], [r_ref[c, x] for c in range(3)]))
@@ -120,54 +124,64 @@
             out_ref[8 * c + y, 3:4, :] = part[0:1]
 
 
-def tail_rows(lo_ref, hi_ref, i, planes):
+def tail_rows(a_ref, b_ref, i, planes):
+    even = even_column()
     if i == 0:
-        return jnp.concatenate([hi_ref[0, planes], lo_ref[0, planes]], axis=1)
+        one, two = a_ref[0, planes], b_ref[0, planes]
+        return jnp.concatenate([jnp.where(even, one, two), jnp.where(even, two, one)], axis=1)
     block, at = 1 + (i - 1) // 2, 2 * ((i - 1) % 2)
-    above, below = hi_ref[block, planes, at : at + 2], lo_ref[block, planes, at : at + 2]
-    none = jnp.zeros((above.shape[0], 4, 128), F32)
-    return jnp.concatenate([above, none, below], axis=1)
+    one, two = a_ref[block, planes, at : at + 2], b_ref[block, planes, at : at + 2]
+    none = jnp.zeros((one.shape[0], 4, 128), F32)
+    return jnp.concatenate([jnp.where(even, one, two), none, jnp.where(even, two, one)], axis=1)
 
 
 PACK = 72 + 4 * 40
 
 
-def pack_kernel(k_ref, label_ref, r_ref, lo_ref, hi_ref, up_ref, down_ref):
+def pack_kernel(k_ref, label_ref, r_ref, a_ref, b_ref, first_ref, second_ref):
     fields = [label_ref] + [r_ref.at[c] for c in range(3)]
-    for ref, deep, near, next_ in ((up_ref, 13, 15, 14), (down_ref, 0, 0, 1)):
-        tails = tail_rows(lo_ref, hi_ref, 0, pl.ds(deep, 3))
+    core = lax.axis_index("c")
+    for ref, up in ((first_ref, core == 0), (second_ref, core == 1)):
+        deep, near, next_ = jnp.where(up, 13, 0), jnp.where(up, 15, 0), jnp.where(up, 14, 1)
+        tails = tail_rows(a_ref, b_ref, 0, pl.ds(deep, 3))
         for i in range(3):
             ref[24 * i : 24 * i + 16] = k_ref[deep + i]
             ref[24 * i + 16 : 24 * i + 24] = tails[i]
         for i, field in enumerate(fields):
             at = 72 + 40 * i
             ref[at : at + 16] = field[near]
-            ref[at + 16 : at + 24] = tail_rows(lo_ref, hi_ref, 1 + i, pl.ds(near, 1))[0]
+            ref[at + 16 : at + 24] = tail_rows(a_ref, b_ref, 1 + i, pl.ds(near, 1))[0]
             ref[at + 24 : at + 40] = field[next_]
 
 
 def extend_kernel(
-    r_ref, k_own_ref, label_own_ref, lo_ref, hi_ref, below_ref, above_ref, k_ref, label_ref, inv_ref, f_ref
+    r_ref, k_own_ref, label_own_ref, a_ref, b_ref, first_ref, second_ref, k_ref, label_ref, inv_ref, f_ref
 ):
     whole = pl.ds(0, 16)
+    core = lax.axis_index("c")
+
+    def sides(rows):
+        one, two = first_ref[rows], second_ref[rows]
+        return jnp.where(core == 0, two, one), jnp.where(core == 0, one, two)
+
     k_ref[3:19, 0:16] = k_own_ref[...]
     label_ref[3:19, 0:16] = label_own_ref[...]
-    k_ref[3:19, 16:24] = tail_rows(lo_ref, hi_ref, 0, whole)
-    label_ref[3:19, 16:24] = tail_rows(lo_ref, hi_ref, 1, whole)
+    k_ref[3:19, 16:24] = tail_rows(a_ref, b_ref, 0, whole)
+    label_ref[3:19, 16:24] = tail_rows(a_ref, b_ref, 1, whole)
     none = jnp.zeros((8, 128), F32)
     for i in range(3):
-        k_ref[i] = below_ref[24 * i : 24 * i + 24]
-        k_ref[19 + i] = above_ref[24 * i : 24 * i + 24]
+        below, above = sides(slice(24 * i, 24 * i + 24))
+        k_ref[i] = below
+        k_ref[19 + i] = above
     targets = [label_ref] + [f_ref.at[c] for c in range(3)]
     for i, ref in enumerate(targets):
         at = 72 + 40 * i
-        for pack, near, next_ in ((below_ref, 2, 1), (above_ref, 19, 20)):
-            ref[near] = pack[at : at + 24]
-            ref[next_, 0:16] = pack[at + 24 : at + 40]
-            ref[next_, 16:24] = none
+        ref[2], ref[19] = sides(slice(at, at + 24))
+        ref[1, 0:16], ref[20, 0:16] = sides(slice(at + 24, at + 40))
+        ref[1, 16:24] = ref[20, 16:24] = none
     for c in range(3):
         f_ref[c, 3:19, 0:16] = r_ref[c]
-        f_ref[c, 3:19, 16:24] = tail_rows(lo_ref, hi_ref, 2 + c, whole)
+        f_ref[c, 3:19, 16:24] = tail_rows(a_ref, b_ref, 2 + c, whole)
 
     def step(x, carry):
         here = k_ref[x]
@@ -511,15 +525,15 @@
     return lax.all_to_all(array, axes, 0, 0, tiled=True)
 
 
-def shifted(array, axis, step):
+def swapped(array, axis, first):
     count = lax.axis_size(axis)
-    pairs = [(i, i + step) for i in range(count) if 0 <= i + step < count]
-    return lax.ppermute(array, axis, pairs)
+    pairs = [(i, i + 1) for i in range(first, count - 1, 2)]
+    return lax.ppermute(array, axis, pairs + [(b, a) for a, b in pairs])
 
 
 def local(right, occ, reg, coarse):
     field, plane = (16, 16, 128), (24, 128)
-    send, lo, hi, r, k_own, label_own, coarse = call(
+    send, one, two, r, k_own, label_own, coarse = call(
         first_kernel,
         (
             shape(NROWS, 4, 128),
@@ -540,20 +554,20 @@
         space=pl.BlockSpec(memory_space=pltpu.HBM),
         limit=24,
     )
-    before = shifted(hi, "y", 1)
-    after = shifted(lo, "y", -1)
+    one = swapped(one, "y", 0)
+    two = swapped(two, "y", 1)
     got = exchange(send, ROWS)
-    up, down = call(
-        pack_kernel, (shape(PACK, 128), shape(PACK, 128)), (k_own, label_own, r, before, after), cost=1000000
-    )
-    below = shifted(up, WIDE, 1)
-    above = shifted(down, WIDE, -1)
+    first, second = call(
+        pack_kernel, (shape(PACK, 128), shape(PACK, 128)), (k_own, label_own, r, one, two), cost=1000000
+    )
+    first = swapped(first, WIDE, 0)
+    second = swapped(second, WIDE, 1)
     send = call(around_kernel, shape(NCOLS, 4, 128), (got,))
     got = exchange(send, COLS)
     k, label, inv, f = call(
         extend_kernel,
         (shape(22, *plane), shape(22, *plane), shape(22, *plane), shape(3, 22, *plane)),
-        (r, k_own, label_own, before, after, below, above),
+        (r, k_own, label_own, one, two, first, second),
         cost=3000000,
     )
     pair = call(

time: 95.8 us -> 91.6 us (0.956)
  starting transfers between devices: 46.6 us -> 42.4 us
    all_to_all x4, starting transfers between devices: 34.8 us -> 31.2 us  [exchange(): return lax.all_to_all(array, axes, 0, 0, tiled=True)]
where the time goes in v4:
time: 91.6 us; the launch traced here: 91.1 us
  starting transfers between devices  42.4 us (46%)
  waiting for transfers between devices  19.9 us (22%)
  Pallas kernels  16.3 us (18%)
  blocking collectives  11.8 us (13%)
    all_to_all x4, starting transfers between devices, exchange(): return lax.all_to_all(array, axes, 0, 0, tiled=True)  31.2 us
    all_to_all x4, waiting for transfers between devices, exchange(): return lax.all_to_all(array, axes, 0, 0, tiled=True)  19.9 us
    pallas_call x11, Pallas kernels, call(): pl.pallas_call(kernel, out_shape=outs, in_specs=[space] * len(ins), out_s...  16.3 us
    all_to_all x1, blocking collectives, exchange(): return lax.all_to_all(array, axes, 0, 0, tiled=True)  11.8 us
    ppermute x4, starting transfers between devices, swapped(): return lax.ppermute(array, axis, pairs + [(b, a) for a, b in pairs])  11.2 us
  transfers between devices with their start and end apart: 8, of which 4 were waited for; matrix products, arithmetic and copies ran while one was open for 0% of the time, Pallas kernels for 8%

profile of v4, /device:TPU:1, one launch (start us, length us, event | category | flops | bytes accessed | tf_op | source)
XLA Modules:
  0.0 91.1 jit_solution(12172821187700315960)
XLA Ops:
  0.6 2.3 %shard_map.68 = (f32[32,4,128]{2,1,0:T(4,128)}, f32[3,16,4,128]{3,2,1,0:T(4,128)S(1)}, f32[3,16,4,128]{3,2,1,0:T(4,128)S(1)}, f32[3,16,16,128]{3,2,1,0:T(8,128)S...) custom-call(f32[3,16,16,128]{3,2,1,0:T(8,128)} %r_ref.1, ...), custom_call_target="tpu_custom_call" | custom-call | tf_op jit(solution)/shard_map/pallas_call | solution.py:26
  2.9 4.0 %collective-permute-start = (f32[3,16,4,128]{3,2,1,0:T(4,128)S(1)}, f32[3,16,4,128]{3,2,1,0:T(4,128)S(1)}, u32[]{:S(2)}, u32[]{:S(2)}) collective-permute-start(f32[3,16,4,128]{3,2,1,0:T(4,128)S(1)} %get-tuple-element.26), channel_id=1, source_target_pairs={{0,1},{2,3},{4,5},{6,7},{1,0},{3,2},{5,4},{7,6},{8,9},{10,11},{12,... | collective-permute-start | bytes 294920 | tf_op jit(solution)/shard_map/ppermute | solution.py:531
  7.0 0.7 collective-permute-start.1
  7.7 12.9 %all-to-all-start = ((f32[32,4,128]{2,1,0:T(4,128)}), f32[32,4,128]{2,1,0:T(4,128)S(1)}, u32[]{:S(2)}, u32[]{:S(2)}) async-start(f32[32,4,128]{2,1,0:T(4,128)} %get-tuple-element.22), calls=%async_computation | async-start | bytes 131072 | tf_op jit(solution)/shard_map/all_to_all | solution.py:525
  20.6 0.0 collective-permute-done.a_ref
  20.6 3.1 %collective-permute-start.2 = (f32[232,128]{1,0:T(8,128)S(1)}, f32[232,128]{1,0:T(8,128)S(1)}, u32[]{:S(2)}, u32[]{:S(2)}) collective-permute-start(f32[232,128]{1,0:T(8,128)S(1)} %get-tuple-element.28), channel_id=1, source_target_pairs={{0,8},{16,24},{32,40},{48,56},{64,72},{80,88},{96,104},{112,120},{... | collective-permute-start | bytes 356360 | tf_op jit(solution)/shard_map/ppermute | solution.py:531
  23.8 3.3 %collective-permute-start.3 = (f32[232,128]{1,0:T(8,128)S(1)}, f32[232,128]{1,0:T(8,128)S(1)}, u32[]{:S(2)}, u32[]{:S(2)}) collective-permute-start(f32[232,128]{1,0:T(8,128)S(1)} %get-tuple-element.29), channel_id=1, source_target_pairs={{8,16},{24,32},{40,48},{56,64},{72,80},{88,96},{104,112},{120,128}... | collective-permute-start | bytes 356360 | tf_op jit(solution)/shard_map/ppermute | solution.py:531
  27.1 2.3 %all-to-all-done.recv_ref = f32[32,4,128]{2,1,0:T(4,128)S(1)} async-done(((f32[32,4,128]{2,1,0:T(4,128)}), f32[32,4,128]{2,1,0:T(4,128)S(1)}, u32[]{:S(2)}, u32[]{:S(2)}) %all-to-all-start) | async-done | bytes 65568 | tf_op jit(solution)/shard_map/all_to_all | solution.py:525
  29.4 0.7 shard_map.69
  30.1 10.4 %all-to-all-start.1 = ((f32[16,4,128]{2,1,0:T(4,128)}), f32[16,4,128]{2,1,0:T(4,128)S(1)}, u32[]{:S(2)}, u32[]{:S(2)}) async-start(f32[16,4,128]{2,1,0:T(4,128)} %shard_map.69), calls=%async_computation.1 | async-start | bytes 65536 | tf_op jit(solution)/shard_map/all_to_all | solution.py:525
  40.6 1.1 %shard_map.71 = (f32[22,24,128]{2,1,0:T(8,128)S(1)}, f32[22,24,128]{2,1,0:T(8,128)S(1)}, f32[22,24,128]{2,1,0:T(8,128)S(1)}, f32[3,22,24,128]{3,2,1,0:T(8,128)S(1)}) custom-call(f32[3,16,16,128]{3,2,1,0:T(8,128)S(1)} %get-tuple-element.23.r_ref, f32[16,16,128]{2,1,0:T(8,128)S(1)} %get-tuple-element.24.k_ref.k_own_ref, ...), custom_call_target="tpu_custom_call" | custom-call | flops 3000000 | bytes 3000000 | tf_op jit(solution)/shard_map/pallas_call | solution.py:26
  41.6 6.0 %all-to-all-done.1.recv_ref = f32[16,4,128]{2,1,0:T(4,128)S(1)} async-done(((f32[16,4,128]{2,1,0:T(4,128)}), f32[16,4,128]{2,1,0:T(4,128)S(1)}, u32[]{:S(2)}, u32[]{:S(2)}) %all-to-all-start.1) | async-done | bytes 32800 | tf_op jit(solution)/shard_map/all_to_all | solution.py:525
  47.6 3.3 %shard_map.72 = (f32[32,4,128]{2,1,0:T(4,128)}, f32[3,22,24,128]{3,2,1,0:T(8,128)S(1)}, f32[3,18,24,128]{3,2,1,0:T(8,128)S(1)}, f32[1,128]{1,0:T(1,128)S(1)}) custom-call(f32[16,4,128]{2,1,0:T(4,128)S(1)} %all-to-all-done.1.recv_ref, f32[3,16,16,128]{3,2,1,0:T(8,128)S(1)} %get-tuple-element.23.r_ref, ...), custom_call_target="tpu_custom_call", output_to_operand_aliasing={{1}: (4, {})} | custom-call | tf_op jit(solution)/shard_map/pallas_call | solution.py:26
  50.9 4.1 %all-to-all-start.2 = ((f32[32,4,128]{2,1,0:T(4,128)}), f32[32,4,128]{2,1,0:T(4,128)S(1)}, u32[]{:S(2)}, u32[]{:S(2)}) async-start(f32[32,4,128]{2,1,0:T(4,128)} %get-tuple-element.34), calls=%async_computation.2 | async-start | bytes 131072 | tf_op jit(solution)/shard_map/all_to_all | solution.py:525
  55.0 2.0 %shard_map.74.pair_ref = f32[3,128]{1,0:T(4,128)S(1)} custom-call(f32[22,24,128]{2,1,0:T(8,128)S(1)} %get-tuple-element.30.k_ref, f32[22,24,128]{2,1,0:T(8,128)S(1)} %get-tuple-element.31.label_ref, f32[88,384]{1,0:T(8,128)S(1)} %copy-done.1), custom_call_target="tpu_custom_call" | custom-call | flops 3000000 | bytes 3000000 | tf_op jit(solution)/shard_map/pallas_call | solution.py:26
  57.0 1.8 %shard_map.73.own_ref = f32[1,128]{1,0:T(1,128)S(1)} custom-call(f32[22,24,128]{2,1,0:T(8,128)S(1)} %get-tuple-element.30.k_ref, f32[22,24,128]{2,1,0:T(8,128)S(1)} %get-tuple-element.31.label_ref, f32[22,24,128]{2,1,0:T(8,128)S(1)} %get-tuple-element.35.inv_ref, f32[3,18,24,128]{3,2,1,0:T(8,128)S(1)} %get-tuple-element.36.w_ref, ...), custom_call_target="tpu_custom_call" | custom-call | flops 3000000 | bytes 3000000 | tf_op jit(solution)/shard_map/pallas_call | solution.py:26
  58.8 5.0 %all-to-all-done.2.recv_ref = f32[32,4,128]{2,1,0:T(4,128)S(1)} async-done(((f32[32,4,128]{2,1,0:T(4,128)}), f32[32,4,128]{2,1,0:T(4,128)S(1)}, u32[]{:S(2)}, u32[]{:S(2)}) %all-to-all-start.2) | async-done | bytes 65568 | tf_op jit(solution)/shard_map/all_to_all | solution.py:525
  63.9 11.8 %all_to_all.25.recv_ref = f32[16,8,128]{2,1,0:T(8,128)S(1)} all-to-all(f32[16,8,128]{2,1,0:T(8,128)S(1)} %shard_map.75), channel_id=1, replica_groups=mesh['x'=4,'z'=8,'c'=2,'y'=8] {'c','y'}, dimensions={0} | all-to-all | bytes 131072 | tf_op jit(solution)/shard_map/all_to_all | solution.py:525
  75.7 1.1 %shard_map.76 = f32[32,1,128]{2,1,0:T(1,128)} custom-call(f32[16,8,128]{2,1,0:T(8,128)S(1)} %all_to_all.25.recv_ref), custom_call_target="tpu_custom_call" | custom-call | tf_op jit(solution)/shard_map/pallas_call | solution.py:26
  76.8 3.8 %all-to-all-start.4 = ((f32[32,1,128]{2,1,0:T(1,128)}), f32[32,1,128]{2,1,0:T(1,128)S(1)}, u32[]{:S(2)}, u32[]{:S(2)}) async-start(f32[32,1,128]{2,1,0:T(1,128)} %shard_map.76), calls=%async_computation.4 | async-start | bytes 32768 | tf_op jit(solution)/shard_map/all_to_all | solution.py:525
  80.6 0.0 copy-start
  80.6 2.0 %shard_map.77 = (f32[1,128]{1,0:T(1,128)S(1)}, f32[3,16,16,128]{3,2,1,0:T(8,128)S(1)}, f32[3,16,16,128]{3,2,1,0:T(8,128)S(1)}) custom-call(f32[16,8,128]{2,1,0:T(8,128)S(1)} %all_to_all.25.recv_ref, f32[22,24,128]{2,1,0:T(8,128)S(1)} %get-tuple-element.30.k_ref, f32[22,24,128]{2,1,0:T(8,128)S(1)} %get-tuple-element.31.label_ref, ...), custom_call_target="tpu_custom_call" | custom-call | flops 3000000 | bytes 3000000 | tf_op jit(solution)/shard_map/pallas_call | solution.py:26
  82.6 6.5 %all-to-all-done.4.recv_ref = f32[32,1,128]{2,1,0:T(1,128)S(1)} async-done(((f32[32,1,128]{2,1,0:T(1,128)}), f32[32,1,128]{2,1,0:T(1,128)S(1)}, u32[]{:S(2)}, u32[]{:S(2)}) %all-to-all-start.4) | async-done | bytes 16416 | tf_op jit(solution)/shard_map/all_to_all | solution.py:525
  89.2 1.9 %shard_map.78 = (f32[3,16,16,128]{3,2,1,0:T(8,128)}, f32[3,16,16,128]{3,2,1,0:T(8,128)}) custom-call(f32[32,1,128]{2,1,0:T(1,128)S(1)} %all-to-all-done.4.recv_ref, f32[1,128]{1,0:T(1,128)S(1)} %get-tuple-element.39.scal_ref, f32[3,16,16,128]{3,2,1,0:T(8,128)S(1)} %copy-done, f32[3,22,24,128]{3,2,1,0:T(8,128)S(1)} %get-tuple-element.38.z_ref, ...), custom_call_target="tpu_custom_call" | custom-call | tf_op jit(solution)/shard_map/pallas_call | solution.py:26
  (8 shorter events, 0.1 us)
Async XLA Ops:
  2.9 17.6 %collective-permute-start = (f32[3,16,4,128]{3,2,1,0:T(4,128)S(1)}, f32[3,16,4,128]{3,2,1,0:T(4,128)S(1)}, u32[]{:S(2)}, u32[]{:S(2)}) collective-permute-start(f32[3,16,4,128]{3,2,1,0:T(4,128)S(1)} %get-tuple-element.26), channel_id=1, source_target_pairs={{0,1},{2,3},{4,5},{6,7},{1,0},{3,2},{5,4},{7,6},{8,9},{10,11},{12,... | collective-permute-start | bytes 294920 | tf_op jit(solution)/shard_map/ppermute | solution.py:531
  7.0 13.6 %collective-permute-start.1 = (f32[3,16,4,128]{3,2,1,0:T(4,128)S(1)}, f32[3,16,4,128]{3,2,1,0:T(4,128)S(1)}, u32[]{:S(2)}, u32[]{:S(2)}) collective-permute-start(f32[3,16,4,128]{3,2,1,0:T(4,128)S(1)} %get-tuple-element.27), channel_id=1, source_target_pairs={{1,2},{3,4},{5,6},{2,1},{4,3},{6,5},{9,10},{11,12},{13,14},{10,9},... | collective-permute-start | bytes 294920 | tf_op jit(solution)/shard_map/ppermute | solution.py:531
  7.7 21.8 %all-to-all-start = ((f32[32,4,128]{2,1,0:T(4,128)}), f32[32,4,128]{2,1,0:T(4,128)S(1)}, u32[]{:S(2)}, u32[]{:S(2)}) async-start(f32[32,4,128]{2,1,0:T(4,128)} %get-tuple-element.22), calls=%async_computation | async-start | bytes 131072 | tf_op jit(solution)/shard_map/all_to_all | solution.py:525
  20.6 19.9 %collective-permute-start.2 = (f32[232,128]{1,0:T(8,128)S(1)}, f32[232,128]{1,0:T(8,128)S(1)}, u32[]{:S(2)}, u32[]{:S(2)}) collective-permute-start(f32[232,128]{1,0:T(8,128)S(1)} %get-tuple-element.28), channel_id=1, source_target_pairs={{0,8},{16,24},{32,40},{48,56},{64,72},{80,88},{96,104},{112,120},{... | collective-permute-start | bytes 356360 | tf_op jit(solution)/shard_map/ppermute | solution.py:531
  23.8 16.8 %collective-permute-start.3 = (f32[232,128]{1,0:T(8,128)S(1)}, f32[232,128]{1,0:T(8,128)S(1)}, u32[]{:S(2)}, u32[]{:S(2)}) collective-permute-start(f32[232,128]{1,0:T(8,128)S(1)} %get-tuple-element.29), channel_id=1, source_target_pairs={{8,16},{24,32},{40,48},{56,64},{72,80},{88,96},{104,112},{120,128}... | collective-permute-start | bytes 356360 | tf_op jit(solution)/shard_map/ppermute | solution.py:531
  30.1 17.5 %all-to-all-start.1 = ((f32[16,4,128]{2,1,0:T(4,128)}), f32[16,4,128]{2,1,0:T(4,128)S(1)}, u32[]{:S(2)}, u32[]{:S(2)}) async-start(f32[16,4,128]{2,1,0:T(4,128)} %shard_map.69), calls=%async_computation.1 | async-start | bytes 65536 | tf_op jit(solution)/shard_map/all_to_all | solution.py:525
  47.6 7.4 %copy-start.1 = (f32[88,384]{1,0:T(8,128)S(1)}, f32[88,384]{1,0:T(8,128)}, u32[]{:S(2)}) copy-start(f32[88,384]{1,0:T(8,128)} %constant.2.clone.select_ref) | copy-start | bytes 405508
  50.9 12.9 %all-to-all-start.2 = ((f32[32,4,128]{2,1,0:T(4,128)}), f32[32,4,128]{2,1,0:T(4,128)S(1)}, u32[]{:S(2)}, u32[]{:S(2)}) async-start(f32[32,4,128]{2,1,0:T(4,128)} %get-tuple-element.34), calls=%async_computation.2 | async-start | bytes 131072 | tf_op jit(solution)/shard_map/all_to_all | solution.py:525
  76.8 12.4 %all-to-all-start.4 = ((f32[32,1,128]{2,1,0:T(1,128)}), f32[32,1,128]{2,1,0:T(1,128)S(1)}, u32[]{:S(2)}, u32[]{:S(2)}) async-start(f32[32,1,128]{2,1,0:T(1,128)} %shard_map.76), calls=%async_computation.4 | async-start | bytes 32768 | tf_op jit(solution)/shard_map/all_to_all | solution.py:525
  80.6 8.6 %copy-start = (f32[3,16,16,128]{3,2,1,0:T(8,128)S(1)}, f32[3,16,16,128]{3,2,1,0:T(8,128)}, u32[]{:S(2)}) copy-start(f32[3,16,16,128]{3,2,1,0:T(8,128)} %r_ref.1) | copy-start | bytes 1179652

commit v5 on v4

--- a/solution.py
+++ b/solution.py
@@ -48,17 +48,23 @@
     return out
 
 
-def in_lanes(acc_ref, at):
-    sums = jnp.sum(jnp.sum(acc_ref[...], axis=1), axis=1, keepdims=True)
+def totals(acc_ref):
+    return jnp.sum(jnp.sum(acc_ref[...], axis=1), axis=1, keepdims=True)
+
+
+def in_lanes(column, at):
     row = lax.broadcasted_iota(jnp.int32, (12, 128), 0)
     lane = lax.broadcasted_iota(jnp.int32, (12, 128), 1)
-    return jnp.sum(jnp.where(lane == row + at, sums, 0.0), axis=0, keepdims=True)
-
-
-def fold(accs, coarse_ref, acc_ref, u_ref, pad_ref, out_ref, sums=()):
-    for i in range(3 * NREG):
-        acc_ref[i] = accs[i]
-    rc = jnp.sum(jnp.sum(acc_ref[...], axis=1), axis=1, keepdims=True)
+    return jnp.sum(jnp.where(lane == row + at, column, 0.0), axis=0, keepdims=True)
+
+
+def in_rows(lanes, at):
+    row = lax.broadcasted_iota(jnp.int32, (12, 128), 0)
+    lane = lax.broadcasted_iota(jnp.int32, (12, 128), 1)
+    return jnp.sum(jnp.where(lane == row + at, lanes, 0.0), axis=1, keepdims=True)
+
+
+def fold(rc, coarse_ref, u_ref, pad_ref, out_ref, sums=()):
     u_ref[...] = jnp.sum(coarse_ref[...] * rc, axis=0, keepdims=True)
     pad_ref[...] = jnp.zeros_like(pad_ref)
     for w in range(2 * NROWS):
@@ -77,7 +83,6 @@
 
 
 FOLD_SCRATCH = (
-    pltpu.VMEM((12, 16, 128), F32),
     pltpu.VMEM((1, 6144), F32),
     pltpu.VMEM((72, 128), F32),
 )
@@ -88,40 +93,40 @@
 
 
 def first_kernel(
-    r_hbm, occ_hbm, reg_hbm, coarse_hbm,
-    out_ref, a_ref, b_ref, r_ref, k_ref, label_ref, coarse_ref,
-    occ_ref, reg_ref, acc_ref, u_ref, pad_ref, sems,
+    r_hbm, reg_hbm, coarse_hbm,
+    out_ref, r_ref, label_ref, coarse_ref, rc_ref,
+    reg_ref, acc_ref, u_ref, pad_ref, sems,
 ):
-    pairs = ((r_hbm, r_ref), (reg_hbm, reg_ref), (occ_hbm, occ_ref), (coarse_hbm, coarse_ref))
+    pairs = ((r_hbm, r_ref), (reg_hbm, reg_ref), (coarse_hbm, coarse_ref))
     copies = [pltpu.make_async_copy(a, b, sems.at[i]) for i, (a, b) in enumerate(pairs)]
     for copy in copies:
         copy.start()
-    for copy in copies[:3]:
+    for copy in copies[:2]:
         copy.wait()
+
+    def step(x, accs):
+        label = reg_ref[x].astype(F32) + 1.0
+        label_ref[x] = label
+        return tuple(add_regions(accs, label, [r_ref[c, x] for c in range(3)]))
+
+    zero = jnp.zeros((16, 128), F32)
+    accs = lax.fori_loop(0, 16, step, (zero,) * 12, unroll=16)
+    for i in range(12):
+        acc_ref[i] = accs[i]
+    rc = totals(acc_ref)
+    rc_ref[...] = jnp.broadcast_to(rc, (12, 128))
+    copies[2].wait()
+    fold(rc, coarse_ref, u_ref, pad_ref, out_ref)
+
+
+def edge_kernel(occ_ref, label_ref, r_ref, k_ref, a_ref, b_ref):
     k_ref[...] = 0.1 + 0.9 * occ_ref[...].astype(F32)
-    label_ref[...] = reg_ref[...].astype(F32) + 1.0
     even = even_column()
     for ref, last in ((a_ref, even), (b_ref, jnp.logical_not(even))):
         ref[0] = jnp.where(last, k_ref[:, 12:16, :], k_ref[:, 0:4, :])
         for i, field in enumerate([label_ref] + [r_ref.at[c] for c in range(3)]):
             at = 2 * (i % 2)
             ref[1 + i // 2, :, at : at + 2] = jnp.where(last, field[:, 14:16, :], field[:, 0:2, :])
-
-    def step(x, accs):
-        return tuple(add_regions(accs, label_ref[x], [r_ref[c, x] for c in range(3)]))
-
-    zero = jnp.zeros((16, 128), F32)
-    accs = lax.fori_loop(0, 16, step, (zero,) * 12, unroll=2)
-    copies[3].wait()
-    fold(accs, coarse_ref, acc_ref, u_ref, pad_ref, out_ref)
-
-
-def hand_out(part, out_ref):
-    for c in range(2):
-        rows = part[c : c + 3]
-        for y in range(8):
-            out_ref[8 * c + y, 0:3, :] = pltpu.roll(rows, (12 - 12 * y) % 128, axis=1)
-            out_ref[8 * c + y, 3:4, :] = part[0:1]
 
 
 def tail_rows(a_ref, b_ref, i, planes):
@@ -193,11 +198,13 @@
             f_ref[c, x] = f_ref[c, x] * inv
         return carry
 
-    lax.fori_loop(1, 21, step, 0, unroll=2)
+    lax.fori_loop(1, 21, step, 0, unroll=20)
 
 
 def around_kernel(recv_ref, out_ref):
-    hand_out(jnp.sum(recv_ref[...], axis=0), out_ref)
+    part = jnp.sum(recv_ref[...], axis=0)
+    for n in range(NCOLS):
+        out_ref[n] = part
 
 
 def pass_kernel(recv_ref, own_ref, pair_ref, out_ref):
@@ -205,6 +212,11 @@
     rows = jnp.concatenate([part, own_ref[...], pair_ref[...]], axis=0)
     for n in range(NCOLS):
         out_ref[n] = rows
+
+
+def around(q):
+    near = jnp.where(lax.axis_index("c") == 0, q[0:3], q[1:4])
+    return pltpu.roll(near, lax.rem(140 - 12 * lax.axis_index("y"), 128), axis=1)
 
 
 def iotas():
@@ -261,55 +273,42 @@
     return out
 
 
-def second_kernel(
-    recv_ref, r_ref, k_ref, label_ref, f_ref, coarse_ref,
-    out_ref, z_ref, w_ref, own_ref,
-    map_ref, acc_ref, u_ref, pad_ref,
-):
-    q = jnp.sum(recv_ref[...], axis=0)
-    spread_maps(q, map_ref)
-
-    def first_step(s):
-        def body(x, carry):
-            label = label_ref[x]
-            for c in range(3):
-                z_ref[c, x] = f_ref[c, x] + spread(label, map_ref, s, c)
-            return carry
-
-        return body
-
-    lax.fori_loop(1, 3, first_step(0), 0)
-    lax.fori_loop(3, 19, first_step(1), 0, unroll=2)
-    lax.fori_loop(19, 21, first_step(2), 0)
-
-    def image(x):
-        here = k_ref[x]
-        faces, diagonal = coefficients(k_ref[x - 1], here, k_ref[x + 1])
-        fields = [z_ref[c, x] for c in range(3)]
-        w = operate(
-            faces, diagonal, here, [z_ref[c, x - 1] for c in range(3)], fields, [z_ref[c, x + 1] for c in range(3)]
-        )
+def image_of(k_ref, x, field_ref, at):
+    here = k_ref[x]
+    faces, diagonal = coefficients(k_ref[x - 1], here, k_ref[x + 1])
+    planes = [[field_ref[c, i] for c in range(3)] for i in (at - 1, at, at + 1)]
+    return planes[1], operate(faces, diagonal, here, *planes)
+
+
+def start_kernel(k_ref, label_ref, f_ref, r_ref, out_ref, acc_ref):
+    def step(x, carry):
+        fields, image = image_of(k_ref, x, f_ref, x)
+        own = [v[0:16] for v in image]
+        rf, faf = carry[12], carry[13]
         for c in range(3):
-            w_ref[c, x - 2] = w[c]
-        return fields, w
-
-    image(2)
-    image(19)
-
-    def second_step(x, carry):
-        fields, w = image(x)
-        own = [v[0:16] for v in w]
-        rz, zw = carry[12], carry[13]
-        for c in range(3):
-            z = fields[c][0:16]
-            rz = rz + r_ref[c, x - 3] * z
-            zw = zw + z * own[c]
-        return (*add_regions(carry[:12], label_ref[x, 0:16], own), rz, zw)
+            f = fields[c][0:16]
+            rf = rf + r_ref[c, x - 3] * f
+            faf = faf + f * own[c]
+        return (*add_regions(carry[:12], label_ref[x, 0:16], own), rf, faf)
 
     zero = jnp.zeros((16, 128), F32)
-    carry = lax.fori_loop(3, 19, second_step, (zero,) * 14)
-    fold(carry[:12], coarse_ref, acc_ref, u_ref, pad_ref, out_ref, (total(carry[12]), total(carry[13])))
-    own_ref[...] = in_lanes(acc_ref, 12)
+    carry = lax.fori_loop(3, 19, step, (zero,) * 14, unroll=16)
+    for i in range(14):
+        acc_ref[i] = carry[i]
+    out_ref[...] = jnp.broadcast_to(totals(acc_ref), (14, 128))
+
+
+def second_kernel(recv_ref, rc_ref, start_ref, rows_ref, coarse_ref, out_ref, own_ref, near_ref, u_ref, pad_ref):
+    near = around(jnp.sum(recv_ref[...], axis=0))
+    near_ref[...] = near
+    product = rows_ref[0] * near[0:1] + rows_ref[1] * near[1:2] + rows_ref[2] * near[2:3]
+    e = start_ref[0:12, 0:1]
+    aggregates = e + jnp.sum(product, axis=1, keepdims=True)
+    q = in_rows(near[1:2], 12)
+    rz = start_ref[12:13, 0:1] + jnp.sum(rc_ref[:, 0:1] * q, axis=0, keepdims=True)
+    zw = start_ref[13:14, 0:1] + jnp.sum(q * (e + aggregates), axis=0, keepdims=True)
+    fold(aggregates, coarse_ref, u_ref, pad_ref, out_ref, (rz, zw))
+    own_ref[...] = in_lanes(aggregates, 12)
 
 
 def selection():
@@ -335,7 +334,7 @@
     return v[0:8] + v[8:16]
 
 
-def pair_kernel(k_ref, label_ref, select_ref, out_ref, acc_ref):
+def pair_kernel(k_ref, label_ref, select_ref, out_ref, rows_ref, acc_ref, sum_ref):
     row = lax.broadcasted_iota(jnp.int32, (24, 128), 0)
     lane = lax.broadcasted_iota(jnp.int32, (24, 128), 1)
 
@@ -360,7 +359,7 @@
         return tuple(out)
 
     zero = jnp.zeros((8, 128), F32)
-    accs = lax.fori_loop(3, 18, lambda x, a: plane(x, a, True), (zero,) * 24)
+    accs = lax.fori_loop(3, 18, lambda x, a: plane(x, a, True), (zero,) * 24, unroll=15)
     accs = plane(18, accs, False)
     for i in range(16):
         acc_ref[i] = accs[i]
@@ -382,24 +381,66 @@
     sums = jnp.sum(jnp.sum(acc_ref[...], axis=1), axis=1, keepdims=True)
     for i in range(3):
         out_ref[i : i + 1] = jnp.sum(select_ref[:, 128 * i : 128 * i + 128] * sums, axis=0, keepdims=True)
-
-
-def moment_kernel(k_ref, label_ref, inv_ref, w_ref, own_ref, out_ref, g_ref, acc_ref):
-    def first_step(x, carry):
+    sum_ref[...] = jnp.broadcast_to(sums, (88, 128))
+    row = lax.broadcasted_iota(jnp.int32, (12, 128), 0)
+    lane = lax.broadcasted_iota(jnp.int32, (12, 128), 1)
+    first = 3 * ((row >= 3).astype(jnp.int32) + (row >= 6).astype(jnp.int32) + (row >= 9).astype(jnp.int32))
+    component = row - first
+
+    def column(indices):
+        return jnp.concatenate([jnp.broadcast_to(sum_ref[i : i + 1], (3, 128)) for i in indices], axis=0)
+
+    def block(n, at):
+        out = jnp.zeros((12, 128), F32)
+        for h in range(NREG):
+            value = column([16 * n + 4 * g + h for g in range(NREG)])
+            if n == 0:
+                value = value + column([4 * h + g for g in range(NREG)])
+            out = out - jnp.where(lane == at + 3 * h + component, value, 0.0)
+        return out
+
+    quarter, coupling = column(range(80, 84)), column(range(84, 88))
+    rows_ref[0] = block(1, 12)
+    rows_ref[1] = (
+        block(0, 12)
+        + block(3, 0)
+        + block(4, 24)
+        + jnp.where(lane == 12 + row, quarter + coupling, 0.0)
+        + jnp.where((lane >= 12 + first) & (lane < 15 + first), quarter, 0.0)
+    )
+    rows_ref[2] = block(2, 12)
+
+
+def moment_kernel(
+    near_ref, k_ref, label_ref, inv_ref, f_ref, own_ref, z_ref, w_ref, out_ref, g_ref, acc_ref, map_ref
+):
+    spread_maps(near_ref[...], map_ref)
+
+    def first_step(s):
+        def body(x, carry):
+            label = label_ref[x]
+            for c in range(3):
+                z_ref[c, x] = f_ref[c, x] + spread(label, map_ref, s, c)
+            return carry
+
+        return body
+
+    lax.fori_loop(1, 3, first_step(0), 0)
+    lax.fori_loop(3, 19, first_step(1), 0, unroll=16)
+    lax.fori_loop(19, 21, first_step(2), 0)
+
+    def second_step(x, carry):
+        _, w = image_of(k_ref, x, z_ref, x)
         inv = inv_ref[x]
         for c in range(3):
-            g_ref[c, x - 2] = w_ref[c, x - 2] * inv
+            w_ref[c, x - 2] = w[c]
+            g_ref[c, x - 2] = w[c] * inv
         return carry
 
-    lax.fori_loop(2, 20, first_step, 0, unroll=2)
+    lax.fori_loop(2, 20, second_step, 0, unroll=18)
 
     def step(x, carry):
-        here = k_ref[x + 2]
-        faces, diagonal = coefficients(k_ref[x + 1], here, k_ref[x + 3])
-        fields = [g_ref[c, x] for c in range(3)]
-        image = operate(
-            faces, diagonal, here, [g_ref[c, x - 1] for c in range(3)], fields, [g_ref[c, x + 1] for c in range(3)]
-        )
+        fields, image = image_of(k_ref, x + 2, g_ref, x)
         own = [v[0:16] for v in image]
         wg, gg = carry[12], carry[13]
         for c in range(3):
@@ -409,11 +450,11 @@
         return (*add_regions(carry[:12], label_ref[x + 2, 0:16], own), wg, gg)
 
     zero = jnp.zeros((16, 128), F32)
-    carry = lax.fori_loop(1, 17, step, (zero,) * 14)
+    carry = lax.fori_loop(1, 17, step, (zero,) * 14, unroll=16)
     for i in range(12):
         acc_ref[i] = carry[i]
     lane = lax.broadcasted_iota(jnp.int32, (1, 128), 1)
-    row = in_lanes(acc_ref, 0) + own_ref[...]
+    row = in_lanes(totals(acc_ref), 0) + own_ref[...]
     out_ref[...] = jnp.where(lane == 24, total(carry[12]), jnp.where(lane == 25, total(carry[13]), row))
 
 
@@ -464,8 +505,7 @@
 
 def third_kernel(recv_ref, k_ref, label_ref, inv_ref, z_ref, w_ref, scal_ref, own_ref, image_ref, znew_ref, map_ref):
     q = jnp.sum(recv_ref[:, 0:4, :], axis=0)
-    near = jnp.where(lax.axis_index("c") == 0, q[0:3], q[1:4])
-    spread_maps(pltpu.roll(near, lax.rem(140 - 12 * lax.axis_index("y"), 128), axis=1), map_ref)
+    spread_maps(around(q), map_ref)
     scal_ref[...] = q[0:1]
     rz, zw = q[0:1, SLAB : SLAB + 1], q[0:1, SLAB + 1 : SLAB + 2]
     alpha = rz / zw
@@ -481,7 +521,7 @@
         return body
 
     first_step(0)(2, 0)
-    lax.fori_loop(3, 19, first_step(1), 0, unroll=2)
+    lax.fori_loop(3, 19, first_step(1), 0, unroll=16)
     first_step(2)(19, 0)
 
     def second_step(x, carry):
@@ -496,7 +536,7 @@
             image_ref[c, x - 1] = image[c][0:16]
         return carry
 
-    lax.fori_loop(1, 17, second_step, 0)
+    lax.fori_loop(1, 17, second_step, 0, unroll=16)
 
 
 def last_kernel(recv_ref, scal_ref, r_ref, z_ref, w_ref, znew_ref, image_ref, x_ref, res_ref):
@@ -533,26 +573,23 @@
 
 def local(right, occ, reg, coarse):
     field, plane = (16, 16, 128), (24, 128)
-    send, one, two, r, k_own, label_own, coarse = call(
+    send, r, label_own, coarse, rc = call(
         first_kernel,
-        (
-            shape(NROWS, 4, 128),
-            shape(3, 16, 4, 128),
-            shape(3, 16, 4, 128),
-            shape(3, *field),
-            shape(*field),
-            shape(*field),
-            shape(12, 6144),
-        ),
-        tuple(pltpu.with_memory_space_constraint(a, pltpu.HBM) for a in (right, occ, reg, coarse)),
+        (shape(NROWS, 4, 128), shape(3, *field), shape(*field), shape(12, 6144), shape(12, 128)),
+        tuple(pltpu.with_memory_space_constraint(a, pltpu.HBM) for a in (right, reg, coarse)),
         (
             pltpu.VMEM(field, jnp.int32),
-            pltpu.VMEM(field, jnp.int32),
+            pltpu.VMEM((12, 16, 128), F32),
             *FOLD_SCRATCH,
-            pltpu.SemaphoreType.DMA((4,)),
+            pltpu.SemaphoreType.DMA((3,)),
         ),
         space=pl.BlockSpec(memory_space=pltpu.HBM),
-        limit=24,
+    )
+    k_own, one, two = call(
+        edge_kernel,
+        (shape(*field), shape(3, 16, 4, 128), shape(3, 16, 4, 128)),
+        (occ, label_own, r),
+        cost=3000000,
     )
     one = swapped(one, "y", 0)
     two = swapped(two, "y", 1)
@@ -570,23 +607,28 @@
         (r, k_own, label_own, one, two, first, second),
         cost=3000000,
     )
-    pair = call(
-        pair_kernel, shape(3, 128), (k, label, jnp.asarray(selection())), (pltpu.VMEM((88, 8, 128), F32),), cost=3000000
-    )
-    send, z, w, own = call(
+    start = call(start_kernel, shape(14, 128), (k, label, f, r), (pltpu.VMEM((14, 16, 128), F32),), cost=3000000)
+    pair, rows = call(
+        pair_kernel,
+        (shape(3, 128), shape(3, 12, 128)),
+        (k, label, jnp.asarray(selection())),
+        (pltpu.VMEM((88, 8, 128), F32), pltpu.VMEM((88, 128), F32)),
+        cost=3000000,
+    )
+    send, own, near = call(
         second_kernel,
-        (shape(NROWS, 4, 128), shape(3, 22, *plane), shape(3, 18, *plane), shape(1, 128)),
-        (got, r, k, label, f, coarse),
-        (pltpu.VMEM((3, 12, *plane), F32), *FOLD_SCRATCH),
-        alias={4: 1},
+        (shape(NROWS, 4, 128), shape(1, 128), shape(3, 128)),
+        (got, rc, start, rows, coarse),
+        FOLD_SCRATCH,
     )
     got = exchange(send, ROWS)
-    own = call(
+    z, w, own = call(
         moment_kernel,
-        shape(1, 128),
-        (k, label, inv, w, own),
-        (pltpu.VMEM((3, 18, *plane), F32), pltpu.VMEM((12, 16, 128), F32)),
+        (shape(3, 22, *plane), shape(3, 18, *plane), shape(1, 128)),
+        (near, k, label, inv, f, own),
+        (pltpu.VMEM((3, 18, *plane), F32), pltpu.VMEM((12, 16, 128), F32), pltpu.VMEM((3, 12, *plane), F32)),
         cost=3000000,
+        alias={4: 0},
     )
     send = call(pass_kernel, shape(NCOLS, 8, 128), (got, own, pair))
     got = exchange(send, COLS)

time: 91.6 us -> 89.3 us (0.975)
  Pallas kernels: 16.3 us -> 12 us
  waiting for transfers between devices: 19.9 us -> 21.6 us
    pallas_call x11 -> x13, Pallas kernels: 16.3 us -> 12 us  [call(): pl.pallas_call(kernel, out_shape=outs, in_specs=[space] * len(ins), out_s...]
    all_to_all x4, waiting for transfers between devices: 19.9 us -> 21.6 us  [exchange(): return lax.all_to_all(array, axes, 0, 0, tiled=True)]
  transfers between devices with their start and end apart: 8 -> 8, of which waited for: 4 -> 4; matrix products, arithmetic and copies ran while one was open for 0% -> 0% of each run, Pallas kernels for 8% -> 6%
where the time goes in v5:
time: 89.3 us; the launch traced here: 88.8 us
  starting transfers between devices  42.4 us (47%)
  waiting for transfers between devices  21.6 us (24%)
  Pallas kernels  12 us (13%)
  blocking collectives  11.8 us (13%)
    all_to_all x4, starting transfers between devices, exchange(): return lax.all_to_all(array, axes, 0, 0, tiled=True)  31.2 us
    all_to_all x4, waiting for transfers between devices, exchange(): return lax.all_to_all(array, axes, 0, 0, tiled=True)  21.6 us
    pallas_call x13, Pallas kernels, call(): pl.pallas_call(kernel, out_shape=outs, in_specs=[space] * len(ins), out_s...  12 us
    all_to_all x1, blocking collectives, exchange(): return lax.all_to_all(array, axes, 0, 0, tiled=True)  11.8 us
    ppermute x4, starting transfers between devices, swapped(): return lax.ppermute(array, axis, pairs + [(b, a) for a, b in pairs])  11.2 us
  transfers between devices with their start and end apart: 8, of which 4 were waited for; matrix products, arithmetic and copies ran while one was open for 0% of the time, Pallas kernels for 6%

profile of v5, /device:TPU:1, one launch (start us, length us, event | category | flops | bytes accessed | tf_op | source)
XLA Modules:
  0.0 88.8 jit_solution(5209575045780148171)
XLA Ops:
  0.6 2.2 %shard_map.68 = (f32[32,4,128]{2,1,0:T(4,128)}, f32[3,16,16,128]{3,2,1,0:T(8,128)S(1)}, f32[16,16,128]{2,1,0:T(8,128)S(1)}, f32[12,6144]{1,0:T(8,128)S(1)}, f32[12,128]{1,0:T(8,128)S(1)}) custom-call(f32[3,16,16,128]{3,2,1,0:T(8,128)} %r_ref.1, s32[16,16,128]{2,1,0:T(8,128)} %reg_hbm.1, f32[12,6144]{1,0:T(8,128)} %coarse_hbm.1), custom_call_target="tpu_custom_call" | custom-call | tf_op jit(solution)/shard_map/pallas_call | solution.py:26
  2.9 4.0 %collective-permute-start = (f32[3,16,4,128]{3,2,1,0:T(4,128)S(1)}, f32[3,16,4,128]{3,2,1,0:T(4,128)S(1)}, u32[]{:S(2)}, u32[]{:S(2)}) collective-permute-start(f32[3,16,4,128]{3,2,1,0:T(4,128)S(1)} %get-tuple-element.32), channel_id=1, source_target_pairs={{0,1},{2,3},{4,5},{6,7},{1,0},{3,2},{5,4},{7,6},{8,9},{10,11},{12,... | collective-permute-start | bytes 294920 | tf_op jit(solution)/shard_map/ppermute | solution.py:571
  7.0 0.7 collective-permute-start.1
  7.6 12.9 %all-to-all-start = ((f32[32,4,128]{2,1,0:T(4,128)}), f32[32,4,128]{2,1,0:T(4,128)S(1)}, u32[]{:S(2)}, u32[]{:S(2)}) async-start(f32[32,4,128]{2,1,0:T(4,128)} %get-tuple-element.27), calls=%async_computation | async-start | bytes 131072 | tf_op jit(solution)/shard_map/all_to_all | solution.py:565
  20.6 3.1 %collective-permute-start.2 = (f32[232,128]{1,0:T(8,128)S(1)}, f32[232,128]{1,0:T(8,128)S(1)}, u32[]{:S(2)}, u32[]{:S(2)}) collective-permute-start(f32[232,128]{1,0:T(8,128)S(1)} %get-tuple-element.34), channel_id=1, source_target_pairs={{0,8},{16,24},{32,40},{48,56},{64,72},{80,88},{96,104},{112,120},{... | collective-permute-start | bytes 356360 | tf_op jit(solution)/shard_map/ppermute | solution.py:571
  23.8 3.3 %collective-permute-start.3 = (f32[232,128]{1,0:T(8,128)S(1)}, f32[232,128]{1,0:T(8,128)S(1)}, u32[]{:S(2)}, u32[]{:S(2)}) collective-permute-start(f32[232,128]{1,0:T(8,128)S(1)} %get-tuple-element.35), channel_id=1, source_target_pairs={{8,16},{24,32},{40,48},{56,64},{72,80},{88,96},{104,112},{120,128}... | collective-permute-start | bytes 356360 | tf_op jit(solution)/shard_map/ppermute | solution.py:571
  27.1 2.3 %all-to-all-done.recv_ref = f32[32,4,128]{2,1,0:T(4,128)S(1)} async-done(((f32[32,4,128]{2,1,0:T(4,128)}), f32[32,4,128]{2,1,0:T(4,128)S(1)}, u32[]{:S(2)}, u32[]{:S(2)}) %all-to-all-start) | async-done | bytes 65568 | tf_op jit(solution)/shard_map/all_to_all | solution.py:565
  29.4 0.7 shard_map.69
  30.0 10.4 %all-to-all-start.1 = ((f32[16,4,128]{2,1,0:T(4,128)}), f32[16,4,128]{2,1,0:T(4,128)S(1)}, u32[]{:S(2)}, u32[]{:S(2)}) async-start(f32[16,4,128]{2,1,0:T(4,128)} %shard_map.69), calls=%async_computation.1 | async-start | bytes 65536 | tf_op jit(solution)/shard_map/all_to_all | solution.py:565
  40.5 0.4 shard_map.72
  40.9 0.7 shard_map.73.start_ref
  41.6 0.2 copy-done.1
  41.8 1.1 %shard_map.74 = (f32[3,128]{1,0:T(4,128)S(1)}, f32[3,12,128]{2,1,0:T(8,128)S(1)}) custom-call(f32[22,24,128]{2,1,0:T(8,128)S(1)} %get-tuple-element.36.k_ref, f32[22,24,128]{2,1,0:T(8,128)S(1)} %get-tuple-element.37.label_ref, f32[88,384]{1,0:T(8,128)S(1)} %copy-done.1), custom_call_target="tpu_custom_call" | custom-call | flops 3000000 | bytes 3000000 | tf_op jit(solution)/shard_map/pallas_call | solution.py:26
  42.9 4.6 %all-to-all-done.1.recv_ref = f32[16,4,128]{2,1,0:T(4,128)S(1)} async-done(((f32[16,4,128]{2,1,0:T(4,128)}), f32[16,4,128]{2,1,0:T(4,128)S(1)}, u32[]{:S(2)}, u32[]{:S(2)}) %all-to-all-start.1) | async-done | bytes 32800 | tf_op jit(solution)/shard_map/all_to_all | solution.py:565
  47.5 1.1 %shard_map.75 = (f32[32,4,128]{2,1,0:T(4,128)}, f32[1,128]{1,0:T(1,128)S(1)}, f32[3,128]{1,0:T(4,128)S(1)}) custom-call(f32[16,4,128]{2,1,0:T(4,128)S(1)} %all-to-all-done.1.recv_ref, f32[12,128]{1,0:T(8,128)S(1)} %get-tuple-element.28.rc_ref, f32[14,128]{1,0:T(8,128)S(1)} %shard_map.73.start_ref, f32[3,12,128]{2,1,0:T(8,128)S(1)} %get-tuple-element.39.rows_ref, ...), custom_call_target="tpu_custom_call" | custom-call | tf_op jit(solution)/shard_map/pallas_call | solution.py:26
  48.6 4.1 %all-to-all-start.2 = ((f32[32,4,128]{2,1,0:T(4,128)}), f32[32,4,128]{2,1,0:T(4,128)S(1)}, u32[]{:S(2)}, u32[]{:S(2)}) async-start(f32[32,4,128]{2,1,0:T(4,128)} %get-tuple-element.41), calls=%async_computation.2 | async-start | bytes 131072 | tf_op jit(solution)/shard_map/all_to_all | solution.py:565
  52.7 1.9 %shard_map.76 = (f32[3,22,24,128]{3,2,1,0:T(8,128)S(1)}, f32[3,18,24,128]{3,2,1,0:T(8,128)S(1)}, f32[1,128]{1,0:T(1,128)S(1)}) custom-call(f32[3,128]{1,0:T(4,128)S(1)} %get-tuple-element.42.near_ref, f32[22,24,128]{2,1,0:T(8,128)S(1)} %get-tuple-element.36.k_ref, f32[22,24,128]{2,1,0:T(8,128)S(1)} %get-tuple-element.37.label_ref, ...), custom_call_target="tpu_custom_call", output_to_operand_aliasing={{0}: (4, {})} | custom-call | flops 3000000 | bytes 3000000 | tf_op jit(solution)/shard_map/pallas_call | solution.py:26
  54.6 6.9 %all-to-all-done.2.recv_ref = f32[32,4,128]{2,1,0:T(4,128)S(1)} async-done(((f32[32,4,128]{2,1,0:T(4,128)}), f32[32,4,128]{2,1,0:T(4,128)S(1)}, u32[]{:S(2)}, u32[]{:S(2)}) %all-to-all-start.2) | async-done | bytes 65568 | tf_op jit(solution)/shard_map/all_to_all | solution.py:565
  61.6 11.8 %all_to_all.25.recv_ref = f32[16,8,128]{2,1,0:T(8,128)S(1)} all-to-all(f32[16,8,128]{2,1,0:T(8,128)S(1)} %shard_map.77), channel_id=1, replica_groups=mesh['x'=4,'z'=8,'c'=2,'y'=8] {'c','y'}, dimensions={0} | all-to-all | bytes 131072 | tf_op jit(solution)/shard_map/all_to_all | solution.py:565
  73.4 1.1 %shard_map.78 = f32[32,1,128]{2,1,0:T(1,128)} custom-call(f32[16,8,128]{2,1,0:T(8,128)S(1)} %all_to_all.25.recv_ref), custom_call_target="tpu_custom_call" | custom-call | tf_op jit(solution)/shard_map/pallas_call | solution.py:26
  74.5 3.8 %all-to-all-start.4 = ((f32[32,1,128]{2,1,0:T(1,128)}), f32[32,1,128]{2,1,0:T(1,128)S(1)}, u32[]{:S(2)}, u32[]{:S(2)}) async-start(f32[32,1,128]{2,1,0:T(1,128)} %shard_map.78), calls=%async_computation.4 | async-start | bytes 32768 | tf_op jit(solution)/shard_map/all_to_all | solution.py:565
  78.3 0.8 shard_map.79
  79.2 7.7 %all-to-all-done.4.recv_ref = f32[32,1,128]{2,1,0:T(1,128)S(1)} async-done(((f32[32,1,128]{2,1,0:T(1,128)}), f32[32,1,128]{2,1,0:T(1,128)S(1)}, u32[]{:S(2)}, u32[]{:S(2)}) %all-to-all-start.4) | async-done | bytes 16416 | tf_op jit(solution)/shard_map/all_to_all | solution.py:565
  86.9 1.9 %shard_map.80 = (f32[3,16,16,128]{3,2,1,0:T(8,128)}, f32[3,16,16,128]{3,2,1,0:T(8,128)}) custom-call(f32[32,1,128]{2,1,0:T(1,128)S(1)} %all-to-all-done.4.recv_ref, f32[1,128]{1,0:T(1,128)S(1)} %get-tuple-element.49.scal_ref, f32[3,16,16,128]{3,2,1,0:T(8,128)S(1)} %copy-done, f32[3,22,24,128]{3,2,1,0:T(8,128)S(1)} %get-tuple-element.47.z_ref, ...), custom_call_target="tpu_custom_call" | custom-call | tf_op jit(solution)/shard_map/pallas_call | solution.py:26
  (12 shorter events, 0.2 us)
Async XLA Ops:
  0.6 2.2 %copy-start.2 = (s32[16,16,128]{2,1,0:T(8,128)S(1)}, s32[16,16,128]{2,1,0:T(8,128)}, u32[]{:S(2)}) copy-start(s32[16,16,128]{2,1,0:T(8,128)} %occ_ref.1) | copy-start | bytes 393220
  2.9 17.6 %collective-permute-start = (f32[3,16,4,128]{3,2,1,0:T(4,128)S(1)}, f32[3,16,4,128]{3,2,1,0:T(4,128)S(1)}, u32[]{:S(2)}, u32[]{:S(2)}) collective-permute-start(f32[3,16,4,128]{3,2,1,0:T(4,128)S(1)} %get-tuple-element.32), channel_id=1, source_target_pairs={{0,1},{2,3},{4,5},{6,7},{1,0},{3,2},{5,4},{7,6},{8,9},{10,11},{12,... | collective-permute-start | bytes 294920 | tf_op jit(solution)/shard_map/ppermute | solution.py:571
  7.0 13.6 %collective-permute-start.1 = (f32[3,16,4,128]{3,2,1,0:T(4,128)S(1)}, f32[3,16,4,128]{3,2,1,0:T(4,128)S(1)}, u32[]{:S(2)}, u32[]{:S(2)}) collective-permute-start(f32[3,16,4,128]{3,2,1,0:T(4,128)S(1)} %get-tuple-element.33), channel_id=1, source_target_pairs={{1,2},{3,4},{5,6},{2,1},{4,3},{6,5},{9,10},{11,12},{13,14},{10,9},... | collective-permute-start | bytes 294920 | tf_op jit(solution)/shard_map/ppermute | solution.py:571
  7.6 21.8 %all-to-all-start = ((f32[32,4,128]{2,1,0:T(4,128)}), f32[32,4,128]{2,1,0:T(4,128)S(1)}, u32[]{:S(2)}, u32[]{:S(2)}) async-start(f32[32,4,128]{2,1,0:T(4,128)} %get-tuple-element.27), calls=%async_computation | async-start | bytes 131072 | tf_op jit(solution)/shard_map/all_to_all | solution.py:565
  20.6 19.9 %collective-permute-start.2 = (f32[232,128]{1,0:T(8,128)S(1)}, f32[232,128]{1,0:T(8,128)S(1)}, u32[]{:S(2)}, u32[]{:S(2)}) collective-permute-start(f32[232,128]{1,0:T(8,128)S(1)} %get-tuple-element.34), channel_id=1, source_target_pairs={{0,8},{16,24},{32,40},{48,56},{64,72},{80,88},{96,104},{112,120},{... | collective-permute-start | bytes 356360 | tf_op jit(solution)/shard_map/ppermute | solution.py:571
  23.8 16.7 %collective-permute-start.3 = (f32[232,128]{1,0:T(8,128)S(1)}, f32[232,128]{1,0:T(8,128)S(1)}, u32[]{:S(2)}, u32[]{:S(2)}) collective-permute-start(f32[232,128]{1,0:T(8,128)S(1)} %get-tuple-element.35), channel_id=1, source_target_pairs={{8,16},{24,32},{40,48},{56,64},{72,80},{88,96},{104,112},{120,128}... | collective-permute-start | bytes 356360 | tf_op jit(solution)/shard_map/ppermute | solution.py:571
  30.0 17.5 %all-to-all-start.1 = ((f32[16,4,128]{2,1,0:T(4,128)}), f32[16,4,128]{2,1,0:T(4,128)S(1)}, u32[]{:S(2)}, u32[]{:S(2)}) async-start(f32[16,4,128]{2,1,0:T(4,128)} %shard_map.69), calls=%async_computation.1 | async-start | bytes 65536 | tf_op jit(solution)/shard_map/all_to_all | solution.py:565
  40.9 0.9 %copy-start.1 = (f32[88,384]{1,0:T(8,128)S(1)}, f32[88,384]{1,0:T(8,128)}, u32[]{:S(2)}) copy-start(f32[88,384]{1,0:T(8,128)} %constant.2.clone.select_ref) | copy-start | bytes 405508
  48.6 12.9 %all-to-all-start.2 = ((f32[32,4,128]{2,1,0:T(4,128)}), f32[32,4,128]{2,1,0:T(4,128)S(1)}, u32[]{:S(2)}, u32[]{:S(2)}) async-start(f32[32,4,128]{2,1,0:T(4,128)} %get-tuple-element.41), calls=%async_computation.2 | async-start | bytes 131072 | tf_op jit(solution)/shard_map/all_to_all | solution.py:565
  74.5 12.4 %all-to-all-start.4 = ((f32[32,1,128]{2,1,0:T(1,128)}), f32[32,1,128]{2,1,0:T(1,128)S(1)}, u32[]{:S(2)}, u32[]{:S(2)}) async-start(f32[32,1,128]{2,1,0:T(1,128)} %shard_map.78), calls=%async_computation.4 | async-start | bytes 32768 | tf_op jit(solution)/shard_map/all_to_all | solution.py:565
  78.3 8.6 %copy-start = (f32[3,16,16,128]{3,2,1,0:T(8,128)S(1)}, f32[3,16,16,128]{3,2,1,0:T(8,128)}, u32[]{:S(2)}) copy-start(f32[3,16,16,128]{3,2,1,0:T(8,128)} %r_ref.1) | copy-start | bytes 1179652

commit v6 on v5

--- a/solution.py
+++ b/solution.py
@@ -16,18 +16,20 @@
 NREG = 4
 SLAB = 96
 VMEM = pl.BlockSpec(memory_space=pltpu.VMEM)
+HBM = pl.BlockSpec(memory_space=pltpu.HBM)
+PARTS = 4
 
 
 def shape(*dims):
     return jax.ShapeDtypeStruct(dims, F32)
 
 
-def call(kernel, outs, ins, scratch=(), space=VMEM, cost=0, limit=24, alias=None):
+def call(kernel, outs, ins, scratch=(), space=VMEM, target=VMEM, cost=0, limit=24, alias=None):
     return pl.pallas_call(
         kernel,
         out_shape=outs,
         in_specs=[space] * len(ins),
-        out_specs=jax.tree.map(lambda _: VMEM, outs),
+        out_specs=jax.tree.map(lambda _: target, outs),
         scratch_shapes=list(scratch),
         input_output_aliases=alias or {},
         cost_estimate=pl.CostEstimate(flops=cost, bytes_accessed=cost, transcendentals=0) if cost else None,
@@ -539,7 +541,7 @@
     lax.fori_loop(1, 17, second_step, 0, unroll=16)
 
 
-def last_kernel(recv_ref, scal_ref, r_ref, z_ref, w_ref, znew_ref, image_ref, x_ref, res_ref):
+def last_kernel(recv_ref, scal_ref, r_ref, z_ref, w_ref, znew_ref, image_ref, x_hbm, res_hbm, x_ref, res_ref, sems):
     sums = jnp.sum(recv_ref[...], axis=0)
     wy, yay = sums[:, 0:1], sums[:, 1:2]
     scal = scal_ref[...]
@@ -552,13 +554,19 @@
     second = new / (zaz + ratio * (2.0 * cross + ratio * zw))
     first = alpha + second * ratio
 
-    def step(x, carry):
-        for c in range(3):
-            x_ref[c, x] = first * z_ref[c, x + 3, 0:16] + second * znew_ref[c, x]
-            res_ref[c, x] = r_ref[c, x] - first * w_ref[c, x + 1, 0:16] - second * image_ref[c, x]
-        return carry
-
-    lax.fori_loop(0, 16, step, 0, unroll=2)
+    copies = []
+    for part in range(PARTS):
+        planes = range(part * 16 // PARTS, (part + 1) * 16 // PARTS)
+        for x in planes:
+            for c in range(3):
+                x_ref[c, x] = first * z_ref[c, x + 3, 0:16] + second * znew_ref[c, x]
+                res_ref[c, x] = r_ref[c, x] - first * w_ref[c, x + 1, 0:16] - second * image_ref[c, x]
+        own = pl.ds(planes[0], len(planes))
+        for i, (ref, out) in enumerate(((x_ref, x_hbm), (res_ref, res_hbm))):
+            copies.append(pltpu.make_async_copy(ref.at[:, own], out.at[:, own], sems.at[2 * part + i]))
+            copies[-1].start()
+    for copy in copies:
+        copy.wait()
 
 
 def exchange(array, axes):
@@ -583,7 +591,7 @@
             *FOLD_SCRATCH,
             pltpu.SemaphoreType.DMA((3,)),
         ),
-        space=pl.BlockSpec(memory_space=pltpu.HBM),
+        space=HBM,
     )
     k_own, one, two = call(
         edge_kernel,
@@ -645,6 +653,8 @@
         last_kernel,
         (shape(3, *field), shape(3, *field)),
         (got, scal, right, z, w, znew, image),
+        (pltpu.VMEM((3, *field), F32), pltpu.VMEM((3, *field), F32), pltpu.SemaphoreType.DMA((2 * PARTS,))),
+        target=HBM,
     )
 
 

time: 89.3 us -> 88.8 us (level)
  no operation moved by 1% of the time
where the time goes in v6:
time: 88.8 us; the launch traced here: 88.3 us
  starting transfers between devices  42.4 us (48%)
  waiting for transfers between devices  21.6 us (24%)
  blocking collectives  11.8 us (13%)
  Pallas kernels  11.5 us (13%)
    all_to_all x4, starting transfers between devices, exchange(): return lax.all_to_all(array, axes, 0, 0, tiled=True)  31.2 us
    all_to_all x4, waiting for transfers between devices, exchange(): return lax.all_to_all(array, axes, 0, 0, tiled=True)  21.6 us
    all_to_all x1, blocking collectives, exchange(): return lax.all_to_all(array, axes, 0, 0, tiled=True)  11.8 us
    pallas_call x13, Pallas kernels, call(): pl.pallas_call(kernel, out_shape=outs, in_specs=[space] * len(ins), out_s...  11.5 us
    ppermute x4, starting transfers between devices, swapped(): return lax.ppermute(array, axis, pairs + [(b, a) for a, b in pairs])  11.2 us
  transfers between devices with their start and end apart: 8, of which 4 were waited for; matrix products, arithmetic and copies ran while one was open for 0% of the time, Pallas kernels for 6%

profile of v6, /device:TPU:1, one launch (start us, length us, event | category | flops | bytes accessed | tf_op | source)
XLA Modules:
  0.0 88.3 jit_solution(5499369821101491897)
XLA Ops:
  0.6 2.2 %shard_map.68 = (f32[32,4,128]{2,1,0:T(4,128)}, f32[3,16,16,128]{3,2,1,0:T(8,128)S(1)}, f32[16,16,128]{2,1,0:T(8,128)S(1)}, f32[12,6144]{1,0:T(8,128)S(1)}, f32[12,128]{1,0:T(8,128)S(1)}) custom-call(f32[3,16,16,128]{3,2,1,0:T(8,128)} %r_ref.1, s32[16,16,128]{2,1,0:T(8,128)} %reg_hbm.1, f32[12,6144]{1,0:T(8,128)} %coarse_hbm.1), custom_call_target="tpu_custom_call" | custom-call | tf_op jit(solution)/shard_map/pallas_call | solution.py:28
  2.9 4.0 %collective-permute-start = (f32[3,16,4,128]{3,2,1,0:T(4,128)S(1)}, f32[3,16,4,128]{3,2,1,0:T(4,128)S(1)}, u32[]{:S(2)}, u32[]{:S(2)}) collective-permute-start(f32[3,16,4,128]{3,2,1,0:T(4,128)S(1)} %get-tuple-element.32), channel_id=1, source_target_pairs={{0,1},{2,3},{4,5},{6,7},{1,0},{3,2},{5,4},{7,6},{8,9},{10,11},{12,... | collective-permute-start | bytes 294920 | tf_op jit(solution)/shard_map/ppermute | solution.py:579
  7.0 0.7 collective-permute-start.1
  7.6 12.9 %all-to-all-start = ((f32[32,4,128]{2,1,0:T(4,128)}), f32[32,4,128]{2,1,0:T(4,128)S(1)}, u32[]{:S(2)}, u32[]{:S(2)}) async-start(f32[32,4,128]{2,1,0:T(4,128)} %get-tuple-element.27), calls=%async_computation | async-start | bytes 131072 | tf_op jit(solution)/shard_map/all_to_all | solution.py:573
  20.6 3.1 %collective-permute-start.2 = (f32[232,128]{1,0:T(8,128)S(1)}, f32[232,128]{1,0:T(8,128)S(1)}, u32[]{:S(2)}, u32[]{:S(2)}) collective-permute-start(f32[232,128]{1,0:T(8,128)S(1)} %get-tuple-element.34), channel_id=1, source_target_pairs={{0,8},{16,24},{32,40},{48,56},{64,72},{80,88},{96,104},{112,120},{... | collective-permute-start | bytes 356360 | tf_op jit(solution)/shard_map/ppermute | solution.py:579
  23.8 3.3 %collective-permute-start.3 = (f32[232,128]{1,0:T(8,128)S(1)}, f32[232,128]{1,0:T(8,128)S(1)}, u32[]{:S(2)}, u32[]{:S(2)}) collective-permute-start(f32[232,128]{1,0:T(8,128)S(1)} %get-tuple-element.35), channel_id=1, source_target_pairs={{8,16},{24,32},{40,48},{56,64},{72,80},{88,96},{104,112},{120,128}... | collective-permute-start | bytes 356360 | tf_op jit(solution)/shard_map/ppermute | solution.py:579
  27.1 2.3 %all-to-all-done.recv_ref = f32[32,4,128]{2,1,0:T(4,128)S(1)} async-done(((f32[32,4,128]{2,1,0:T(4,128)}), f32[32,4,128]{2,1,0:T(4,128)S(1)}, u32[]{:S(2)}, u32[]{:S(2)}) %all-to-all-start) | async-done | bytes 65568 | tf_op jit(solution)/shard_map/all_to_all | solution.py:573
  29.4 0.7 shard_map.69
  30.0 10.4 %all-to-all-start.1 = ((f32[16,4,128]{2,1,0:T(4,128)}), f32[16,4,128]{2,1,0:T(4,128)S(1)}, u32[]{:S(2)}, u32[]{:S(2)}) async-start(f32[16,4,128]{2,1,0:T(4,128)} %shard_map.69), calls=%async_computation.1 | async-start | bytes 65536 | tf_op jit(solution)/shard_map/all_to_all | solution.py:573
  40.5 0.4 shard_map.72
  40.9 0.7 shard_map.73.start_ref
  41.6 0.2 copy-done.1
  41.8 1.1 %shard_map.74 = (f32[3,128]{1,0:T(4,128)S(1)}, f32[3,12,128]{2,1,0:T(8,128)S(1)}) custom-call(f32[22,24,128]{2,1,0:T(8,128)S(1)} %get-tuple-element.36.k_ref, f32[22,24,128]{2,1,0:T(8,128)S(1)} %get-tuple-element.37.label_ref, f32[88,384]{1,0:T(8,128)S(1)} %copy-done.1), custom_call_target="tpu_custom_call" | custom-call | flops 3000000 | bytes 3000000 | tf_op jit(solution)/shard_map/pallas_call | solution.py:28
  42.9 4.6 %all-to-all-done.1.recv_ref = f32[16,4,128]{2,1,0:T(4,128)S(1)} async-done(((f32[16,4,128]{2,1,0:T(4,128)}), f32[16,4,128]{2,1,0:T(4,128)S(1)}, u32[]{:S(2)}, u32[]{:S(2)}) %all-to-all-start.1) | async-done | bytes 32800 | tf_op jit(solution)/shard_map/all_to_all | solution.py:573
  47.5 1.1 %shard_map.75 = (f32[32,4,128]{2,1,0:T(4,128)}, f32[1,128]{1,0:T(1,128)S(1)}, f32[3,128]{1,0:T(4,128)S(1)}) custom-call(f32[16,4,128]{2,1,0:T(4,128)S(1)} %all-to-all-done.1.recv_ref, f32[12,128]{1,0:T(8,128)S(1)} %get-tuple-element.28.rc_ref, f32[14,128]{1,0:T(8,128)S(1)} %shard_map.73.start_ref, f32[3,12,128]{2,1,0:T(8,128)S(1)} %get-tuple-element.39.rows_ref, ...), custom_call_target="tpu_custom_call" | custom-call | tf_op jit(solution)/shard_map/pallas_call | solution.py:28
  48.6 4.1 %all-to-all-start.2 = ((f32[32,4,128]{2,1,0:T(4,128)}), f32[32,4,128]{2,1,0:T(4,128)S(1)}, u32[]{:S(2)}, u32[]{:S(2)}) async-start(f32[32,4,128]{2,1,0:T(4,128)} %get-tuple-element.41), calls=%async_computation.2 | async-start | bytes 131072 | tf_op jit(solution)/shard_map/all_to_all | solution.py:573
  52.7 1.9 %shard_map.76 = (f32[3,22,24,128]{3,2,1,0:T(8,128)S(1)}, f32[3,18,24,128]{3,2,1,0:T(8,128)S(1)}, f32[1,128]{1,0:T(1,128)S(1)}) custom-call(f32[3,128]{1,0:T(4,128)S(1)} %get-tuple-element.42.near_ref, f32[22,24,128]{2,1,0:T(8,128)S(1)} %get-tuple-element.36.k_ref, f32[22,24,128]{2,1,0:T(8,128)S(1)} %get-tuple-element.37.label_ref, ...), custom_call_target="tpu_custom_call", output_to_operand_aliasing={{0}: (4, {})} | custom-call | flops 3000000 | bytes 3000000 | tf_op jit(solution)/shard_map/pallas_call | solution.py:28
  54.6 6.9 %all-to-all-done.2.recv_ref = f32[32,4,128]{2,1,0:T(4,128)S(1)} async-done(((f32[32,4,128]{2,1,0:T(4,128)}), f32[32,4,128]{2,1,0:T(4,128)S(1)}, u32[]{:S(2)}, u32[]{:S(2)}) %all-to-all-start.2) | async-done | bytes 65568 | tf_op jit(solution)/shard_map/all_to_all | solution.py:573
  61.6 11.8 %all_to_all.25.recv_ref = f32[16,8,128]{2,1,0:T(8,128)S(1)} all-to-all(f32[16,8,128]{2,1,0:T(8,128)S(1)} %shard_map.77), channel_id=1, replica_groups=mesh['x'=4,'z'=8,'c'=2,'y'=8] {'c','y'}, dimensions={0} | all-to-all | bytes 131072 | tf_op jit(solution)/shard_map/all_to_all | solution.py:573
  73.4 1.1 %shard_map.78 = f32[32,1,128]{2,1,0:T(1,128)} custom-call(f32[16,8,128]{2,1,0:T(8,128)S(1)} %all_to_all.25.recv_ref), custom_call_target="tpu_custom_call" | custom-call | tf_op jit(solution)/shard_map/pallas_call | solution.py:28
  74.5 3.8 %all-to-all-start.4 = ((f32[32,1,128]{2,1,0:T(1,128)}), f32[32,1,128]{2,1,0:T(1,128)S(1)}, u32[]{:S(2)}, u32[]{:S(2)}) async-start(f32[32,1,128]{2,1,0:T(1,128)} %shard_map.78), calls=%async_computation.4 | async-start | bytes 32768 | tf_op jit(solution)/shard_map/all_to_all | solution.py:573
  78.3 0.8 shard_map.79
  79.2 7.7 %all-to-all-done.4.recv_ref = f32[32,1,128]{2,1,0:T(1,128)S(1)} async-done(((f32[32,1,128]{2,1,0:T(1,128)}), f32[32,1,128]{2,1,0:T(1,128)S(1)}, u32[]{:S(2)}, u32[]{:S(2)}) %all-to-all-start.4) | async-done | bytes 16416 | tf_op jit(solution)/shard_map/all_to_all | solution.py:573
  86.9 1.4 %shard_map.80 = (f32[3,16,16,128]{3,2,1,0:T(8,128)}, f32[3,16,16,128]{3,2,1,0:T(8,128)}) custom-call(f32[32,1,128]{2,1,0:T(1,128)S(1)} %all-to-all-done.4.recv_ref, f32[1,128]{1,0:T(1,128)S(1)} %get-tuple-element.49.scal_ref, f32[3,16,16,128]{3,2,1,0:T(8,128)S(1)} %copy-done, f32[3,22,24,128]{3,2,1,0:T(8,128)S(1)} %get-tuple-element.47.z_ref, ...), custom_call_target="tpu_custom_call" | custom-call | tf_op jit(solution)/shard_map/pallas_call | solution.py:28
  (12 shorter events, 0.2 us)
Async XLA Ops:
  0.6 2.2 %copy-start.2 = (s32[16,16,128]{2,1,0:T(8,128)S(1)}, s32[16,16,128]{2,1,0:T(8,128)}, u32[]{:S(2)}) copy-start(s32[16,16,128]{2,1,0:T(8,128)} %occ_ref.1) | copy-start | bytes 393220
  2.9 17.6 %collective-permute-start = (f32[3,16,4,128]{3,2,1,0:T(4,128)S(1)}, f32[3,16,4,128]{3,2,1,0:T(4,128)S(1)}, u32[]{:S(2)}, u32[]{:S(2)}) collective-permute-start(f32[3,16,4,128]{3,2,1,0:T(4,128)S(1)} %get-tuple-element.32), channel_id=1, source_target_pairs={{0,1},{2,3},{4,5},{6,7},{1,0},{3,2},{5,4},{7,6},{8,9},{10,11},{12,... | collective-permute-start | bytes 294920 | tf_op jit(solution)/shard_map/ppermute | solution.py:579
  7.0 13.6 %collective-permute-start.1 = (f32[3,16,4,128]{3,2,1,0:T(4,128)S(1)}, f32[3,16,4,128]{3,2,1,0:T(4,128)S(1)}, u32[]{:S(2)}, u32[]{:S(2)}) collective-permute-start(f32[3,16,4,128]{3,2,1,0:T(4,128)S(1)} %get-tuple-element.33), channel_id=1, source_target_pairs={{1,2},{3,4},{5,6},{2,1},{4,3},{6,5},{9,10},{11,12},{13,14},{10,9},... | collective-permute-start | bytes 294920 | tf_op jit(solution)/shard_map/ppermute | solution.py:579
  7.6 21.8 %all-to-all-start = ((f32[32,4,128]{2,1,0:T(4,128)}), f32[32,4,128]{2,1,0:T(4,128)S(1)}, u32[]{:S(2)}, u32[]{:S(2)}) async-start(f32[32,4,128]{2,1,0:T(4,128)} %get-tuple-element.27), calls=%async_computation | async-start | bytes 131072 | tf_op jit(solution)/shard_map/all_to_all | solution.py:573
  20.6 19.9 %collective-permute-start.2 = (f32[232,128]{1,0:T(8,128)S(1)}, f32[232,128]{1,0:T(8,128)S(1)}, u32[]{:S(2)}, u32[]{:S(2)}) collective-permute-start(f32[232,128]{1,0:T(8,128)S(1)} %get-tuple-element.34), channel_id=1, source_target_pairs={{0,8},{16,24},{32,40},{48,56},{64,72},{80,88},{96,104},{112,120},{... | collective-permute-start | bytes 356360 | tf_op jit(solution)/shard_map/ppermute | solution.py:579
  23.8 16.7 %collective-permute-start.3 = (f32[232,128]{1,0:T(8,128)S(1)}, f32[232,128]{1,0:T(8,128)S(1)}, u32[]{:S(2)}, u32[]{:S(2)}) collective-permute-start(f32[232,128]{1,0:T(8,128)S(1)} %get-tuple-element.35), channel_id=1, source_target_pairs={{8,16},{24,32},{40,48},{56,64},{72,80},{88,96},{104,112},{120,128}... | collective-permute-start | bytes 356360 | tf_op jit(solution)/shard_map/ppermute | solution.py:579
  30.0 17.5 %all-to-all-start.1 = ((f32[16,4,128]{2,1,0:T(4,128)}), f32[16,4,128]{2,1,0:T(4,128)S(1)}, u32[]{:S(2)}, u32[]{:S(2)}) async-start(f32[16,4,128]{2,1,0:T(4,128)} %shard_map.69), calls=%async_computation.1 | async-start | bytes 65536 | tf_op jit(solution)/shard_map/all_to_all | solution.py:573
  40.9 0.9 %copy-start.1 = (f32[88,384]{1,0:T(8,128)S(1)}, f32[88,384]{1,0:T(8,128)}, u32[]{:S(2)}) copy-start(f32[88,384]{1,0:T(8,128)} %constant.2.clone.select_ref) | copy-start | bytes 405508
  48.6 12.9 %all-to-all-start.2 = ((f32[32,4,128]{2,1,0:T(4,128)}), f32[32,4,128]{2,1,0:T(4,128)S(1)}, u32[]{:S(2)}, u32[]{:S(2)}) async-start(f32[32,4,128]{2,1,0:T(4,128)} %get-tuple-element.41), calls=%async_computation.2 | async-start | bytes 131072 | tf_op jit(solution)/shard_map/all_to_all | solution.py:573
  74.5 12.4 %all-to-all-start.4 = ((f32[32,1,128]{2,1,0:T(1,128)}), f32[32,1,128]{2,1,0:T(1,128)S(1)}, u32[]{:S(2)}, u32[]{:S(2)}) async-start(f32[32,1,128]{2,1,0:T(1,128)} %shard_map.78), calls=%async_computation.4 | async-start | bytes 32768 | tf_op jit(solution)/shard_map/all_to_all | solution.py:573
  78.3 8.6 %copy-start = (f32[3,16,16,128]{3,2,1,0:T(8,128)S(1)}, f32[3,16,16,128]{3,2,1,0:T(8,128)}, u32[]{:S(2)}) copy-start(f32[3,16,16,128]{3,2,1,0:T(8,128)} %r_ref.1) | copy-start | bytes 1179652

commit v7 on v6

--- a/solution.py
+++ b/solution.py
@@ -18,6 +18,7 @@
 VMEM = pl.BlockSpec(memory_space=pltpu.VMEM)
 HBM = pl.BlockSpec(memory_space=pltpu.HBM)
 PARTS = 4
+CHUNK = 8
 
 
 def shape(*dims):
@@ -29,7 +30,7 @@
         kernel,
         out_shape=outs,
         in_specs=[space] * len(ins),
-        out_specs=jax.tree.map(lambda _: target, outs),
+        out_specs=target if isinstance(target, tuple) else jax.tree.map(lambda _: target, outs),
         scratch_shapes=list(scratch),
         input_output_aliases=alias or {},
         cost_estimate=pl.CostEstimate(flops=cost, bytes_accessed=cost, transcendentals=0) if cost else None,
@@ -66,7 +67,7 @@
     return jnp.sum(jnp.where(lane == row + at, lanes, 0.0), axis=1, keepdims=True)
 
 
-def fold(rc, coarse_ref, u_ref, pad_ref, out_ref, sums=()):
+def fold(rc, coarse_ref, u_ref, pad_ref, send_ref, sems, out_ref, sums=()):
     u_ref[...] = jnp.sum(coarse_ref[...] * rc, axis=0, keepdims=True)
     pad_ref[...] = jnp.zeros_like(pad_ref)
     for w in range(2 * NROWS):
@@ -77,16 +78,24 @@
         for i, s in enumerate(sums):
             row = jnp.where(lane == SLAB + i, s, row)
         tail = jnp.broadcast_to(row, (4, 128))
+    copies = []
     for n in range(NROWS):
         window = pad_ref[2 * n : 2 * n + 4, :]
         if sums:
             window = window + tail
-        out_ref[n] = window
+        send_ref[n] = window
+        if n % CHUNK == CHUNK - 1:
+            part = pl.ds(n + 1 - CHUNK, CHUNK)
+            copies.append(pltpu.make_async_copy(send_ref.at[part], out_ref.at[part], sems.at[n // CHUNK]))
+            copies[-1].start()
+    return copies
 
 
 FOLD_SCRATCH = (
     pltpu.VMEM((1, 6144), F32),
     pltpu.VMEM((72, 128), F32),
+    pltpu.VMEM((NROWS, 4, 128), F32),
+    pltpu.SemaphoreType.DMA((NROWS // 8,)),
 )
 
 
@@ -95,11 +104,11 @@
 
 
 def first_kernel(
-    r_hbm, reg_hbm, coarse_hbm,
-    out_ref, r_ref, label_ref, coarse_ref, rc_ref,
-    reg_ref, acc_ref, u_ref, pad_ref, sems,
+    r_hbm, reg_hbm, coarse_hbm, occ_hbm,
+    out_hbm, r_ref, label_ref, coarse_ref, rc_ref, k_ref, a_ref, b_ref,
+    reg_ref, occ_ref, acc_ref, sems, u_ref, pad_ref, send_ref, send_sems,
 ):
-    pairs = ((r_hbm, r_ref), (reg_hbm, reg_ref), (coarse_hbm, coarse_ref))
+    pairs = ((r_hbm, r_ref), (reg_hbm, reg_ref), (coarse_hbm, coarse_ref), (occ_hbm, occ_ref))
     copies = [pltpu.make_async_copy(a, b, sems.at[i]) for i, (a, b) in enumerate(pairs)]
     for copy in copies:
         copy.start()
@@ -118,10 +127,8 @@
     rc = totals(acc_ref)
     rc_ref[...] = jnp.broadcast_to(rc, (12, 128))
     copies[2].wait()
-    fold(rc, coarse_ref, u_ref, pad_ref, out_ref)
-
-
-def edge_kernel(occ_ref, label_ref, r_ref, k_ref, a_ref, b_ref):
+    sends = fold(rc, coarse_ref, u_ref, pad_ref, send_ref, send_sems, out_hbm)
+    copies[3].wait()
     k_ref[...] = 0.1 + 0.9 * occ_ref[...].astype(F32)
     even = even_column()
     for ref, last in ((a_ref, even), (b_ref, jnp.logical_not(even))):
@@ -129,6 +136,8 @@
         for i, field in enumerate([label_ref] + [r_ref.at[c] for c in range(3)]):
             at = 2 * (i % 2)
             ref[1 + i // 2, :, at : at + 2] = jnp.where(last, field[:, 14:16, :], field[:, 0:2, :])
+    for copy in sends:
+        copy.wait()
 
 
 def tail_rows(a_ref, b_ref, i, planes):
@@ -300,7 +309,10 @@
     out_ref[...] = jnp.broadcast_to(totals(acc_ref), (14, 128))
 
 
-def second_kernel(recv_ref, rc_ref, start_ref, rows_ref, coarse_ref, out_ref, own_ref, near_ref, u_ref, pad_ref):
+def second_kernel(
+    recv_ref, rc_ref, start_ref, rows_ref, coarse_ref,
+    out_hbm, own_ref, near_ref, u_ref, pad_ref, send_ref, send_sems,
+):
     near = around(jnp.sum(recv_ref[...], axis=0))
     near_ref[...] = near
     product = rows_ref[0] * near[0:1] + rows_ref[1] * near[1:2] + rows_ref[2] * near[2:3]
@@ -309,8 +321,10 @@
     q = in_rows(near[1:2], 12)
     rz = start_ref[12:13, 0:1] + jnp.sum(rc_ref[:, 0:1] * q, axis=0, keepdims=True)
     zw = start_ref[13:14, 0:1] + jnp.sum(q * (e + aggregates), axis=0, keepdims=True)
-    fold(aggregates, coarse_ref, u_ref, pad_ref, out_ref, (rz, zw))
+    sends = fold(aggregates, coarse_ref, u_ref, pad_ref, send_ref, send_sems, out_hbm, (rz, zw))
     own_ref[...] = in_lanes(aggregates, 12)
+    for copy in sends:
+        copy.wait()
 
 
 def selection():
@@ -581,23 +595,28 @@
 
 def local(right, occ, reg, coarse):
     field, plane = (16, 16, 128), (24, 128)
-    send, r, label_own, coarse, rc = call(
+    send, r, label_own, coarse, rc, k_own, one, two = call(
         first_kernel,
-        (shape(NROWS, 4, 128), shape(3, *field), shape(*field), shape(12, 6144), shape(12, 128)),
-        tuple(pltpu.with_memory_space_constraint(a, pltpu.HBM) for a in (right, reg, coarse)),
+        (
+            shape(NROWS, 4, 128),
+            shape(3, *field),
+            shape(*field),
+            shape(12, 6144),
+            shape(12, 128),
+            shape(*field),
+            shape(3, 16, 4, 128),
+            shape(3, 16, 4, 128),
+        ),
+        tuple(pltpu.with_memory_space_constraint(a, pltpu.HBM) for a in (right, reg, coarse, occ)),
         (
             pltpu.VMEM(field, jnp.int32),
+            pltpu.VMEM(field, jnp.int32),
             pltpu.VMEM((12, 16, 128), F32),
+            pltpu.SemaphoreType.DMA((4,)),
             *FOLD_SCRATCH,
-            pltpu.SemaphoreType.DMA((3,)),
         ),
         space=HBM,
-    )
-    k_own, one, two = call(
-        edge_kernel,
-        (shape(*field), shape(3, 16, 4, 128), shape(3, 16, 4, 128)),
-        (occ, label_own, r),
-        cost=3000000,
+        target=(HBM,) + (VMEM,) * 7,
     )
     one = swapped(one, "y", 0)
     two = swapped(two, "y", 1)
@@ -628,6 +647,7 @@
         (shape(NROWS, 4, 128), shape(1, 128), shape(3, 128)),
         (got, rc, start, rows, coarse),
         FOLD_SCRATCH,
+        target=(HBM, VMEM, VMEM),
     )
     got = exchange(send, ROWS)
     z, w, own = call(

time: 88.8 us -> 88.7 us (level)
    pallas_call x13 -> x12, Pallas kernels: 11.5 us -> 11.4 us  [call(): pl.pallas_call(kernel, out_shape=outs, in_specs=[space] * len(ins), out_s...]
where the time goes in v7:
time: 88.7 us; the launch traced here: 88.2 us
  starting transfers between devices  42.4 us (48%)
  waiting for transfers between devices  21.6 us (24%)
  blocking collectives  11.8 us (13%)
  Pallas kernels  11.4 us (13%)
    all_to_all x4, starting transfers between devices, exchange(): return lax.all_to_all(array, axes, 0, 0, tiled=True)  31.2 us
    all_to_all x4, waiting for transfers between devices, exchange(): return lax.all_to_all(array, axes, 0, 0, tiled=True)  21.6 us
    all_to_all x1, blocking collectives, exchange(): return lax.all_to_all(array, axes, 0, 0, tiled=True)  11.8 us
    pallas_call x12, Pallas kernels, call(): pl.pallas_call(kernel, out_shape=outs, in_specs=[space] * len(ins), out_s...  11.4 us
    ppermute x4, starting transfers between devices, swapped(): return lax.ppermute(array, axis, pairs + [(b, a) for a, b in pairs])  11.2 us
  transfers between devices with their start and end apart: 8, of which 4 were waited for; matrix products, arithmetic and copies ran while one was open for 0% of the time, Pallas kernels for 6%

profile of v7, /device:TPU:1, one launch (start us, length us, event | category | flops | bytes accessed | tf_op | source)
XLA Modules:
  0.0 88.2 jit_solution(3822845254731637807)
XLA Ops:
  0.6 2.1 %shard_map.68 = (f32[32,4,128]{2,1,0:T(4,128)}, f32[3,16,16,128]{3,2,1,0:T(8,128)S(1)}, f32[16,16,128]{2,1,0:T(8,128)S(1)}, f32[12,6144]{1,0:T(8,128)S(1)}, f32[...) custom-call(f32[3,16,16,128]{3,2,1,0:T(8,128)} %r_ref.1, ...), custom_call_target="tpu_custom_call" | custom-call | tf_op jit(solution)/shard_map/pallas_call | solution.py:29
  2.8 4.0 %collective-permute-start = (f32[3,16,4,128]{3,2,1,0:T(4,128)S(1)}, f32[3,16,4,128]{3,2,1,0:T(4,128)S(1)}, u32[]{:S(2)}, u32[]{:S(2)}) collective-permute-start(f32[3,16,4,128]{3,2,1,0:T(4,128)S(1)} %get-tuple-element.32), channel_id=1, source_target_pairs={{0,1},{2,3},{4,5},{6,7},{1,0},{3,2},{5,4},{7,6},{8,9},{10,11},{12,... | collective-permute-start | bytes 294920 | tf_op jit(solution)/shard_map/ppermute | solution.py:593
  6.8 0.7 collective-permute-start.1
  7.5 12.9 %all-to-all-start = ((f32[32,4,128]{2,1,0:T(4,128)}), f32[32,4,128]{2,1,0:T(4,128)S(1)}, u32[]{:S(2)}, u32[]{:S(2)}) async-start(f32[32,4,128]{2,1,0:T(4,128)} %get-tuple-element.27), calls=%async_computation | async-start | bytes 131072 | tf_op jit(solution)/shard_map/all_to_all | solution.py:587
  20.5 3.1 %collective-permute-start.2 = (f32[232,128]{1,0:T(8,128)S(1)}, f32[232,128]{1,0:T(8,128)S(1)}, u32[]{:S(2)}, u32[]{:S(2)}) collective-permute-start(f32[232,128]{1,0:T(8,128)S(1)} %get-tuple-element.34), channel_id=1, source_target_pairs={{0,8},{16,24},{32,40},{48,56},{64,72},{80,88},{96,104},{112,120},{... | collective-permute-start | bytes 356360 | tf_op jit(solution)/shard_map/ppermute | solution.py:593
  23.6 3.3 %collective-permute-start.3 = (f32[232,128]{1,0:T(8,128)S(1)}, f32[232,128]{1,0:T(8,128)S(1)}, u32[]{:S(2)}, u32[]{:S(2)}) collective-permute-start(f32[232,128]{1,0:T(8,128)S(1)} %get-tuple-element.35), channel_id=1, source_target_pairs={{8,16},{24,32},{40,48},{56,64},{72,80},{88,96},{104,112},{120,128}... | collective-permute-start | bytes 356360 | tf_op jit(solution)/shard_map/ppermute | solution.py:593
  26.9 2.3 %all-to-all-done.recv_ref = f32[32,4,128]{2,1,0:T(4,128)S(1)} async-done(((f32[32,4,128]{2,1,0:T(4,128)}), f32[32,4,128]{2,1,0:T(4,128)S(1)}, u32[]{:S(2)}, u32[]{:S(2)}) %all-to-all-start) | async-done | bytes 65568 | tf_op jit(solution)/shard_map/all_to_all | solution.py:587
  29.3 0.7 shard_map.69
  29.9 10.4 %all-to-all-start.1 = ((f32[16,4,128]{2,1,0:T(4,128)}), f32[16,4,128]{2,1,0:T(4,128)S(1)}, u32[]{:S(2)}, u32[]{:S(2)}) async-start(f32[16,4,128]{2,1,0:T(4,128)} %shard_map.69), calls=%async_computation.1 | async-start | bytes 65536 | tf_op jit(solution)/shard_map/all_to_all | solution.py:587
  40.4 0.4 shard_map.71
  40.8 0.7 shard_map.72.start_ref
  41.5 0.2 copy-done.1
  41.7 1.1 %shard_map.73 = (f32[3,128]{1,0:T(4,128)S(1)}, f32[3,12,128]{2,1,0:T(8,128)S(1)}) custom-call(f32[22,24,128]{2,1,0:T(8,128)S(1)} %get-tuple-element.36.k_ref, f32[22,24,128]{2,1,0:T(8,128)S(1)} %get-tuple-element.37.label_ref, f32[88,384]{1,0:T(8,128)S(1)} %copy-done.1), custom_call_target="tpu_custom_call" | custom-call | flops 3000000 | bytes 3000000 | tf_op jit(solution)/shard_map/pallas_call | solution.py:29
  42.7 4.6 %all-to-all-done.1.recv_ref = f32[16,4,128]{2,1,0:T(4,128)S(1)} async-done(((f32[16,4,128]{2,1,0:T(4,128)}), f32[16,4,128]{2,1,0:T(4,128)S(1)}, u32[]{:S(2)}, u32[]{:S(2)}) %all-to-all-start.1) | async-done | bytes 32800 | tf_op jit(solution)/shard_map/all_to_all | solution.py:587
  47.4 1.1 %shard_map.74 = (f32[32,4,128]{2,1,0:T(4,128)}, f32[1,128]{1,0:T(1,128)S(1)}, f32[3,128]{1,0:T(4,128)S(1)}) custom-call(f32[16,4,128]{2,1,0:T(4,128)S(1)} %all-to-all-done.1.recv_ref, f32[12,128]{1,0:T(8,128)S(1)} %get-tuple-element.28.rc_ref, f32[14,128]{1,0:T(8,128)S(1)} %shard_map.72.start_ref, f32[3,12,128]{2,1,0:T(8,128)S(1)} %get-tuple-element.39.rows_ref, ...), custom_call_target="tpu_custom_call" | custom-call | tf_op jit(solution)/shard_map/pallas_call | solution.py:29
  48.5 4.1 %all-to-all-start.2 = ((f32[32,4,128]{2,1,0:T(4,128)}), f32[32,4,128]{2,1,0:T(4,128)S(1)}, u32[]{:S(2)}, u32[]{:S(2)}) async-start(f32[32,4,128]{2,1,0:T(4,128)} %get-tuple-element.41), calls=%async_computation.2 | async-start | bytes 131072 | tf_op jit(solution)/shard_map/all_to_all | solution.py:587
  52.6 1.9 %shard_map.75 = (f32[3,22,24,128]{3,2,1,0:T(8,128)S(1)}, f32[3,18,24,128]{3,2,1,0:T(8,128)S(1)}, f32[1,128]{1,0:T(1,128)S(1)}) custom-call(f32[3,128]{1,0:T(4,128)S(1)} %get-tuple-element.42.near_ref, f32[22,24,128]{2,1,0:T(8,128)S(1)} %get-tuple-element.36.k_ref, f32[22,24,128]{2,1,0:T(8,128)S(1)} %get-tuple-element.37.label_ref, ...), custom_call_target="tpu_custom_call", output_to_operand_aliasing={{0}: (4, {})} | custom-call | flops 3000000 | bytes 3000000 | tf_op jit(solution)/shard_map/pallas_call | solution.py:29
  54.5 6.9 %all-to-all-done.2.recv_ref = f32[32,4,128]{2,1,0:T(4,128)S(1)} async-done(((f32[32,4,128]{2,1,0:T(4,128)}), f32[32,4,128]{2,1,0:T(4,128)S(1)}, u32[]{:S(2)}, u32[]{:S(2)}) %all-to-all-start.2) | async-done | bytes 65568 | tf_op jit(solution)/shard_map/all_to_all | solution.py:587
  61.5 11.8 %all_to_all.25.recv_ref = f32[16,8,128]{2,1,0:T(8,128)S(1)} all-to-all(f32[16,8,128]{2,1,0:T(8,128)S(1)} %shard_map.76), channel_id=1, replica_groups=mesh['x'=4,'z'=8,'c'=2,'y'=8] {'c','y'}, dimensions={0} | all-to-all | bytes 131072 | tf_op jit(solution)/shard_map/all_to_all | solution.py:587
  73.3 1.1 %shard_map.77 = f32[32,1,128]{2,1,0:T(1,128)} custom-call(f32[16,8,128]{2,1,0:T(8,128)S(1)} %all_to_all.25.recv_ref), custom_call_target="tpu_custom_call" | custom-call | tf_op jit(solution)/shard_map/pallas_call | solution.py:29
  74.4 3.8 %all-to-all-start.4 = ((f32[32,1,128]{2,1,0:T(1,128)}), f32[32,1,128]{2,1,0:T(1,128)S(1)}, u32[]{:S(2)}, u32[]{:S(2)}) async-start(f32[32,1,128]{2,1,0:T(1,128)} %shard_map.77), calls=%async_computation.4 | async-start | bytes 32768 | tf_op jit(solution)/shard_map/all_to_all | solution.py:587
  78.2 0.8 shard_map.78
  79.1 7.7 %all-to-all-done.4.recv_ref = f32[32,1,128]{2,1,0:T(1,128)S(1)} async-done(((f32[32,1,128]{2,1,0:T(1,128)}), f32[32,1,128]{2,1,0:T(1,128)S(1)}, u32[]{:S(2)}, u32[]{:S(2)}) %all-to-all-start.4) | async-done | bytes 16416 | tf_op jit(solution)/shard_map/all_to_all | solution.py:587
  86.8 1.4 %shard_map.79 = (f32[3,16,16,128]{3,2,1,0:T(8,128)}, f32[3,16,16,128]{3,2,1,0:T(8,128)}) custom-call(f32[32,1,128]{2,1,0:T(1,128)S(1)} %all-to-all-done.4.recv_ref, f32[1,128]{1,0:T(1,128)S(1)} %get-tuple-element.49.scal_ref, f32[3,16,16,128]{3,2,1,0:T(8,128)S(1)} %copy-done, f32[3,22,24,128]{3,2,1,0:T(8,128)S(1)} %get-tuple-element.47.z_ref, ...), custom_call_target="tpu_custom_call" | custom-call | tf_op jit(solution)/shard_map/pallas_call | solution.py:29
  (9 shorter events, 0.1 us)
Async XLA Ops:
  2.8 17.6 %collective-permute-start = (f32[3,16,4,128]{3,2,1,0:T(4,128)S(1)}, f32[3,16,4,128]{3,2,1,0:T(4,128)S(1)}, u32[]{:S(2)}, u32[]{:S(2)}) collective-permute-start(f32[3,16,4,128]{3,2,1,0:T(4,128)S(1)} %get-tuple-element.32), channel_id=1, source_target_pairs={{0,1},{2,3},{4,5},{6,7},{1,0},{3,2},{5,4},{7,6},{8,9},{10,11},{12,... | collective-permute-start | bytes 294920 | tf_op jit(solution)/shard_map/ppermute | solution.py:593
  6.8 13.6 %collective-permute-start.1 = (f32[3,16,4,128]{3,2,1,0:T(4,128)S(1)}, f32[3,16,4,128]{3,2,1,0:T(4,128)S(1)}, u32[]{:S(2)}, u32[]{:S(2)}) collective-permute-start(f32[3,16,4,128]{3,2,1,0:T(4,128)S(1)} %get-tuple-element.33), channel_id=1, source_target_pairs={{1,2},{3,4},{5,6},{2,1},{4,3},{6,5},{9,10},{11,12},{13,14},{10,9},... | collective-permute-start | bytes 294920 | tf_op jit(solution)/shard_map/ppermute | solution.py:593
  7.5 21.8 %all-to-all-start = ((f32[32,4,128]{2,1,0:T(4,128)}), f32[32,4,128]{2,1,0:T(4,128)S(1)}, u32[]{:S(2)}, u32[]{:S(2)}) async-start(f32[32,4,128]{2,1,0:T(4,128)} %get-tuple-element.27), calls=%async_computation | async-start | bytes 131072 | tf_op jit(solution)/shard_map/all_to_all | solution.py:587
  20.5 19.9 %collective-permute-start.2 = (f32[232,128]{1,0:T(8,128)S(1)}, f32[232,128]{1,0:T(8,128)S(1)}, u32[]{:S(2)}, u32[]{:S(2)}) collective-permute-start(f32[232,128]{1,0:T(8,128)S(1)} %get-tuple-element.34), channel_id=1, source_target_pairs={{0,8},{16,24},{32,40},{48,56},{64,72},{80,88},{96,104},{112,120},{... | collective-permute-start | bytes 356360 | tf_op jit(solution)/shard_map/ppermute | solution.py:593
  23.6 16.7 %collective-permute-start.3 = (f32[232,128]{1,0:T(8,128)S(1)}, f32[232,128]{1,0:T(8,128)S(1)}, u32[]{:S(2)}, u32[]{:S(2)}) collective-permute-start(f32[232,128]{1,0:T(8,128)S(1)} %get-tuple-element.35), channel_id=1, source_target_pairs={{8,16},{24,32},{40,48},{56,64},{72,80},{88,96},{104,112},{120,128}... | collective-permute-start | bytes 356360 | tf_op jit(solution)/shard_map/ppermute | solution.py:593
  29.9 17.5 %all-to-all-start.1 = ((f32[16,4,128]{2,1,0:T(4,128)}), f32[16,4,128]{2,1,0:T(4,128)S(1)}, u32[]{:S(2)}, u32[]{:S(2)}) async-start(f32[16,4,128]{2,1,0:T(4,128)} %shard_map.69), calls=%async_computation.1 | async-start | bytes 65536 | tf_op jit(solution)/shard_map/all_to_all | solution.py:587
  40.8 0.9 %copy-start.1 = (f32[88,384]{1,0:T(8,128)S(1)}, f32[88,384]{1,0:T(8,128)}, u32[]{:S(2)}) copy-start(f32[88,384]{1,0:T(8,128)} %constant.2.clone.select_ref) | copy-start | bytes 405508
  48.5 13.0 %all-to-all-start.2 = ((f32[32,4,128]{2,1,0:T(4,128)}), f32[32,4,128]{2,1,0:T(4,128)S(1)}, u32[]{:S(2)}, u32[]{:S(2)}) async-start(f32[32,4,128]{2,1,0:T(4,128)} %get-tuple-element.41), calls=%async_computation.2 | async-start | bytes 131072 | tf_op jit(solution)/shard_map/all_to_all | solution.py:587
  74.4 12.4 %all-to-all-start.4 = ((f32[32,1,128]{2,1,0:T(1,128)}), f32[32,1,128]{2,1,0:T(1,128)S(1)}, u32[]{:S(2)}, u32[]{:S(2)}) async-start(f32[32,1,128]{2,1,0:T(1,128)} %shard_map.77), calls=%async_computation.4 | async-start | bytes 32768 | tf_op jit(solution)/shard_map/all_to_all | solution.py:587
  78.2 8.6 %copy-start = (f32[3,16,16,128]{3,2,1,0:T(8,128)S(1)}, f32[3,16,16,128]{3,2,1,0:T(8,128)}, u32[]{:S(2)}) copy-start(f32[3,16,16,128]{3,2,1,0:T(8,128)} %r_ref.1) | copy-start | bytes 1179652

commit v8 on v7

--- a/solution.py
+++ b/solution.py
@@ -177,7 +177,7 @@
     core = lax.axis_index("c")
 
     def sides(rows):
-        one, two = first_ref[rows], second_ref[rows]
+        one, two = first_ref[1 - core, rows], second_ref[rows]
         return jnp.where(core == 0, two, one), jnp.where(core == 0, one, two)
 
     k_ref[3:19, 0:16] = k_own_ref[...]
@@ -624,7 +624,7 @@
     first, second = call(
         pack_kernel, (shape(PACK, 128), shape(PACK, 128)), (k_own, label_own, r, one, two), cost=1000000
     )
-    first = swapped(first, WIDE, 0)
+    first = lax.all_gather(first, "c")
     second = swapped(second, WIDE, 1)
     send = call(around_kernel, shape(NCOLS, 4, 128), (got,))
     got = exchange(send, COLS)

time: 88.7 us -> 89.3 us (level)
  blocking collectives: 11.8 us -> 14.6 us
  starting transfers between devices: 42.4 us -> 40.3 us
    all_gather x0 -> x1, blocking collectives: none -> 1.96 us  [local(): first = lax.all_gather(first, 'c')]
    ppermute x4 -> x3, starting transfers between devices: 11.2 us -> 9.24 us  [swapped(): return lax.ppermute(array, axis, pairs + [(b, a) for a, b in pairs])]
  transfers between devices with their start and end apart: 8 -> 7, of which waited for: 4 -> 4; matrix products, arithmetic and copies ran while one was open for 0% -> 0% of each run, Pallas kernels for 6% -> 6%
where the time goes in v8:
time: 89.3 us; the launch traced here: 88.8 us
  starting transfers between devices  40.3 us (45%)
  waiting for transfers between devices  21.6 us (24%)
  blocking collectives  14.6 us (16%)
  Pallas kernels  11.4 us (13%)
    all_to_all x4, starting transfers between devices, exchange(): return lax.all_to_all(array, axes, 0, 0, tiled=True)  31 us
    all_to_all x4, waiting for transfers between devices, exchange(): return lax.all_to_all(array, axes, 0, 0, tiled=True)  21.6 us
    all_to_all x1, blocking collectives, exchange(): return lax.all_to_all(array, axes, 0, 0, tiled=True)  12.6 us
    pallas_call x12, Pallas kernels, call(): pl.pallas_call(kernel, out_shape=outs, in_specs=[space] * len(ins), out_s...  11.4 us
    ppermute x3, starting transfers between devices, swapped(): return lax.ppermute(array, axis, pairs + [(b, a) for a, b in pairs])  9.24 us
    all_gather x1, blocking collectives, local(): first = lax.all_gather(first, 'c')  1.96 us
  transfers between devices with their start and end apart: 7, of which 4 were waited for; matrix products, arithmetic and copies ran while one was open for 0% of the time, Pallas kernels for 6%

profile of v8, /device:TPU:1, one launch (start us, length us, event | category | flops | bytes accessed | tf_op | source)
XLA Modules:
  0.0 88.8 jit_solution(841662758795428183)
XLA Ops:
  0.6 2.1 %shard_map.68 = (f32[32,4,128]{2,1,0:T(4,128)}, f32[3,16,16,128]{3,2,1,0:T(8,128)S(1)}, f32[16,16,128]{2,1,0:T(8,128)S(1)}, f32[12,6144]{1,0:T(8,128)S(1)}, f32[...) custom-call(f32[3,16,16,128]{3,2,1,0:T(8,128)} %r_ref.1, ...), custom_call_target="tpu_custom_call" | custom-call | tf_op jit(solution)/shard_map/pallas_call | solution.py:29
  2.8 4.0 %collective-permute-start = (f32[3,16,4,128]{3,2,1,0:T(4,128)S(1)}, f32[3,16,4,128]{3,2,1,0:T(4,128)S(1)}, u32[]{:S(2)}, u32[]{:S(2)}) collective-permute-start(f32[3,16,4,128]{3,2,1,0:T(4,128)S(1)} %get-tuple-element.32), channel_id=1, source_target_pairs={{0,1},{2,3},{4,5},{6,7},{1,0},{3,2},{5,4},{7,6},{8,9},{10,11},{12,... | collective-permute-start | bytes 294920 | tf_op jit(solution)/shard_map/ppermute | solution.py:593
  6.8 0.7 collective-permute-start.1
  7.5 12.9 %all-to-all-start = ((f32[32,4,128]{2,1,0:T(4,128)}), f32[32,4,128]{2,1,0:T(4,128)S(1)}, u32[]{:S(2)}, u32[]{:S(2)}) async-start(f32[32,4,128]{2,1,0:T(4,128)} %get-tuple-element.27), calls=%async_computation | async-start | bytes 131072 | tf_op jit(solution)/shard_map/all_to_all | solution.py:587
  20.5 4.5 %collective-permute-start.2 = (f32[232,128]{1,0:T(8,128)S(1)}, f32[232,128]{1,0:T(8,128)S(1)}, u32[]{:S(2)}, u32[]{:S(2)}) collective-permute-start(f32[232,128]{1,0:T(8,128)S(1)} %get-tuple-element.35), channel_id=1, source_target_pairs={{8,16},{24,32},{40,48},{56,64},{72,80},{88,96},{104,112},{120,128}... | collective-permute-start | bytes 356360 | tf_op jit(solution)/shard_map/ppermute | solution.py:593
  25.0 4.2 %all-to-all-done.recv_ref = f32[32,4,128]{2,1,0:T(4,128)S(1)} async-done(((f32[32,4,128]{2,1,0:T(4,128)}), f32[32,4,128]{2,1,0:T(4,128)S(1)}, u32[]{:S(2)}, u32[]{:S(2)}) %all-to-all-start) | async-done | bytes 65568 | tf_op jit(solution)/shard_map/all_to_all | solution.py:587
  29.3 0.7 shard_map.69
  29.9 10.4 %all-to-all-start.1 = ((f32[16,4,128]{2,1,0:T(4,128)}), f32[16,4,128]{2,1,0:T(4,128)S(1)}, u32[]{:S(2)}, u32[]{:S(2)}) async-start(f32[16,4,128]{2,1,0:T(4,128)} %shard_map.69), calls=%async_computation.1 | async-start | bytes 65536 | tf_op jit(solution)/shard_map/all_to_all | solution.py:587
  40.3 2.0 %all-gather = f32[464,128]{1,0:T(8,128)S(1)} all-gather(f32[232,128]{1,0:T(8,128)S(1)} %get-tuple-element.34), channel_id=2, replica_groups=mesh['x'=4,'z'=8,'c'=2,'y'=8] {'c'}, dimensions={0}, use_global_device_ids=true | all-gather | bytes 356352 | tf_op jit(solution)/shard_map/all_gather | solution.py:627
  42.3 0.4 shard_map.71
  42.7 0.7 shard_map.72.start_ref
  43.4 0.2 copy-done.1
  43.6 1.1 %shard_map.73 = (f32[3,128]{1,0:T(4,128)S(1)}, f32[3,12,128]{2,1,0:T(8,128)S(1)}) custom-call(f32[22,24,128]{2,1,0:T(8,128)S(1)} %get-tuple-element.36.k_ref, f32[22,24,128]{2,1,0:T(8,128)S(1)} %get-tuple-element.37.label_ref, f32[88,384]{1,0:T(8,128)S(1)} %copy-done.1), custom_call_target="tpu_custom_call" | custom-call | flops 3000000 | bytes 3000000 | tf_op jit(solution)/shard_map/pallas_call | solution.py:29
  44.7 2.7 %all-to-all-done.1.recv_ref = f32[16,4,128]{2,1,0:T(4,128)S(1)} async-done(((f32[16,4,128]{2,1,0:T(4,128)}), f32[16,4,128]{2,1,0:T(4,128)S(1)}, u32[]{:S(2)}, u32[]{:S(2)}) %all-to-all-start.1) | async-done | bytes 32800 | tf_op jit(solution)/shard_map/all_to_all | solution.py:587
  47.4 1.1 %shard_map.74 = (f32[32,4,128]{2,1,0:T(4,128)}, f32[1,128]{1,0:T(1,128)S(1)}, f32[3,128]{1,0:T(4,128)S(1)}) custom-call(f32[16,4,128]{2,1,0:T(4,128)S(1)} %all-to-all-done.1.recv_ref, f32[12,128]{1,0:T(8,128)S(1)} %get-tuple-element.28.rc_ref, f32[14,128]{1,0:T(8,128)S(1)} %shard_map.72.start_ref, f32[3,12,128]{2,1,0:T(8,128)S(1)} %get-tuple-element.39.rows_ref, ...), custom_call_target="tpu_custom_call" | custom-call | tf_op jit(solution)/shard_map/pallas_call | solution.py:29
  48.5 3.9 %all-to-all-start.2 = ((f32[32,4,128]{2,1,0:T(4,128)}), f32[32,4,128]{2,1,0:T(4,128)S(1)}, u32[]{:S(2)}, u32[]{:S(2)}) async-start(f32[32,4,128]{2,1,0:T(4,128)} %get-tuple-element.41), calls=%async_computation.2 | async-start | bytes 131072 | tf_op jit(solution)/shard_map/all_to_all | solution.py:587
  52.4 1.9 %shard_map.75 = (f32[3,22,24,128]{3,2,1,0:T(8,128)S(1)}, f32[3,18,24,128]{3,2,1,0:T(8,128)S(1)}, f32[1,128]{1,0:T(1,128)S(1)}) custom-call(f32[3,128]{1,0:T(4,128)S(1)} %get-tuple-element.42.near_ref, f32[22,24,128]{2,1,0:T(8,128)S(1)} %get-tuple-element.36.k_ref, f32[22,24,128]{2,1,0:T(8,128)S(1)} %get-tuple-element.37.label_ref, ...), custom_call_target="tpu_custom_call", output_to_operand_aliasing={{0}: (4, {})} | custom-call | flops 3000000 | bytes 3000000 | tf_op jit(solution)/shard_map/pallas_call | solution.py:29
  54.3 6.9 %all-to-all-done.2.recv_ref = f32[32,4,128]{2,1,0:T(4,128)S(1)} async-done(((f32[32,4,128]{2,1,0:T(4,128)}), f32[32,4,128]{2,1,0:T(4,128)S(1)}, u32[]{:S(2)}, u32[]{:S(2)}) %all-to-all-start.2) | async-done | bytes 65568 | tf_op jit(solution)/shard_map/all_to_all | solution.py:587
  61.3 12.6 %all_to_all.25.recv_ref = f32[16,8,128]{2,1,0:T(8,128)S(1)} all-to-all(f32[16,8,128]{2,1,0:T(8,128)S(1)} %shard_map.76), channel_id=1, replica_groups=mesh['x'=4,'z'=8,'c'=2,'y'=8] {'c','y'}, dimensions={0} | all-to-all | bytes 131072 | tf_op jit(solution)/shard_map/all_to_all | solution.py:587
  73.9 1.1 %shard_map.77 = f32[32,1,128]{2,1,0:T(1,128)} custom-call(f32[16,8,128]{2,1,0:T(8,128)S(1)} %all_to_all.25.recv_ref), custom_call_target="tpu_custom_call" | custom-call | tf_op jit(solution)/shard_map/pallas_call | solution.py:29
  75.0 3.8 %all-to-all-start.4 = ((f32[32,1,128]{2,1,0:T(1,128)}), f32[32,1,128]{2,1,0:T(1,128)S(1)}, u32[]{:S(2)}, u32[]{:S(2)}) async-start(f32[32,1,128]{2,1,0:T(1,128)} %shard_map.77), calls=%async_computation.4 | async-start | bytes 32768 | tf_op jit(solution)/shard_map/all_to_all | solution.py:587
  78.9 0.8 shard_map.78
  79.7 7.7 %all-to-all-done.4.recv_ref = f32[32,1,128]{2,1,0:T(1,128)S(1)} async-done(((f32[32,1,128]{2,1,0:T(1,128)}), f32[32,1,128]{2,1,0:T(1,128)S(1)}, u32[]{:S(2)}, u32[]{:S(2)}) %all-to-all-start.4) | async-done | bytes 16416 | tf_op jit(solution)/shard_map/all_to_all | solution.py:587
  87.4 1.4 %shard_map.79 = (f32[3,16,16,128]{3,2,1,0:T(8,128)}, f32[3,16,16,128]{3,2,1,0:T(8,128)}) custom-call(f32[32,1,128]{2,1,0:T(1,128)S(1)} %all-to-all-done.4.recv_ref, f32[1,128]{1,0:T(1,128)S(1)} %get-tuple-element.49.scal_ref, f32[3,16,16,128]{3,2,1,0:T(8,128)S(1)} %copy-done, f32[3,22,24,128]{3,2,1,0:T(8,128)S(1)} %get-tuple-element.47.z_ref, ...), custom_call_target="tpu_custom_call" | custom-call | tf_op jit(solution)/shard_map/pallas_call | solution.py:29
  (8 shorter events, 0.1 us)
Async XLA Ops:
  2.8 17.6 %collective-permute-start = (f32[3,16,4,128]{3,2,1,0:T(4,128)S(1)}, f32[3,16,4,128]{3,2,1,0:T(4,128)S(1)}, u32[]{:S(2)}, u32[]{:S(2)}) collective-permute-start(f32[3,16,4,128]{3,2,1,0:T(4,128)S(1)} %get-tuple-element.32), channel_id=1, source_target_pairs={{0,1},{2,3},{4,5},{6,7},{1,0},{3,2},{5,4},{7,6},{8,9},{10,11},{12,... | collective-permute-start | bytes 294920 | tf_op jit(solution)/shard_map/ppermute | solution.py:593
  6.8 13.6 %collective-permute-start.1 = (f32[3,16,4,128]{3,2,1,0:T(4,128)S(1)}, f32[3,16,4,128]{3,2,1,0:T(4,128)S(1)}, u32[]{:S(2)}, u32[]{:S(2)}) collective-permute-start(f32[3,16,4,128]{3,2,1,0:T(4,128)S(1)} %get-tuple-element.33), channel_id=1, source_target_pairs={{1,2},{3,4},{5,6},{2,1},{4,3},{6,5},{9,10},{11,12},{13,14},{10,9},... | collective-permute-start | bytes 294920 | tf_op jit(solution)/shard_map/ppermute | solution.py:593
  7.5 21.8 %all-to-all-start = ((f32[32,4,128]{2,1,0:T(4,128)}), f32[32,4,128]{2,1,0:T(4,128)S(1)}, u32[]{:S(2)}, u32[]{:S(2)}) async-start(f32[32,4,128]{2,1,0:T(4,128)} %get-tuple-element.27), calls=%async_computation | async-start | bytes 131072 | tf_op jit(solution)/shard_map/all_to_all | solution.py:587
  20.5 21.8 %collective-permute-start.2 = (f32[232,128]{1,0:T(8,128)S(1)}, f32[232,128]{1,0:T(8,128)S(1)}, u32[]{:S(2)}, u32[]{:S(2)}) collective-permute-start(f32[232,128]{1,0:T(8,128)S(1)} %get-tuple-element.35), channel_id=1, source_target_pairs={{8,16},{24,32},{40,48},{56,64},{72,80},{88,96},{104,112},{120,128}... | collective-permute-start | bytes 356360 | tf_op jit(solution)/shard_map/ppermute | solution.py:593
  29.9 17.5 %all-to-all-start.1 = ((f32[16,4,128]{2,1,0:T(4,128)}), f32[16,4,128]{2,1,0:T(4,128)S(1)}, u32[]{:S(2)}, u32[]{:S(2)}) async-start(f32[16,4,128]{2,1,0:T(4,128)} %shard_map.69), calls=%async_computation.1 | async-start | bytes 65536 | tf_op jit(solution)/shard_map/all_to_all | solution.py:587
  42.7 0.9 %copy-start.1 = (f32[88,384]{1,0:T(8,128)S(1)}, f32[88,384]{1,0:T(8,128)}, u32[]{:S(2)}) copy-start(f32[88,384]{1,0:T(8,128)} %constant.2.clone.select_ref) | copy-start | bytes 405508
  48.5 12.7 %all-to-all-start.2 = ((f32[32,4,128]{2,1,0:T(4,128)}), f32[32,4,128]{2,1,0:T(4,128)S(1)}, u32[]{:S(2)}, u32[]{:S(2)}) async-start(f32[32,4,128]{2,1,0:T(4,128)} %get-tuple-element.41), calls=%async_computation.2 | async-start | bytes 131072 | tf_op jit(solution)/shard_map/all_to_all | solution.py:587
  75.0 12.4 %all-to-all-start.4 = ((f32[32,1,128]{2,1,0:T(1,128)}), f32[32,1,128]{2,1,0:T(1,128)S(1)}, u32[]{:S(2)}, u32[]{:S(2)}) async-start(f32[32,1,128]{2,1,0:T(1,128)} %shard_map.77), calls=%async_computation.4 | async-start | bytes 32768 | tf_op jit(solution)/shard_map/all_to_all | solution.py:587
  78.9 8.6 %copy-start = (f32[3,16,16,128]{3,2,1,0:T(8,128)S(1)}, f32[3,16,16,128]{3,2,1,0:T(8,128)}, u32[]{:S(2)}) copy-start(f32[3,16,16,128]{3,2,1,0:T(8,128)} %r_ref.1) | copy-start | bytes 1179652

commit v9 on v7

--- a/solution.py
+++ b/solution.py
@@ -8,7 +8,7 @@
 from jax.sharding import PartitionSpec as P
 
 WIDE = ("x", "z", "c")
-ROWS = ("x", "z")
+ROWS = ("z", "x")
 COLS = ("c", "y")
 NROWS = 32
 NCOLS = 16
@@ -80,7 +80,8 @@
         tail = jnp.broadcast_to(row, (4, 128))
     copies = []
     for n in range(NROWS):
-        window = pad_ref[2 * n : 2 * n + 4, :]
+        at = 2 * (n % 4 * 8 + n // 4)
+        window = pad_ref[at : at + 4, :]
         if sums:
             window = window + tail
         send_ref[n] = window

time: 88.7 us -> 88.6 us (level)
  no operation moved by 1% of the time
where the time goes in v9:
time: 88.6 us; the launch traced here: 88.1 us
  starting transfers between devices  42.4 us (48%)
  waiting for transfers between devices  21.5 us (24%)
  blocking collectives  11.8 us (13%)
  Pallas kernels  11.4 us (13%)
    all_to_all x4, starting transfers between devices, exchange(): return lax.all_to_all(array, axes, 0, 0, tiled=True)  31.2 us
    all_to_all x4, waiting for transfers between devices, exchange(): return lax.all_to_all(array, axes, 0, 0, tiled=True)  21.5 us
    all_to_all x1, blocking collectives, exchange(): return lax.all_to_all(array, axes, 0, 0, tiled=True)  11.8 us
    pallas_call x12, Pallas kernels, call(): pl.pallas_call(kernel, out_shape=outs, in_specs=[space] * len(ins), out_s...  11.4 us
    ppermute x4, starting transfers between devices, swapped(): return lax.ppermute(array, axis, pairs + [(b, a) for a, b in pairs])  11.2 us
  transfers between devices with their start and end apart: 8, of which 4 were waited for; matrix products, arithmetic and copies ran while one was open for 0% of the time, Pallas kernels for 6%

profile of v9, /device:TPU:1, one launch (start us, length us, event | category | flops | bytes accessed | tf_op | source)
XLA Modules:
  0.0 88.1 jit_solution(11030214568948374148)
XLA Ops:
  0.6 2.2 %shard_map.68 = (f32[32,4,128]{2,1,0:T(4,128)}, f32[3,16,16,128]{3,2,1,0:T(8,128)S(1)}, f32[16,16,128]{2,1,0:T(8,128)S(1)}, f32[12,6144]{1,0:T(8,128)S(1)}, f32[...) custom-call(f32[3,16,16,128]{3,2,1,0:T(8,128)} %r_ref.1, ...), custom_call_target="tpu_custom_call" | custom-call | tf_op jit(solution)/shard_map/pallas_call | solution.py:29
  2.8 4.0 %collective-permute-start = (f32[3,16,4,128]{3,2,1,0:T(4,128)S(1)}, f32[3,16,4,128]{3,2,1,0:T(4,128)S(1)}, u32[]{:S(2)}, u32[]{:S(2)}) collective-permute-start(f32[3,16,4,128]{3,2,1,0:T(4,128)S(1)} %get-tuple-element.32), channel_id=1, source_target_pairs={{0,1},{2,3},{4,5},{6,7},{1,0},{3,2},{5,4},{7,6},{8,9},{10,11},{12,... | collective-permute-start | bytes 294920 | tf_op jit(solution)/shard_map/ppermute | solution.py:594
  6.8 0.7 collective-permute-start.1
  7.5 12.9 %all-to-all-start = ((f32[32,4,128]{2,1,0:T(4,128)}), f32[32,4,128]{2,1,0:T(4,128)S(1)}, u32[]{:S(2)}, u32[]{:S(2)}) async-start(f32[32,4,128]{2,1,0:T(4,128)} %get-tuple-element.27), calls=%async_computation | async-start | bytes 131072 | tf_op jit(solution)/shard_map/all_to_all | solution.py:588
  20.5 3.1 %collective-permute-start.2 = (f32[232,128]{1,0:T(8,128)S(1)}, f32[232,128]{1,0:T(8,128)S(1)}, u32[]{:S(2)}, u32[]{:S(2)}) collective-permute-start(f32[232,128]{1,0:T(8,128)S(1)} %get-tuple-element.34), channel_id=1, source_target_pairs={{0,8},{16,24},{32,40},{48,56},{64,72},{80,88},{96,104},{112,120},{... | collective-permute-start | bytes 356360 | tf_op jit(solution)/shard_map/ppermute | solution.py:594
  23.6 3.3 %collective-permute-start.3 = (f32[232,128]{1,0:T(8,128)S(1)}, f32[232,128]{1,0:T(8,128)S(1)}, u32[]{:S(2)}, u32[]{:S(2)}) collective-permute-start(f32[232,128]{1,0:T(8,128)S(1)} %get-tuple-element.35), channel_id=1, source_target_pairs={{8,16},{24,32},{40,48},{56,64},{72,80},{88,96},{104,112},{120,128}... | collective-permute-start | bytes 356360 | tf_op jit(solution)/shard_map/ppermute | solution.py:594
  27.0 2.3 %all-to-all-done.recv_ref = f32[32,4,128]{2,1,0:T(4,128)S(1)} async-done(((f32[32,4,128]{2,1,0:T(4,128)}), f32[32,4,128]{2,1,0:T(4,128)S(1)}, u32[]{:S(2)}, u32[]{:S(2)}) %all-to-all-start) | async-done | bytes 65568 | tf_op jit(solution)/shard_map/all_to_all | solution.py:588
  29.2 0.7 shard_map.69
  29.9 10.4 %all-to-all-start.1 = ((f32[16,4,128]{2,1,0:T(4,128)}), f32[16,4,128]{2,1,0:T(4,128)S(1)}, u32[]{:S(2)}, u32[]{:S(2)}) async-start(f32[16,4,128]{2,1,0:T(4,128)} %shard_map.69), calls=%async_computation.1 | async-start | bytes 65536 | tf_op jit(solution)/shard_map/all_to_all | solution.py:588
  40.3 0.4 shard_map.71
  40.7 0.7 shard_map.72.start_ref
  41.4 0.2 copy-done.1
  41.6 1.1 %shard_map.73 = (f32[3,128]{1,0:T(4,128)S(1)}, f32[3,12,128]{2,1,0:T(8,128)S(1)}) custom-call(f32[22,24,128]{2,1,0:T(8,128)S(1)} %get-tuple-element.36.k_ref, f32[22,24,128]{2,1,0:T(8,128)S(1)} %get-tuple-element.37.label_ref, f32[88,384]{1,0:T(8,128)S(1)} %copy-done.1), custom_call_target="tpu_custom_call" | custom-call | flops 3000000 | bytes 3000000 | tf_op jit(solution)/shard_map/pallas_call | solution.py:29
  42.7 4.6 %all-to-all-done.1.recv_ref = f32[16,4,128]{2,1,0:T(4,128)S(1)} async-done(((f32[16,4,128]{2,1,0:T(4,128)}), f32[16,4,128]{2,1,0:T(4,128)S(1)}, u32[]{:S(2)}, u32[]{:S(2)}) %all-to-all-start.1) | async-done | bytes 32800 | tf_op jit(solution)/shard_map/all_to_all | solution.py:588
  47.4 1.1 %shard_map.74 = (f32[32,4,128]{2,1,0:T(4,128)}, f32[1,128]{1,0:T(1,128)S(1)}, f32[3,128]{1,0:T(4,128)S(1)}) custom-call(f32[16,4,128]{2,1,0:T(4,128)S(1)} %all-to-all-done.1.recv_ref, f32[12,128]{1,0:T(8,128)S(1)} %get-tuple-element.28.rc_ref, f32[14,128]{1,0:T(8,128)S(1)} %shard_map.72.start_ref, f32[3,12,128]{2,1,0:T(8,128)S(1)} %get-tuple-element.39.rows_ref, ...), custom_call_target="tpu_custom_call" | custom-call | tf_op jit(solution)/shard_map/pallas_call | solution.py:29
  48.5 4.1 %all-to-all-start.2 = ((f32[32,4,128]{2,1,0:T(4,128)}), f32[32,4,128]{2,1,0:T(4,128)S(1)}, u32[]{:S(2)}, u32[]{:S(2)}) async-start(f32[32,4,128]{2,1,0:T(4,128)} %get-tuple-element.41), calls=%async_computation.2 | async-start | bytes 131072 | tf_op jit(solution)/shard_map/all_to_all | solution.py:588
  52.6 1.9 %shard_map.75 = (f32[3,22,24,128]{3,2,1,0:T(8,128)S(1)}, f32[3,18,24,128]{3,2,1,0:T(8,128)S(1)}, f32[1,128]{1,0:T(1,128)S(1)}) custom-call(f32[3,128]{1,0:T(4,128)S(1)} %get-tuple-element.42.near_ref, f32[22,24,128]{2,1,0:T(8,128)S(1)} %get-tuple-element.36.k_ref, f32[22,24,128]{2,1,0:T(8,128)S(1)} %get-tuple-element.37.label_ref, ...), custom_call_target="tpu_custom_call", output_to_operand_aliasing={{0}: (4, {})} | custom-call | flops 3000000 | bytes 3000000 | tf_op jit(solution)/shard_map/pallas_call | solution.py:29
  54.5 6.9 %all-to-all-done.2.recv_ref = f32[32,4,128]{2,1,0:T(4,128)S(1)} async-done(((f32[32,4,128]{2,1,0:T(4,128)}), f32[32,4,128]{2,1,0:T(4,128)S(1)}, u32[]{:S(2)}, u32[]{:S(2)}) %all-to-all-start.2) | async-done | bytes 65568 | tf_op jit(solution)/shard_map/all_to_all | solution.py:588
  61.4 11.8 %all_to_all.25.recv_ref = f32[16,8,128]{2,1,0:T(8,128)S(1)} all-to-all(f32[16,8,128]{2,1,0:T(8,128)S(1)} %shard_map.76), channel_id=1, replica_groups=mesh['x'=4,'z'=8,'c'=2,'y'=8] {'c','y'}, dimensions={0} | all-to-all | bytes 131072 | tf_op jit(solution)/shard_map/all_to_all | solution.py:588
  73.2 1.1 %shard_map.77 = f32[32,1,128]{2,1,0:T(1,128)} custom-call(f32[16,8,128]{2,1,0:T(8,128)S(1)} %all_to_all.25.recv_ref), custom_call_target="tpu_custom_call" | custom-call | tf_op jit(solution)/shard_map/pallas_call | solution.py:29
  74.3 3.8 %all-to-all-start.4 = ((f32[32,1,128]{2,1,0:T(1,128)}), f32[32,1,128]{2,1,0:T(1,128)S(1)}, u32[]{:S(2)}, u32[]{:S(2)}) async-start(f32[32,1,128]{2,1,0:T(1,128)} %shard_map.77), calls=%async_computation.4 | async-start | bytes 32768 | tf_op jit(solution)/shard_map/all_to_all | solution.py:588
  78.2 0.8 shard_map.78
  79.0 7.7 %all-to-all-done.4.recv_ref = f32[32,1,128]{2,1,0:T(1,128)S(1)} async-done(((f32[32,1,128]{2,1,0:T(1,128)}), f32[32,1,128]{2,1,0:T(1,128)S(1)}, u32[]{:S(2)}, u32[]{:S(2)}) %all-to-all-start.4) | async-done | bytes 16416 | tf_op jit(solution)/shard_map/all_to_all | solution.py:588
  86.7 1.4 %shard_map.79 = (f32[3,16,16,128]{3,2,1,0:T(8,128)}, f32[3,16,16,128]{3,2,1,0:T(8,128)}) custom-call(f32[32,1,128]{2,1,0:T(1,128)S(1)} %all-to-all-done.4.recv_ref, f32[1,128]{1,0:T(1,128)S(1)} %get-tuple-element.49.scal_ref, f32[3,16,16,128]{3,2,1,0:T(8,128)S(1)} %copy-done, f32[3,22,24,128]{3,2,1,0:T(8,128)S(1)} %get-tuple-element.47.z_ref, ...), custom_call_target="tpu_custom_call" | custom-call | tf_op jit(solution)/shard_map/pallas_call | solution.py:29
  (9 shorter events, 0.1 us)
Async XLA Ops:
  2.8 17.6 %collective-permute-start = (f32[3,16,4,128]{3,2,1,0:T(4,128)S(1)}, f32[3,16,4,128]{3,2,1,0:T(4,128)S(1)}, u32[]{:S(2)}, u32[]{:S(2)}) collective-permute-start(f32[3,16,4,128]{3,2,1,0:T(4,128)S(1)} %get-tuple-element.32), channel_id=1, source_target_pairs={{0,1},{2,3},{4,5},{6,7},{1,0},{3,2},{5,4},{7,6},{8,9},{10,11},{12,... | collective-permute-start | bytes 294920 | tf_op jit(solution)/shard_map/ppermute | solution.py:594
  6.8 13.6 %collective-permute-start.1 = (f32[3,16,4,128]{3,2,1,0:T(4,128)S(1)}, f32[3,16,4,128]{3,2,1,0:T(4,128)S(1)}, u32[]{:S(2)}, u32[]{:S(2)}) collective-permute-start(f32[3,16,4,128]{3,2,1,0:T(4,128)S(1)} %get-tuple-element.33), channel_id=1, source_target_pairs={{1,2},{3,4},{5,6},{2,1},{4,3},{6,5},{9,10},{11,12},{13,14},{10,9},... | collective-permute-start | bytes 294920 | tf_op jit(solution)/shard_map/ppermute | solution.py:594
  7.5 21.7 %all-to-all-start = ((f32[32,4,128]{2,1,0:T(4,128)}), f32[32,4,128]{2,1,0:T(4,128)S(1)}, u32[]{:S(2)}, u32[]{:S(2)}) async-start(f32[32,4,128]{2,1,0:T(4,128)} %get-tuple-element.27), calls=%async_computation | async-start | bytes 131072 | tf_op jit(solution)/shard_map/all_to_all | solution.py:588
  20.5 19.8 %collective-permute-start.2 = (f32[232,128]{1,0:T(8,128)S(1)}, f32[232,128]{1,0:T(8,128)S(1)}, u32[]{:S(2)}, u32[]{:S(2)}) collective-permute-start(f32[232,128]{1,0:T(8,128)S(1)} %get-tuple-element.34), channel_id=1, source_target_pairs={{0,8},{16,24},{32,40},{48,56},{64,72},{80,88},{96,104},{112,120},{... | collective-permute-start | bytes 356360 | tf_op jit(solution)/shard_map/ppermute | solution.py:594
  23.6 16.7 %collective-permute-start.3 = (f32[232,128]{1,0:T(8,128)S(1)}, f32[232,128]{1,0:T(8,128)S(1)}, u32[]{:S(2)}, u32[]{:S(2)}) collective-permute-start(f32[232,128]{1,0:T(8,128)S(1)} %get-tuple-element.35), channel_id=1, source_target_pairs={{8,16},{24,32},{40,48},{56,64},{72,80},{88,96},{104,112},{120,128}... | collective-permute-start | bytes 356360 | tf_op jit(solution)/shard_map/ppermute | solution.py:594
  29.9 17.5 %all-to-all-start.1 = ((f32[16,4,128]{2,1,0:T(4,128)}), f32[16,4,128]{2,1,0:T(4,128)S(1)}, u32[]{:S(2)}, u32[]{:S(2)}) async-start(f32[16,4,128]{2,1,0:T(4,128)} %shard_map.69), calls=%async_computation.1 | async-start | bytes 65536 | tf_op jit(solution)/shard_map/all_to_all | solution.py:588
  40.7 0.9 %copy-start.1 = (f32[88,384]{1,0:T(8,128)S(1)}, f32[88,384]{1,0:T(8,128)}, u32[]{:S(2)}) copy-start(f32[88,384]{1,0:T(8,128)} %constant.2.clone.select_ref) | copy-start | bytes 405508
  48.5 12.9 %all-to-all-start.2 = ((f32[32,4,128]{2,1,0:T(4,128)}), f32[32,4,128]{2,1,0:T(4,128)S(1)}, u32[]{:S(2)}, u32[]{:S(2)}) async-start(f32[32,4,128]{2,1,0:T(4,128)} %get-tuple-element.41), calls=%async_computation.2 | async-start | bytes 131072 | tf_op jit(solution)/shard_map/all_to_all | solution.py:588
  74.3 12.4 %all-to-all-start.4 = ((f32[32,1,128]{2,1,0:T(1,128)}), f32[32,1,128]{2,1,0:T(1,128)S(1)}, u32[]{:S(2)}, u32[]{:S(2)}) async-start(f32[32,1,128]{2,1,0:T(1,128)} %shard_map.77), calls=%async_computation.4 | async-start | bytes 32768 | tf_op jit(solution)/shard_map/all_to_all | solution.py:588
  78.2 8.5 %copy-start = (f32[3,16,16,128]{3,2,1,0:T(8,128)S(1)}, f32[3,16,16,128]{3,2,1,0:T(8,128)}, u32[]{:S(2)}) copy-start(f32[3,16,16,128]{3,2,1,0:T(8,128)} %r_ref.1) | copy-start | bytes 1179652
